TPU v7x, 512 devices: a whole 4x8x8 slice. The times are simulated.
512 devices in a mesh: dp: 64 (over z_hi, y, x), tensor: 8 (over z_lo, core).
Axes of the slice: x: 4, y: 8, z: 8 (z_hi: 2, z_lo: 4; z = z_hi * 4 + z_lo), core: 2. Of those that a mesh axis runs over, the one named last changes fastest.
Arguments:
- frames: bfloat16 [16384, 1536], P('dp', 'tensor'), may hold values from -6 to 6
- norm_gain: float32 [1536], replicated, may hold values from 0.5 to 2
- norm_bias: float32 [1536], replicated, may hold values from -3 to 3
- input_weight: bfloat16 [2, 1536, 1536], P(None, 'tensor'), may hold values from -0.15625 to 0.15625
- depth_weight: float32 [32, 1536], P(None, 'tensor'), may hold values from -1.5 to 1.5
- batch_scale: float32 [1536], P('tensor'), may hold values from 0.5 to 2
- batch_shift: float32 [1536], P('tensor'), may hold values from -3 to 3
- output_weight: bfloat16 [1536, 1536], P('tensor'), may hold values from -0.15625 to 0.15625
- upstream: bfloat16 [32768, 1536], P(('dp', 'tensor')), may hold values from -6 to 6
- replica_blocks: int32 [64], replicated, may hold values from 0 to 64, as said below
- segment: int32 [32768], P('dp'), may hold values from 0 to 32, as said below
Outputs:
- block_output: bfloat16 [32768, 1536], P(('dp', 'tensor'))
- frame_gradient: bfloat16 [16384, 1536], P('dp', 'tensor')
- input_weight_gradient: bfloat16 [2, 1536, 1536], P(None, 'tensor')
- output_weight_gradient: bfloat16 [1536, 1536], P('tensor')
- depth_weight_gradient: float32 [32, 1536], P(None, 'tensor')
- gain_gradient: float32 [1536], P('tensor')
- bias_gradient: float32 [1536], P('tensor')
Inputs may be any that keep to these rules, and one draw needn't show every extreme that they name: `replica_blocks`: the counts sum to 2048. `segment`: within a replica's 512 slots the number starts at 0 and never falls.
All inputs are finite; a program needn't handle non-finite values.
Results may differ from a plain program's by a relative error of at most 0.017.
Values may be sent and summed in bfloat16 or wider, within the bound.
No kernel may reach another device: no remote copies, remote signals or barrier semaphores. Data moves between devices by JAX's collectives and lax.ppermute only.
A program may use at most 64 MiB of HBM per device.

v0:
```python
import jax
import jax.numpy as jnp
from jax import lax
from jax.sharding import PartitionSpec as P

BLK = 8


epsilon = 1e-05


def routes(replica_blocks, replicas, my_index, load_blocks, cap_blocks, per_peer):
    run_ends = jnp.cumsum(replica_blocks)
    starts = run_ends - replica_blocks
    peer_ids = jnp.arange(replicas, dtype=jnp.int32)
    blocks = jnp.arange(load_blocks, dtype=jnp.int32)
    numbers = my_index + replicas * blocks
    target = jnp.sum((run_ends[None, :] <= numbers[:, None]).astype(jnp.int32), axis=1)
    target_start = jnp.sum(
        jnp.where(peer_ids[None, :] == target[:, None], starts[None, :], 0), axis=1
    )
    slot_out = blocks - (jnp.maximum(target_start - my_index, 0) + replicas - 1) // replicas
    is_mine = peer_ids == my_index
    my_start = jnp.sum(jnp.where(is_mine, starts, 0))
    my_end = jnp.sum(jnp.where(is_mine, run_ends, 0))
    bucket_pos = jnp.arange(per_peer, dtype=jnp.int32)
    skipped = (jnp.maximum(my_start - peer_ids, 0) + replicas - 1) // replicas
    arriving = peer_ids[:, None] + replicas * (skipped[:, None] + bucket_pos[None, :])
    filled = arriving < my_end
    landing = jnp.where(filled, arriving - my_start, cap_blocks)
    return (target, slot_out, landing, filled, my_end - my_start)


def on_device(
    frames,
    norm_gain,
    norm_bias,
    input_weight,
    depth_weight,
    batch_scale,
    batch_shift,
    output_weight,
    upstream,
    replica_blocks,
    segment,
):
    replicas = lax.axis_size("dp")
    my_index = lax.axis_index("dp")
    tensor_index = lax.axis_index("tensor")
    full_width = norm_gain.shape[0]
    load_rows, part_width = frames.shape
    row_count = segment.shape[0]
    rows_part = upstream.shape[0]
    kernel_taps = depth_weight.shape[0]
    load_blocks = load_rows // BLK
    cap_blocks = row_count // BLK
    per_peer = (cap_blocks + replicas - 1) // replicas
    target, slot_out, landing, filled, my_blocks = routes(
        replica_blocks, replicas, my_index, load_blocks, cap_blocks, per_peer
    )
    outbox = (
        jnp.zeros((replicas, per_peer, BLK, part_width), jnp.bfloat16)
        .at[target, slot_out]
        .set(frames.reshape(load_blocks, BLK, part_width))
    )
    arrived = lax.all_to_all(outbox, "dp", split_axis=0, concat_axis=0, tiled=True)
    packed = (
        jnp.zeros((cap_blocks, BLK, part_width), jnp.bfloat16)
        .at[landing.reshape(-1)]
        .set(arrived.reshape(-1, BLK, part_width), mode="drop")
    )
    local_rows = packed.reshape(row_count, part_width)
    active = jnp.arange(row_count, dtype=jnp.int32) // BLK < my_blocks
    row_start = tensor_index * rows_part
    active_mine = lax.dynamic_slice_in_dim(active, row_start, rows_part)[:, None]
    column_start = tensor_index * part_width
    gain_part = lax.dynamic_slice_in_dim(norm_gain, column_start, part_width)
    local_float = local_rows.astype(jnp.float32)
    gathered = lax.all_gather(local_rows, "tensor", axis=1, tiled=True)
    gathered_float = gathered.astype(jnp.float32)
    center = jnp.mean(gathered_float, axis=1, keepdims=True)
    spread = jnp.mean(jnp.square(gathered_float - center), axis=1, keepdims=True)
    scale_row = lax.rsqrt(spread + epsilon)
    normed = ((gathered_float - center) * scale_row * norm_gain + norm_bias).astype(jnp.bfloat16)
    residual_part = lax.dynamic_slice_in_dim(gathered, row_start, rows_part, 0)
    projected = jnp.einsum("td,kcd->ktc", normed, input_weight, preferred_element_type=jnp.float32)
    linear = projected[0]
    gate_sigmoid = jax.nn.sigmoid(projected[1])
    glu = (linear * gate_sigmoid).astype(jnp.bfloat16)
    front = kernel_taps // 2
    back = kernel_taps - 1 - front
    seg_pad = jnp.pad(segment, (front, back), constant_values=-1)
    active_pad = jnp.pad(active, (front, back))
    glu_pad = jnp.pad(glu, ((front, back), (0, 0)))
    tap_masks = []
    for offset in range(kernel_taps):
        same = (seg_pad[offset : offset + row_count] == segment) & active_pad[
            offset : offset + row_count
        ]
        tap_masks.append(same.astype(jnp.float32)[:, None])
    conv_sum = jnp.zeros((row_count, part_width), jnp.float32)
    for offset in range(kernel_taps):
        conv_sum = (
            conv_sum
            + depth_weight[offset]
            * glu_pad[offset : offset + row_count].astype(jnp.float32)
            * tap_masks[offset]
        )
    preswish = conv_sum * batch_scale + batch_shift
    pre_sigmoid = jax.nn.sigmoid(preswish)
    swish = (preswish * pre_sigmoid).astype(jnp.bfloat16)
    mixed_sum = lax.psum_scatter(
        jnp.dot(swish, output_weight, preferred_element_type=jnp.float32).astype(jnp.bfloat16),
        "tensor",
        scatter_dimension=0,
        tiled=True,
    ).astype(jnp.float32)
    block_output = jnp.where(
        active_mine, residual_part.astype(jnp.float32) + mixed_sum, 0.0
    ).astype(jnp.bfloat16)
    delta_piece = jnp.where(active_mine, upstream, jnp.zeros_like(upstream))
    delta_whole = lax.all_gather(delta_piece, "tensor", axis=0, tiled=True)
    delta_part = lax.dynamic_slice_in_dim(delta_whole, column_start, part_width, 1)
    delta_swish = lax.dot_general(
        delta_whole, output_weight, (((1,), (1,)), ((), ())), preferred_element_type=jnp.float32
    )
    out_local = lax.dot_general(
        swish, delta_whole, (((0,), (0,)), ((), ())), preferred_element_type=jnp.float32
    )
    delta_conv = delta_swish * pre_sigmoid * (1.0 + preswish * (1.0 - pre_sigmoid)) * batch_scale
    delta_pad = jnp.zeros((row_count + kernel_taps - 1, part_width), jnp.float32)
    tap_rows = []
    for offset in range(kernel_taps):
        contrib = delta_conv * tap_masks[offset]
        delta_pad = delta_pad.at[offset : offset + row_count].add(depth_weight[offset] * contrib)
        tap_rows.append(
            jnp.sum(contrib * glu_pad[offset : offset + row_count].astype(jnp.float32), axis=0)
        )
    delta_glu = delta_pad[front : front + row_count]
    tap_local = jnp.stack(tap_rows)
    delta_linear = (delta_glu * gate_sigmoid).astype(jnp.bfloat16)
    delta_gate = (delta_glu * linear * gate_sigmoid * (1.0 - gate_sigmoid)).astype(jnp.bfloat16)
    stacked = jnp.stack([delta_linear, delta_gate])
    weight_local = jnp.einsum("ktc,td->kcd", stacked, normed, preferred_element_type=jnp.float32)
    back_terms = jnp.einsum(
        "ktc,kcd->td", stacked, input_weight, preferred_element_type=jnp.float32
    )
    delta_normed = lax.psum_scatter(
        back_terms.astype(jnp.bfloat16), "tensor", scatter_dimension=1, tiled=True
    ).astype(jnp.float32)
    standard = (local_float - center) * scale_row
    gain_local = jnp.sum(delta_normed * standard, axis=0)
    bias_local = jnp.sum(delta_normed, axis=0)
    delta_standard = delta_normed * gain_part
    unit_total, cross_total = lax.psum(
        (jnp.sum(delta_standard, axis=1), jnp.sum(delta_standard * standard, axis=1)), "tensor"
    )
    delta_rows = delta_part.astype(jnp.float32) + scale_row * (
        delta_standard
        - (unit_total / full_width)[:, None]
        - standard * (cross_total / full_width)[:, None]
    )
    delta_blocks = delta_rows.astype(jnp.bfloat16).reshape(cap_blocks, BLK, part_width)
    homebound = jnp.where(
        filled[:, :, None, None],
        delta_blocks[jnp.minimum(landing, cap_blocks - 1)],
        jnp.zeros((), jnp.bfloat16),
    )
    returned = lax.all_to_all(homebound, "dp", split_axis=0, concat_axis=0, tiled=True)
    frame_gradient = returned[target, slot_out].reshape(load_rows, part_width)
    weight_summed, out_summed, tap_summed, gain_summed, bias_summed = lax.psum(
        (weight_local, out_local, tap_local, gain_local, bias_local), "dp"
    )
    return (
        block_output,
        frame_gradient,
        weight_summed.astype(jnp.bfloat16),
        out_summed.astype(jnp.bfloat16),
        tap_summed,
        gain_summed,
        bias_summed,
    )


def solution(mesh):
    in_specs = (
        P("dp", "tensor"),
        P(),
        P(),
        P(None, "tensor", None),
        P(None, "tensor"),
        P("tensor"),
        P("tensor"),
        P("tensor", None),
        P(("dp", "tensor"), None),
        P(),
        P("dp"),
    )
    out_specs = (
        P(("dp", "tensor"), None),
        P("dp", "tensor"),
        P(None, "tensor", None),
        P("tensor", None),
        P(None, "tensor"),
        P("tensor"),
        P("tensor"),
    )
    return jax.shard_map(
        on_device, mesh=mesh, in_specs=in_specs, out_specs=out_specs, check_vma=False
    )
```

profile of v0, /device:TPU:192, one launch (start us, length us, event | category | flops | bytes accessed | tf_op | source)
XLA Modules:
  0.0 834.8 jit_solution(11168631513885018504)
XLA Ops:
  11.7 3.7 scatter_fusion
  15.4 16.3 %all-to-all-start = ((bf16[64,1,8,192]{3,2,1,0:T(8,128)(2,1)}), bf16[64,1,8,192]{3,2,1,0:T(8,128)(2,1)S(1)}, u32[]{:S(2)}, u32[]{:S(2)}) async-start(bf16[64,1,8,192]{3,2,1,0:T(8,128)(2,1)} %bitcast.7), calls=%async_computation | async-start | bytes 524288 | tf_op jit(solution)/shard_map/all_to_all | solution.py:66
  33.0 15.9 %all-to-all-done = bf16[64,1,8,192]{3,2,1,0:T(8,128)(2,1)S(1)} async-done(((bf16[64,1,8,192]{3,2,1,0:T(8,128)(2,1)}), bf16[64,1,8,192]{3,2,1,0:T(8,128)(2,1)S(1)}, u32[]{:S(2)}, u32[]{:S(2)}) %all-to-all-start) | async-done | bytes 196640 | tf_op jit(solution)/shard_map/all_to_all | solution.py:66
  55.1 28.5 %all-gather.3.cloned.1.call-done = bf16[512,1536]{0,1:T(8,128)(2,1)} async-done(((bf16[512,192]{0,1:T(8,128)(2,1)}), bf16[512,1536]{0,1:T(8,128)(2,1)}) %all-gather.3.cloned.1.call-update) | async-done | bytes 1572880 | tf_op jit(solution)/shard_map/all_gather | solution.py:79
  87.1 4.0 fusion.106
  91.1 35.6 %all-gather.5.cloned.1.call-done = bf16[512,1536]{1,0:T(8,128)(2,1)} async-done(((bf16[64,1536]{1,0:T(8,128)(2,1)}), bf16[512,1536]{1,0:T(8,128)(2,1)}) %all-gather.5.cloned.1.call-update) | async-done | bytes 1572880 | tf_op jit(solution)/shard_map/all_gather | solution.py:122
  129.9 2.9 scatter-add.109
  133.8 2.9 scatter-add.110
  137.6 2.9 scatter-add.111
  141.4 2.9 scatter-add.114
  145.2 2.9 scatter-add.115
  149.1 2.9 scatter-add.116
  164.4 2.9 scatter-add.124
  168.2 2.9 scatter-add.125
  179.7 2.9 scatter-add.130
  183.5 3.1 scatter-add.131
  187.5 2.9 scatter-add.134
  206.6 2.9 scatter-add.141
  238.1 2.9 scatter-add.155
  259.1 3.6 fusion.20
  270.3 22.7 %reduce-scatter.7.cloned.1.call-done = bf16[192,512]{1,0:T(8,128)(2,1)} async-done(((bf16[1536,512]{1,0:T(8,128)(2,1)}), bf16[192,512]{1,0:T(8,128)(2,1)}) %reduce-scatter.7.cloned.1.call-update) | async-done | bytes 196624
  294.5 13.4 %all-reduce.5 = (f32[512]{0:T(512)S(1)}, f32[512]{0:T(512)S(1)}) all-reduce(f32[512]{0:T(512)S(1)} %get-tuple-element.445, f32[512]{0:T(512)S(1)} %get-tuple-element.446), channel_id=1, replica_groups=mesh['dp'=64,'tensor'=8] {'tensor'}, use_global_device_ids=true, to_apply=%region_14.15 | all-reduce | flops 1024 | bytes 8192 | tf_op jit(solution)/shard_map/psum | solution.py:155
  310.9 14.0 %all-to-all-start.1 = ((bf16[64,1,8,192]{3,2,1,0:T(8,128)(2,1)}), bf16[64,1,8,192]{3,2,1,0:T(8,128)(2,1)S(1)}, u32[]{:S(2)}, u32[]{:S(2)}) async-start(bf16[64,1,8,192]{3,2,1,0:T(8,128)(2,1)} %bitcast_select_fusion), calls=%async_computation.2 | async-start | bytes 524288 | tf_op jit(solution)/shard_map/all_to_all | solution.py:169
  325.0 499.8 %all-reduce.7 = (bf16[2,192,1536]{2,1,0:T(8,128)(2,1)}, bf16[192,1536]{1,0:T(8,128)(2,1)}, f32[32,192]{1,0:T(8,128)}, f32[192]{0:T(256)}, f32[192]{0:T(256)}) all-reduce(f32[2,192,1536]{2,1,0:T(8,128)} %fusion.20, f32[192,1536]{1,0:T(8,128)S(1)} %fusion.233, f32[32,192]{1,0:T(8,128)S(1)} %stack.143, ...), channel_id=1, replica_groups=mesh['dp'=64,'tensor'=8] {'dp'}, use_global_device_ids=true, to_apply=%region_15.16 | all-reduce | flops 891264 | bytes 5360640 | tf_op jit(solution)/shard_map/psum | solution.py:171
  (272 shorter events, 123.0 us)
Async XLA Ops:
  15.4 33.5 %all-to-all-start = ((bf16[64,1,8,192]{3,2,1,0:T(8,128)(2,1)}), bf16[64,1,8,192]{3,2,1,0:T(8,128)(2,1)S(1)}, u32[]{:S(2)}, u32[]{:S(2)}) async-start(bf16[64,1,8,192]{3,2,1,0:T(8,128)(2,1)} %bitcast.7), calls=%async_computation | async-start | bytes 524288 | tf_op jit(solution)/shard_map/all_to_all | solution.py:66
  31.8 51.8 %all-gather.3.cloned.1.call-start = ((), (), s32[]{:S(2)}) async-start(), calls=%async_computation.4 | async-start | bytes 1769472 | tf_op jit(solution)/shard_map/all_gather | solution.py:79
  52.2 74.4 %all-gather.5.cloned.1.call-start = ((), (), s32[]{:S(2)}) async-start(), calls=%async_computation.6 | async-start | bytes 1769472 | tf_op jit(solution)/shard_map/all_gather | solution.py:122
  54.4 238.6 %reduce-scatter.7.cloned.1.call-start = ((), (), s32[]{:S(2)}) async-start(), calls=%async_computation.7 | async-start | bytes 1769472
  54.5 151.1 %copy-start.21 = (f32[512]{0:T(512)}, f32[512]{0:T(512)S(1)}, u32[]{:S(2)}) copy-start(f32[512]{0:T(512)S(1)} %get-tuple-element.500) | copy-start | bytes 6148
  54.6 154.9 %copy-start.19 = (f32[512]{0:T(512)}, f32[512]{0:T(512)S(1)}, u32[]{:S(2)}) copy-start(f32[512]{0:T(512)S(1)} %get-tuple-element.499) | copy-start | bytes 6148
  54.6 158.8 %copy-start.17 = (f32[512]{0:T(512)}, f32[512]{0:T(512)S(1)}, u32[]{:S(2)}) copy-start(f32[512]{0:T(512)S(1)} %get-tuple-element.498) | copy-start | bytes 6148
  54.7 116.4 %copy-start.37 = (f32[512]{0:T(512)}, f32[512]{0:T(512)S(1)}, u32[]{:S(2)}) copy-start(f32[512]{0:T(512)S(1)} %get-tuple-element.509) | copy-start | bytes 6148
  54.7 120.2 %copy-start.35 = (f32[512]{0:T(512)}, f32[512]{0:T(512)S(1)}, u32[]{:S(2)}) copy-start(f32[512]{0:T(512)S(1)} %get-tuple-element.508) | copy-start | bytes 6148
  54.7 124.0 %copy-start.33 = (f32[512]{0:T(512)}, f32[512]{0:T(512)S(1)}, u32[]{:S(2)}) copy-start(f32[512]{0:T(512)S(1)} %get-tuple-element.507) | copy-start | bytes 6148
  54.7 127.8 %copy-start.31 = (f32[512]{0:T(512)}, f32[512]{0:T(512)S(1)}, u32[]{:S(2)}) copy-start(f32[512]{0:T(512)S(1)} %get-tuple-element.506) | copy-start | bytes 6148
  54.7 135.7 %copy-start.29 = (f32[512]{0:T(512)}, f32[512]{0:T(512)S(1)}, u32[]{:S(2)}) copy-start(f32[512]{0:T(512)S(1)} %get-tuple-element.505) | copy-start | bytes 6148
  54.7 139.5 %copy-start.27 = (f32[512]{0:T(512)}, f32[512]{0:T(512)S(1)}, u32[]{:S(2)}) copy-start(f32[512]{0:T(512)S(1)} %get-tuple-element.504) | copy-start | bytes 6148
  54.7 143.3 %copy-start.25 = (f32[512]{0:T(512)}, f32[512]{0:T(512)S(1)}, u32[]{:S(2)}) copy-start(f32[512]{0:T(512)S(1)} %get-tuple-element.503) | copy-start | bytes 6148
  54.8 147.1 %copy-start.23 = (f32[512]{0:T(512)}, f32[512]{0:T(512)S(1)}, u32[]{:S(2)}) copy-start(f32[512]{0:T(512)S(1)} %get-tuple-element.502) | copy-start | bytes 6148
  54.8 186.2 %copy-start.11 = (f32[512]{0:T(512)}, f32[512]{0:T(512)S(1)}, u32[]{:S(2)}) copy-start(f32[512]{0:T(512)S(1)} %get-tuple-element.522) | copy-start | bytes 6148
  54.9 190.0 %copy-start.15 = (f32[512]{0:T(512)}, f32[512]{0:T(512)S(1)}, u32[]{:S(2)}) copy-start(f32[512]{0:T(512)S(1)} %get-tuple-element.521) | copy-start | bytes 6148
  55.0 100.7 %copy-start.45 = (f32[512]{0:T(512)}, f32[512]{0:T(512)S(1)}, u32[]{:S(2)}) copy-start(f32[512]{0:T(512)S(1)} %get-tuple-element.514) | copy-start | bytes 6148
  55.0 104.6 %copy-start.43 = (f32[512]{0:T(512)}, f32[512]{0:T(512)S(1)}, u32[]{:S(2)}) copy-start(f32[512]{0:T(512)S(1)} %get-tuple-element.513) | copy-start | bytes 6148
  55.0 108.4 %copy-start.41 = (f32[512]{0:T(512)}, f32[512]{0:T(512)S(1)}, u32[]{:S(2)}) copy-start(f32[512]{0:T(512)S(1)} %get-tuple-element.512) | copy-start | bytes 6148
  55.0 112.2 %copy-start.39 = (f32[512]{0:T(512)}, f32[512]{0:T(512)S(1)}, u32[]{:S(2)}) copy-start(f32[512]{0:T(512)S(1)} %get-tuple-element.511) | copy-start | bytes 6148
  251.7 573.0 %reduce-scatter.5.cloned.1.call-start = ((), (), s32[]{:S(2)}) async-start(), calls=%async_computation.5 | async-start | bytes 1769472 | tf_op jit(solution)/shard_map/reduce_scatter | solution.py:112
  310.9 515.5 %all-to-all-start.1 = ((bf16[64,1,8,192]{3,2,1,0:T(8,128)(2,1)}), bf16[64,1,8,192]{3,2,1,0:T(8,128)(2,1)S(1)}, u32[]{:S(2)}, u32[]{:S(2)}) async-start(bf16[64,1,8,192]{3,2,1,0:T(8,128)(2,1)} %bitcast_select_fusion), calls=%async_computation.2 | async-start | bytes 524288 | tf_op jit(solution)/shard_map/all_to_all | solution.py:169
  325.0 499.8 %copy-start.72 = (pred[64]{0:T(512)(128)(4,1)S(1)}, pred[64]{0:T(512)(128)(4,1)}, u32[]{:S(2)}) copy-start(pred[64]{0:T(512)(128)(4,1)} %copy-done.71) | copy-start | bytes 196
  (61 other events, 1150.1 us)
Sparse Core Ops, SparseCore 0:
  52.4 31.1 all-gather.2
  86.2 40.3 all-gather.4
  251.9 41.0 reduce-scatter.6
  295.7 44.0 reduce-scatter.4
where the time goes:
time: 843 us; the launch traced here: 835 us
  blocking collectives  513 us (61%)
  local copies, waits for them, and re-layouts  107 us (13%)
  waiting for transfers between devices  103 us (12%)
  other arithmetic  52.8 us (6%)
  starting transfers between devices  30.8 us (4%)
  between operations  16.9 us (2%)
  matrix products  11.3 us (1%)
    psum x1, blocking collectives, on_device(): lax.psum((weight_local, out_local, tap_local, gain_local, bias_local), 'dp')  500 us
    scatter-add x32, local copies, waits for them, and re-layouts, on_device(): delta_pad.at[offset:offset + row_count].add(depth_weight[offset] * contrib)  89 us
    all_gather x1, waiting for transfers between devices, on_device(): delta_whole = lax.all_gather(delta_piece, 'tensor', axis=0, tiled=True)  35.6 us
    all_gather x1, waiting for transfers between devices, on_device(): gathered = lax.all_gather(local_rows, 'tensor', axis=1, tiled=True)  28.5 us
    add x30, other arithmetic, on_device(): delta_pad.at[offset:offset + row_count].add(depth_weight[offset] * contrib)  28.3 us
    unnamed x5, waiting for transfers between devices  22.8 us
  transfers between devices with their start and end apart: 6, of which 4 were waited for; matrix products, arithmetic and copies ran while one was open for 4% of the time, Pallas kernels for 0%

commit v1 on v0

v1 whole, which is shorter than its diff:
```python
import functools

import jax
import jax.numpy as jnp
from jax import lax
from jax.experimental import pallas as pl
from jax.experimental.pallas import tpu as pltpu
from jax.sharding import Mesh
from jax.sharding import PartitionSpec as P

BLK = 8
LANES = 128
EDGE = 16
epsilon = 1e-05
VMEM_LIMIT = 40 * 1024 * 1024

f32 = jnp.float32
bf16 = jnp.bfloat16
DP = ("zh", "y", "x")
TENSOR = ("zl", "core")


def dot_general(a, b, ca, cb):
    return lax.dot_general(a, b, (((ca,), (cb,)), ((), ())), preferred_element_type=f32)


def full_call(kernel, out_shape, scratch, smem, flops, nbytes):
    def call(*args):
        specs = [pl.BlockSpec(memory_space=pltpu.SMEM)] * smem
        specs += [pl.BlockSpec(memory_space=pltpu.VMEM)] * (len(args) - smem)
        outs = jax.tree.map(lambda _: pl.BlockSpec(memory_space=pltpu.VMEM), out_shape)
        return pl.pallas_call(
            kernel,
            out_shape=out_shape,
            in_specs=specs,
            out_specs=outs,
            scratch_shapes=scratch,
            compiler_params=pltpu.CompilerParams(vmem_limit_bytes=VMEM_LIMIT),
            cost_estimate=pl.CostEstimate(flops=flops, bytes_accessed=nbytes, transcendentals=0),
        )(*args)

    return call


def pack_kernel(scalars, arrived, rows_out, cols_out, held):
    start, blocks = scalars[0], scalars[1]
    count, _, width = arrived.shape
    for p in range(count):
        block = arrived[lax.rem(start + p, count)].astype(f32)
        held[p * BLK : (p + 1) * BLK, :] = jnp.where(p < blocks, block, 0.0)
    rows = held[...]
    rows_out[...] = rows.astype(bf16)
    for c in range(0, width, LANES):
        e = min(width, c + LANES)
        cols_out[c:e, :] = jnp.transpose(held[:, c:e]).astype(bf16)


def shift_masks(seg_s, base, offset, step, rows):
    return seg_s[pl.ds(base + offset, rows), :] == seg_s[pl.ds(base + EDGE, rows), :]


def main_kernel(
    scalars,
    x_ref,
    gb_ref,
    win_ref,
    taps_ref,
    scale_ref,
    shift_ref,
    seg_ref,
    delta_ref,
    wout_ref,
    normed_ref,
    swish_ref,
    dlt_ref,
    back_ref,
    tap_ref,
    stats_ref,
    totals_ref,
    glu_s,
    dc_s,
    seg_s,
    w_s,
    bn_s,
    pre_s,
    dglu_s,
    lin_s,
    sig_s,
    tap_s,
):
    width, slots = x_ref.shape
    part = win_ref.shape[1]
    taps = taps_ref.shape[0]
    rest = part - LANES
    live = scalars[1] * BLK
    chunk = 64
    steps = width // chunk

    def fold(v):
        return jnp.sum(v.reshape(chunk // BLK, BLK, slots), axis=0)

    def sum_body(i, acc):
        return acc + fold(x_ref[pl.ds(i * chunk, chunk), :].astype(f32))

    zero = jnp.zeros((BLK, slots), f32)
    center = jnp.sum(lax.fori_loop(0, steps, sum_body, zero, unroll=2), axis=0, keepdims=True) / width

    def square_body(i, acc):
        return acc + fold(jnp.square(x_ref[pl.ds(i * chunk, chunk), :].astype(f32) - center))

    spread = jnp.sum(lax.fori_loop(0, steps, square_body, zero, unroll=2), axis=0, keepdims=True) / width
    row_scale = lax.rsqrt(spread + epsilon)
    stats_ref[...] = jnp.zeros_like(stats_ref)
    stats_ref[0:1, :] = center
    stats_ref[1:2, :] = row_scale

    def norm_body(i, carry):
        at = pl.ds(i * chunk, chunk)
        standard = (x_ref[at, :].astype(f32) - center) * row_scale
        normed_ref[at, :] = (standard * gb_ref[at, 0:1] + gb_ref[at, 1:2]).astype(bf16)
        return carry

    lax.fori_loop(0, steps, norm_body, 0, unroll=2)

    glu_s[...] = jnp.zeros_like(glu_s)
    dc_s[...] = jnp.zeros_like(dc_s)
    normed = normed_ref[...]
    linear = dot_general(win_ref[0], normed, 1, 0)
    gate_sigmoid = jax.nn.sigmoid(dot_general(win_ref[1], normed, 1, 0))
    lin_s[...] = linear
    sig_s[...] = gate_sigmoid
    is_live = lax.broadcasted_iota(jnp.int32, (part, slots), 1) < live
    glu = jnp.where(is_live, (linear * gate_sigmoid).astype(bf16).astype(f32), 0.0)
    glu_s[0, EDGE : EDGE + slots, :] = jnp.transpose(glu[0:LANES])
    glu_s[1, EDGE : EDGE + slots, 0:rest] = jnp.transpose(glu[LANES:part])

    w_s[...] = jnp.zeros_like(w_s)
    w_s[0] = taps_ref[:, 0:LANES]
    w_s[1, :, 0:rest] = taps_ref[:, LANES:part]
    bn_s[...] = jnp.zeros_like(bn_s)
    bn_s[0, 0:1, :] = scale_ref[:, 0:LANES]
    bn_s[1, 0:1, 0:rest] = scale_ref[:, LANES:part]
    bn_s[0, 1:2, :] = shift_ref[:, 0:LANES]
    bn_s[1, 1:2, 0:rest] = shift_ref[:, LANES:part]
    seg_s[...] = jnp.full(seg_s.shape, -1, jnp.int32)
    seg_s[EDGE : EDGE + slots, :] = jnp.broadcast_to(seg_ref[...], (slots, LANES))

    rows = 64
    blocks = slots // rows

    def conv_body(i, carry):
        base = pl.multiple_of(i * rows, rows)
        here = seg_s[pl.ds(base + EDGE, rows), :]
        acc = [jnp.zeros((rows, LANES), f32) for _ in range(2)]
        for j in range(taps):
            same = seg_s[pl.ds(base + j, rows), :] == here
            for h in range(2):
                value = jnp.where(same, glu_s[h, pl.ds(base + j, rows), :], 0.0)
                acc[h] = acc[h] + value * w_s[h, j : j + 1, :]
        for h in range(2):
            pre_s[h, pl.ds(base, rows), :] = acc[h] * bn_s[h, 0:1, :] + bn_s[h, 1:2, :]
        return carry

    lax.fori_loop(0, blocks, conv_body, 0)

    delta_swish = dot_general(delta_ref[...], wout_ref[...], 1, 1)
    row_live = lax.broadcasted_iota(jnp.int32, (slots, LANES), 0) < live
    for h in range(2):
        pre = pre_s[h]
        s = jax.nn.sigmoid(pre)
        swish = jnp.where(row_live, pre * s, 0.0).astype(bf16)
        slope = jnp.where(row_live, s * (1.0 + pre * (1.0 - s)) * bn_s[h, 0:1, :], 0.0)
        if h == 0:
            swish_ref[:, 0:LANES] = swish
            dc_s[h, EDGE : EDGE + slots, :] = delta_swish[:, 0:LANES] * slope
        else:
            swish_ref[:, LANES:part] = swish[:, 0:rest]
            dc_s[h, EDGE : EDGE + slots, 0:rest] = delta_swish[:, LANES:part] * slope[:, 0:rest]

    tap_s[...] = jnp.zeros_like(tap_s)

    def back_body(i, carry):
        base = pl.multiple_of(i * rows, rows)
        here = seg_s[pl.ds(base + EDGE, rows), :]
        alive = (base + lax.broadcasted_iota(jnp.int32, (rows, LANES), 0)) < live
        glu_here = [glu_s[h, pl.ds(base + EDGE, rows), :] for h in range(2)]
        acc = [jnp.zeros((rows, LANES), f32) for _ in range(2)]
        for j in range(taps):
            at = pl.ds(base + (2 * EDGE - j), rows)
            same = seg_s[at, :] == here
            for h in range(2):
                value = jnp.where(same, dc_s[h, at, :], 0.0)
                acc[h] = acc[h] + value * w_s[h, j : j + 1, :]
                tap_s[h, j] += jnp.sum((value * glu_here[h]).reshape(rows // BLK, BLK, LANES), axis=0)
        for h in range(2):
            dglu_s[h, pl.ds(base, rows), :] = jnp.where(alive, acc[h], 0.0)
        return carry

    lax.fori_loop(0, blocks, back_body, 0)
    for h in range(2):
        tap_ref[h] = jnp.sum(tap_s[h], axis=1)

    for h, (c, e) in enumerate(((0, LANES), (LANES, part))):
        dglu = jnp.transpose(dglu_s[h])[0 : e - c]
        s = sig_s[c:e, :]
        dlt_ref[0, c:e, :] = (dglu * s).astype(bf16)
        dlt_ref[1, c:e, :] = (dglu * lin_s[c:e, :] * s * (1.0 - s)).astype(bf16)

    unit = jnp.zeros((BLK, slots), f32)
    cross = jnp.zeros((BLK, slots), f32)
    wide = 256
    for d in range(0, width, wide):
        term = dot_general(win_ref[0, :, d : d + wide], dlt_ref[0], 0, 0)
        term = term + dot_general(win_ref[1, :, d : d + wide], dlt_ref[1], 0, 0)
        term = term.astype(bf16)
        back_ref[d : d + wide, :] = term
        weighted = term.astype(f32) * gb_ref[d : d + wide, 0:1]
        standard = (x_ref[d : d + wide, :].astype(f32) - center) * row_scale
        unit = unit + jnp.sum(weighted.reshape(wide // BLK, BLK, slots), axis=0)
        cross = cross + jnp.sum((weighted * standard).reshape(wide // BLK, BLK, slots), axis=0)
    totals_ref[0:1, :] = jnp.sum(unit, axis=0, keepdims=True)
    totals_ref[1:2, :] = jnp.sum(cross, axis=0, keepdims=True)


def weight_kernel(normed_ref, swish_ref, dlt_ref, delta_ref, wout_ref, tap_ref, mixed_ref, grad_ref):
    width = normed_ref.shape[0]
    part = swish_ref.shape[1]
    taps = tap_ref.shape[1]
    rest = part - LANES
    pieces = grad_ref.shape[0]
    per = part // BLK
    extra = grad_ref.shape[2] - width
    cols = 512
    mixed_ref[...] = dot_general(swish_ref[...], wout_ref[...], 1, 0).astype(bf16)
    swish_t = jnp.transpose(swish_ref[...].astype(f32)).astype(bf16)
    for d in range(0, width, cols):
        for k in range(2):
            block = dot_general(dlt_ref[k], normed_ref[d : d + cols, :], 1, 1).astype(bf16)
            grad_ref[k * per : (k + 1) * per, :, d : d + cols] = block.reshape(per, BLK, cols)
        block = dot_general(swish_t, delta_ref[:, d : d + cols], 1, 0).astype(bf16)
        left = pieces - 2 * per
        grad_ref[2 * per : pieces, :, d : d + cols] = block[0 : left * BLK].reshape(left, BLK, cols)
        over = block[left * BLK :].reshape(per - left, BLK, cols)
        for r in range(per - left):
            for c in range(0, cols, extra):
                at = r * (width // extra) + (d + c) // extra
                grad_ref[at, :, width : width + extra] = over[r, :, c : c + extra]
    first = (per - left) * (width // extra)
    grad_ref[first:pieces, :, width : width + extra] = jnp.zeros((pieces - first, BLK, extra), bf16)
    for r in range(taps // BLK):
        at = slice(r * BLK, (r + 1) * BLK)
        grad_ref[first + r, :, width : width + LANES] = tap_ref[0, at, :].astype(bf16)
        grad_ref[first + r, :, width + LANES : width + part] = tap_ref[1, at, 0:rest].astype(bf16)


def row_kernel(scalars, dn_ref, x_ref, stats_ref, totals_ref, gain_ref, delta_ref, out_ref, held):
    start, blocks = scalars[0], scalars[1]
    part, slots = dn_ref.shape
    width = scalars[2].astype(f32)
    rest = part - LANES
    count = slots // BLK
    live = blocks * BLK
    side = jnp.concatenate([stats_ref[0:2, :], totals_ref[...], jnp.zeros((4, slots), f32)], axis=0)
    side = jnp.transpose(side)
    center, row_scale = side[:, 0:1], side[:, 1:2]
    unit, cross = side[:, 2:3] / width, side[:, 3:4] / width
    sums = []
    for h, (c, e) in enumerate(((0, LANES), (LANES, part))):
        dn = jnp.transpose(dn_ref[c:e, :].astype(f32))
        standard = (x_ref[:, c:e].astype(f32) - center) * row_scale
        sums.append((jnp.sum(dn * standard, axis=0, keepdims=True), jnp.sum(dn, axis=0, keepdims=True)))
        on = lax.broadcasted_iota(jnp.int32, (slots, e - c), 0) < live
        own = jnp.where(on, delta_ref[:, c:e].astype(f32), 0.0)
        held[h, :, 0 : e - c] = own + row_scale * (dn * gain_ref[:, c:e] - unit - standard * cross)
    held[1, :, rest:LANES] = jnp.zeros((slots, LANES - rest), f32)
    row = lax.broadcasted_iota(jnp.int32, (BLK, LANES), 0)
    lane = lax.broadcasted_iota(jnp.int32, (BLK, LANES), 1)
    beside = jnp.zeros((BLK, LANES), f32)
    for k in range(2):
        low = jnp.broadcast_to(sums[0][k], (BLK, LANES))
        high = jnp.broadcast_to(jnp.concatenate([sums[1][k], sums[1][k]], axis=1), (BLK, LANES))
        beside = jnp.where(row == 3 * k, pltpu.roll(low, 64, 1), beside)
        beside = jnp.where(row == 3 * k + 1, low, beside)
        beside = jnp.where(row == 3 * k + 2, high, beside)
    for s in range(count):
        at = pl.ds(pl.multiple_of(lax.rem(s - start + 16 * count, count) * BLK, BLK), BLK)
        out_ref[s, :, 0:LANES] = held[0, at, :].astype(bf16)
        out_ref[s, :, LANES : 2 * LANES] = jnp.where(lane < rest, held[1, at, :], beside).astype(bf16)


def on_device(
    frames,
    norm_gain,
    norm_bias,
    input_weight,
    depth_weight,
    batch_scale,
    batch_shift,
    output_weight,
    upstream,
    replica_blocks,
    segment,
):
    replicas = lax.axis_size(DP)
    my_index = lax.axis_index(DP)
    tensor_index = lax.axis_index(TENSOR)
    width = norm_gain.shape[0]
    load_rows, part = frames.shape
    slots = segment.shape[0]
    rows_part = upstream.shape[0]
    taps = depth_weight.shape[0]
    load_blocks = load_rows // BLK
    count = slots // BLK

    delta = lax.all_gather(upstream, TENSOR, axis=0, tiled=True)

    ends = jnp.cumsum(replica_blocks)
    starts = ends - replica_blocks
    send = jnp.clip((starts - my_index + replicas - 1) // replicas, 0, load_blocks - 1)
    numbers = my_index + replicas * jnp.arange(load_blocks, dtype=jnp.int32)
    target = jnp.sum((ends[None, :] <= numbers[:, None]).astype(jnp.int32), axis=1)
    is_mine = jnp.arange(replicas, dtype=jnp.int32) == my_index
    my_start = jnp.sum(jnp.where(is_mine, starts, 0))
    my_blocks = jnp.sum(jnp.where(is_mine, replica_blocks, 0))
    scalars = jnp.stack([lax.rem(my_start, replicas), my_blocks, jnp.int32(width)])

    outbox = frames.reshape(load_blocks, BLK, part)[send]
    arrived = lax.all_to_all(outbox, DP, split_axis=0, concat_axis=0, tiled=True)

    sds = jax.ShapeDtypeStruct
    packed, packed_t = full_call(
        pack_kernel,
        (sds((slots, part), bf16), sds((part, slots), bf16)),
        [pltpu.VMEM((slots, part), f32)],
        1,
        1000,
        1000000,
    )(scalars, arrived)
    gathered = lax.all_gather(packed_t, TENSOR, axis=0, tiled=True)

    both = jnp.stack([norm_gain, norm_bias], axis=1)
    normed, swish, dlt, back, tap, stats, totals = full_call(
        main_kernel,
        (
            sds((width, slots), bf16),
            sds((slots, part), bf16),
            sds((2, part, slots), bf16),
            sds((width, slots), bf16),
            sds((2, taps, LANES), f32),
            sds((BLK, slots), f32),
            sds((2, slots), f32),
        ),
        [
            pltpu.VMEM((2, slots + 2 * EDGE, LANES), f32),
            pltpu.VMEM((2, slots + 2 * EDGE, LANES), f32),
            pltpu.VMEM((slots + 2 * EDGE, LANES), jnp.int32),
            pltpu.VMEM((2, taps, LANES), f32),
            pltpu.VMEM((2, BLK, LANES), f32),
            pltpu.VMEM((2, slots, LANES), f32),
            pltpu.VMEM((2, slots, LANES), f32),
            pltpu.VMEM((part, slots), f32),
            pltpu.VMEM((part, slots), f32),
            pltpu.VMEM((2, taps, BLK, LANES), f32),
        ],
        1,
        2000000000,
        10000000,
    )(
        scalars,
        gathered,
        both,
        input_weight,
        depth_weight,
        batch_scale[None],
        batch_shift[None],
        segment[:, None],
        delta,
        output_weight,
    )
    delta_normed = lax.psum_scatter(back, TENSOR, scatter_dimension=0, tiled=True)
    totals = lax.psum(totals, TENSOR)

    pieces = replicas
    mixed, grads = full_call(
        weight_kernel,
        (sds((slots, width), bf16), sds((pieces, BLK, width + 2 * LANES), bf16)),
        [],
        0,
        1500000000,
        8000000,
    )(normed, swish, dlt, delta, output_weight, tap)
    mixed_sum = lax.psum_scatter(mixed, TENSOR, scatter_dimension=0, tiled=True)

    grads = lax.all_to_all(grads, DP, split_axis=0, concat_axis=0, tiled=True)
    mine = jnp.sum(grads.astype(f32), axis=0).astype(bf16)
    spread = jnp.broadcast_to(mine[None], (pieces,) + mine.shape)

    column_start = tensor_index * part
    gain_part = lax.dynamic_slice_in_dim(norm_gain, column_start, part)[None]
    delta_part = lax.dynamic_slice_in_dim(delta, column_start, part, 1)
    homebound = full_call(
        row_kernel,
        sds((count, BLK, 2 * LANES), bf16),
        [pltpu.VMEM((2, slots, LANES), f32)],
        1,
        1000000,
        1000000,
    )(scalars, delta_normed, packed, stats, totals, gain_part, delta_part)
    returned = lax.all_to_all(homebound, DP, split_axis=0, concat_axis=0, tiled=True)
    frame_gradient = returned[target][:, :, :part].reshape(load_rows, part)
    side = jnp.sum(returned[:, 0:6, part:].astype(f32), axis=0).reshape(2, part)

    whole = lax.all_to_all(spread, DP, split_axis=0, concat_axis=0, tiled=True)
    per = part // BLK
    weight_grad = whole[: 2 * per, :, :width].reshape(2, part, width)
    over = whole[: 2 * per, :, width:].reshape(BLK, 6, BLK, 2 * LANES)
    over = over.transpose(0, 2, 1, 3).reshape(BLK * BLK, width)
    out_grad = jnp.concatenate([whole[2 * per :, :, :width].reshape(-1, width), over], axis=0)
    tap_grad = whole[2 * per : 2 * per + taps // BLK, :, width : width + part]
    tap_grad = tap_grad.reshape(taps, part).astype(f32)

    row_start = tensor_index * rows_part
    live_mine = (row_start + jnp.arange(rows_part, dtype=jnp.int32) < my_blocks * BLK)[:, None]
    residual = lax.dynamic_slice_in_dim(gathered, row_start, rows_part, 1).T
    block_output = jnp.where(
        live_mine, residual.astype(f32) + mixed_sum.astype(f32), 0.0
    ).astype(bf16)
    return (block_output, frame_gradient, weight_grad, out_grad, tap_grad, side[0], side[1])


def solution(mesh):
    fine = Mesh(mesh.devices.reshape(2, 8, 4, 4, 2), DP + TENSOR)
    in_specs = (
        P(DP, TENSOR),
        P(),
        P(),
        P(None, TENSOR, None),
        P(None, TENSOR),
        P(TENSOR),
        P(TENSOR),
        P(TENSOR, None),
        P(DP + TENSOR, None),
        P(),
        P(DP),
    )
    out_specs = (
        P(DP + TENSOR, None),
        P(DP, TENSOR),
        P(None, TENSOR, None),
        P(TENSOR, None),
        P(None, TENSOR),
        P(TENSOR),
        P(TENSOR),
    )
    return jax.shard_map(
        on_device, mesh=fine, in_specs=in_specs, out_specs=out_specs, check_vma=False
    )
```

time: 843 us -> 302 us (0.36)
  the two profiles are of different devices: /device:TPU:192 before, /device:TPU:38 now
where the time goes in v1:
time: 302 us; the launch traced here: 301 us
  waiting for transfers between devices  134 us (44%)
  starting transfers between devices  56.9 us (19%)
  blocking collectives  50.8 us (17%)
  Pallas kernels  19.5 us (6%)
  between operations  16.7 us (6%)
  local copies, waits for them, and re-layouts  15.3 us (5%)
  other arithmetic  7.55 us (2%)
    psum x1, blocking collectives, on_device(): totals = lax.psum(totals, TENSOR)  50.8 us
    reduce_scatter x1, waiting for transfers between devices, on_device(): mixed_sum = lax.psum_scatter(mixed, TENSOR, scatter_dimension=0, tiled=True)  45.6 us
    all_gather x1, waiting for transfers between devices, on_device(): gathered = lax.all_gather(packed_t, TENSOR, axis=0, tiled=True)  44.8 us
    pallas_call x4, Pallas kernels, call(): pl.pallas_call(kernel, out_shape=out_shape, in_specs=specs, out_specs=out...  19.5 us
    all_to_all x1, starting transfers between devices, on_device(): lax.all_to_all(outbox, DP, split_axis=0, concat_axis=0, tiled=True)  18.6 us
    all_to_all x1, starting transfers between devices, on_device(): lax.all_to_all(homebound, DP, split_axis=0, concat_axis=0, tiled=True)  14 us
    all_to_all x1, starting transfers between devices, on_device(): grads = lax.all_to_all(grads, DP, split_axis=0, concat_axis=0, tiled=True)  13.8 us
    all_gather x1, waiting for transfers between devices, on_device(): delta = lax.all_gather(upstream, TENSOR, axis=0, tiled=True)  12.7 us
  transfers between devices with their start and end apart: 8, of which 6 were waited for; matrix products, arithmetic and copies ran while one was open for 5% of the time, Pallas kernels for 1%

profile of v1, /device:TPU:38, one launch (start us, length us, event | category | flops | bytes accessed | tf_op | source)
XLA Modules:
  0.0 301.0 jit_solution(11315842907353444509)
XLA Ops:
  10.0 1.3 fusion.4
  11.3 1.3 gather_fusion
  12.6 18.6 %all-to-all-start = ((bf16[64,8,192]{2,1,0:T(8,128)(2,1)}), bf16[64,8,192]{2,1,0:T(8,128)(2,1)S(1)}, u32[]{:S(2)}, u32[]{:S(2)}) async-start(bf16[64,8,192]{2,1,0:T(8,128)(2,1)} %gather_fusion), calls=%async_computation | async-start | bytes 524288 | tf_op jit(solution)/shard_map/all_to_all | solution.py:328
  33.9 9.4 %all-to-all-done.arrived = bf16[64,8,192]{2,1,0:T(8,128)(2,1)S(1)} async-done(((bf16[64,8,192]{2,1,0:T(8,128)(2,1)}), bf16[64,8,192]{2,1,0:T(8,128)(2,1)S(1)}, u32[]{:S(2)}, u32[]{:S(2)}) %all-to-all-start) | async-done | bytes 196640 | tf_op jit(solution)/shard_map/all_to_all | solution.py:328
  43.3 1.5 shard_map.162
  45.4 12.7 %all-gather.5.cloned.1.call-done.delta_ref = bf16[512,1536]{1,0:T(8,128)(2,1)} async-done(((bf16[64,1536]{1,0:T(8,128)(2,1)}), bf16[512,1536]{1,0:T(8,128)(2,1)}) %all-gather.5.cloned.1.call-update) | async-done | bytes 1572880 | tf_op jit(solution)/shard_map/all_gather | solution.py:315
  58.1 44.8 %all-gather.3.cloned.1.call-done.x_ref = bf16[1536,512]{1,0:T(8,128)(2,1)} async-done(((bf16[192,512]{1,0:T(8,128)(2,1)}), bf16[1536,512]{1,0:T(8,128)(2,1)}) %all-gather.3.cloned.1.call-update) | async-done | bytes 1572880 | tf_op jit(solution)/shard_map/all_gather | solution.py:339
  103.0 1.4 copy-done.1
  104.4 1.4 copy-done.2
  105.8 1.3 copy-done.4
  107.1 12.9 %shard_map.163 = (bf16[1536,512]{1,0:T(8,128)(2,1)S(1)}, bf16[512,192]{1,0:T(8,128)(2,1)S(1)}, bf16[2,192,512]{2,1,0:T(8,128)(2,1)S(1)}, bf16[1536,512]{1,0:T(8,...) custom-call(s32[3]{0:T(128)S(1)} %pad_add_fusion.scalars, ...), custom_call_target="tpu_custom_call" | custom-call | flops 2000000000 | bytes 10000000 | tf_op jit(solution)/shard_map/pallas_call | solution.py:32
  119.9 3.1 %shard_map.164 = (bf16[512,1536]{1,0:T(8,128)(2,1)}, bf16[64,8,1792]{2,1,0:T(8,128)(2,1)}) custom-call(bf16[1536,512]{1,0:T(8,128)(2,1)S(1)} %get-tuple-element.19.normed_ref, bf16[512,192]{1,0:T(8,128)(2,1)S(1)} %get-tuple-element.20.swish_ref, bf16[2,192,512]{2,1,0:T(8,128)(2,1)S(1)} %get-tuple-element.21.dlt_ref, bf16[512,1536]{1,0:T(8,128)(2,1)S(1)} %copy-done.3, ...), custom_call_target="tpu_custom_call" | custom-call | flops 1500000000 | bytes 8000000 | tf_op jit(solution)/shard_map/pallas_call | solution.py:32
  123.1 13.8 %all-to-all-start.2 = ((bf16[64,8,1792]{2,1,0:T(8,128)(2,1)}), bf16[64,8,1792]{2,1,0:T(8,128)(2,1)}, u32[]{:S(2)}, u32[]{:S(2)}) async-start(bf16[64,8,1792]{2,1,0:T(8,128)(2,1)} %get-tuple-element.28), calls=%async_computation.4 | async-start | bytes 3670016 | tf_op jit(solution)/shard_map/all_to_all | solution.py:394
  138.3 50.8 %psum.7.totals_ref = f32[2,512]{1,0:T(2,128)S(1)} all-reduce(f32[2,512]{1,0:T(2,128)S(1)} %get-tuple-element.27), channel_id=1, replica_groups=mesh['zh'=2,'y'=8,'x'=4,'zl'=4,'core'=2] {'zl','core'}, use_global_device_ids=true, to_apply=%region_5.6 | all-reduce | flops 1024 | bytes 8192 | tf_op jit(solution)/shard_map/psum | solution.py:381
  189.1 11.4 %reduce-scatter.5.cloned.1.call-done.dn_ref = bf16[192,512]{1,0:T(8,128)(2,1)} async-done(((bf16[1536,512]{1,0:T(8,128)(2,1)}), bf16[192,512]{1,0:T(8,128)(2,1)}) %reduce-scatter.5.cloned.1.call-update) | async-done | bytes 196624 | tf_op jit(solution)/shard_map/reduce_scatter | solution.py:380
  201.5 2.0 shard_map.165
  203.5 14.0 %all-to-all-start.1 = ((bf16[64,8,256]{2,1,0:T(8,128)(2,1)}), bf16[64,8,256]{2,1,0:T(8,128)(2,1)S(1)}, u32[]{:S(2)}, u32[]{:S(2)}) async-start(bf16[64,8,256]{2,1,0:T(8,128)(2,1)} %shard_map.165), calls=%async_computation.3 | async-start | bytes 524288 | tf_op jit(solution)/shard_map/all_to_all | solution.py:409
  217.5 1.8 reduce_sum.54
  219.3 8.6 %all-to-all-done.1 = bf16[64,8,256]{2,1,0:T(8,128)(2,1)S(1)} async-done(((bf16[64,8,256]{2,1,0:T(8,128)(2,1)}), bf16[64,8,256]{2,1,0:T(8,128)(2,1)S(1)}, u32[]{:S(2)}, u32[]{:S(2)}) %all-to-all-start.1) | async-done | bytes 262176 | tf_op jit(solution)/shard_map/all_to_all | solution.py:409
  227.9 1.4 broadcast_in_dim.50
  229.2 10.3 %all-to-all-start.3 = ((bf16[64,8,1792]{2,1,0:T(8,128)(2,1)}), bf16[64,8,1792]{2,1,0:T(8,128)(2,1)S(1)}, u32[]{:S(2)}, u32[]{:S(2)}) async-start(bf16[64,8,1792]{2,1,0:T(8,128)(2,1)} %broadcast_in_dim.50), calls=%async_computation.5 | async-start | bytes 3670016 | tf_op jit(solution)/shard_map/all_to_all | solution.py:413
  240.4 1.2 constant_dynamic-slice_fusion.1
  241.7 45.6 %reduce-scatter.3.cloned.1.call-done = bf16[64,1536]{1,0:T(8,128)(2,1)} async-done(((bf16[512,1536]{1,0:T(8,128)(2,1)}), bf16[64,1536]{1,0:T(8,128)(2,1)}) %reduce-scatter.3.cloned.1.call-update) | async-done | bytes 196624 | tf_op jit(solution)/shard_map/reduce_scatter | solution.py:392
  287.3 1.7 fusion.1
  (62 shorter events, 12.1 us)
Async XLA Ops:
  7.2 37.7 %copy-start.10 = (f32[1536]{0:T(1024)S(1)}, f32[1536]{0:T(1024)}, u32[]{:S(2)}) copy-start(f32[1536]{0:T(1024)} %param.13) | copy-start | bytes 18436
  7.2 37.7 %copy-start.9 = (f32[1536]{0:T(1024)S(1)}, f32[1536]{0:T(1024)}, u32[]{:S(2)}) copy-start(f32[1536]{0:T(1024)} %param.12) | copy-start | bytes 18436
  7.2 38.1 %copy-start.11 = (s32[512]{0:T(512)S(1)}, s32[512]{0:T(512)}, u32[]{:S(2)}) copy-start(s32[512]{0:T(512)} %param.21) | copy-start | bytes 6148
  7.2 50.9 %all-gather.5.cloned.1.call-start = ((), (), s32[]{:S(2)}) async-start(), calls=%async_computation.7 | async-start | bytes 1769472 | tf_op jit(solution)/shard_map/all_gather | solution.py:315
  7.9 95.0 %copy-start.5 = (bf16[192,1536]{1,0:T(8,128)(2,1)S(1)}, bf16[192,1536]{1,0:T(8,128)(2,1)}, u32[]{:S(2)}) copy-start(bf16[192,1536]{1,0:T(8,128)(2,1)} %wout_ref.3) | copy-start | bytes 1769476
  7.9 95.0 %copy-start.6 = (f32[32,192]{1,0:T(8,128)S(1)}, f32[32,192]{1,0:T(8,128)}, u32[]{:S(2)}) copy-start(f32[32,192]{1,0:T(8,128)} %taps_ref.1) | copy-start | bytes 73732
  8.0 95.0 %copy-start.7 = (f32[192]{0:T(256)S(1)}, f32[192]{0:T(256)}, u32[]{:S(2)}) copy-start(f32[192]{0:T(256)} %param.16) | copy-start | bytes 2308
  8.0 95.0 %copy-start.8 = (f32[192]{0:T(256)S(1)}, f32[192]{0:T(256)}, u32[]{:S(2)}) copy-start(f32[192]{0:T(256)} %param.17) | copy-start | bytes 2308
  12.6 30.7 %all-to-all-start = ((bf16[64,8,192]{2,1,0:T(8,128)(2,1)}), bf16[64,8,192]{2,1,0:T(8,128)(2,1)S(1)}, u32[]{:S(2)}, u32[]{:S(2)}) async-start(bf16[64,8,192]{2,1,0:T(8,128)(2,1)} %gather_fusion), calls=%async_computation | async-start | bytes 524288 | tf_op jit(solution)/shard_map/all_to_all | solution.py:328
  31.2 71.7 %all-gather.3.cloned.1.call-start = ((), (), s32[]{:S(2)}) async-start(), calls=%async_computation.6 | async-start | bytes 1769472 | tf_op jit(solution)/shard_map/all_gather | solution.py:339
  103.0 1.4 copy-start.1
  104.4 1.4 copy-start.2
  105.8 1.3 copy-start.4
  107.1 12.9 %copy-start.3 = (bf16[512,1536]{1,0:T(8,128)(2,1)S(1)}, bf16[512,1536]{1,0:T(8,128)(2,1)}, u32[]{:S(2)}) copy-start(bf16[512,1536]{1,0:T(8,128)(2,1)} %all-gather.5.cloned.1.call-done.delta_ref) | copy-start | bytes 4718596
  123.1 80.4 %all-to-all-start.2 = ((bf16[64,8,1792]{2,1,0:T(8,128)(2,1)}), bf16[64,8,1792]{2,1,0:T(8,128)(2,1)}, u32[]{:S(2)}, u32[]{:S(2)}) async-start(bf16[64,8,1792]{2,1,0:T(8,128)(2,1)} %get-tuple-element.28), calls=%async_computation.4 | async-start | bytes 3670016 | tf_op jit(solution)/shard_map/all_to_all | solution.py:394
  136.9 63.7 %reduce-scatter.5.cloned.1.call-start = ((), (), s32[]{:S(2)}) async-start(), calls=%async_computation.9 | async-start | bytes 1769472 | tf_op jit(solution)/shard_map/reduce_scatter | solution.py:380
  137.6 149.7 %reduce-scatter.3.cloned.1.call-start = ((), (), s32[]{:S(2)}) async-start(), calls=%async_computation.8 | async-start | bytes 1769472 | tf_op jit(solution)/shard_map/reduce_scatter | solution.py:392
  200.6 0.9 copy-start
  203.5 24.4 %all-to-all-start.1 = ((bf16[64,8,256]{2,1,0:T(8,128)(2,1)}), bf16[64,8,256]{2,1,0:T(8,128)(2,1)S(1)}, u32[]{:S(2)}, u32[]{:S(2)}) async-start(bf16[64,8,256]{2,1,0:T(8,128)(2,1)} %shard_map.165), calls=%async_computation.3 | async-start | bytes 524288 | tf_op jit(solution)/shard_map/all_to_all | solution.py:409
  229.2 62.6 %all-to-all-start.3 = ((bf16[64,8,1792]{2,1,0:T(8,128)(2,1)}), bf16[64,8,1792]{2,1,0:T(8,128)(2,1)S(1)}, u32[]{:S(2)}, u32[]{:S(2)}) async-start(bf16[64,8,1792]{2,1,0:T(8,128)(2,1)} %broadcast_in_dim.50), calls=%async_computation.5 | async-start | bytes 3670016 | tf_op jit(solution)/shard_map/all_to_all | solution.py:413
Sparse Core Ops, SparseCore 0:
  10.1 47.9 all-gather.4
  60.8 42.1 all-gather.2
  140.5 59.9 reduce-scatter.4
  203.3 84.0 reduce-scatter.2

commit v2 on v1

--- a/solution.py
+++ b/solution.py
@@ -11,11 +11,13 @@
 BLK = 8
 LANES = 128
 EDGE = 16
+SIDE = 16
 epsilon = 1e-05
-VMEM_LIMIT = 40 * 1024 * 1024
+MIB = 1024 * 1024
 
 f32 = jnp.float32
 bf16 = jnp.bfloat16
+SWAP = ((0, 1), (1, 0))
 DP = ("zh", "y", "x")
 TENSOR = ("zl", "core")
 
@@ -24,22 +26,39 @@
     return lax.dot_general(a, b, (((ca,), (cb,)), ((), ())), preferred_element_type=f32)
 
 
-def full_call(kernel, out_shape, scratch, smem, flops, nbytes):
+def full_call(kernel, out_shape, scratch, smem, flops, nbytes, copied=(), sent=(), room=16):
     def call(*args):
         specs = [pl.BlockSpec(memory_space=pltpu.SMEM)] * smem
         specs += [pl.BlockSpec(memory_space=pltpu.VMEM)] * (len(args) - smem)
+        for place in copied:
+            specs[place] = pl.BlockSpec(memory_space=pl.ANY)
         outs = jax.tree.map(lambda _: pl.BlockSpec(memory_space=pltpu.VMEM), out_shape)
+        if sent:
+            outs = tuple(
+                pl.BlockSpec(memory_space=pl.ANY if k in sent else pltpu.VMEM)
+                for k in range(len(out_shape))
+            )
         return pl.pallas_call(
             kernel,
             out_shape=out_shape,
             in_specs=specs,
             out_specs=outs,
             scratch_shapes=scratch,
-            compiler_params=pltpu.CompilerParams(vmem_limit_bytes=VMEM_LIMIT),
+            compiler_params=pltpu.CompilerParams(vmem_limit_bytes=room * MIB),
             cost_estimate=pl.CostEstimate(flops=flops, bytes_accessed=nbytes, transcendentals=0),
         )(*args)
 
     return call
+
+
+def outbox_kernel(send, frames_t, out_ref, held):
+    part = frames_t.shape[0]
+    for c in range(0, part, LANES):
+        e = min(part, c + LANES)
+        held[:, c:e] = jnp.transpose(frames_t[c:e, :].astype(f32))
+    for r in range(out_ref.shape[0]):
+        at = pl.ds(pl.multiple_of(send[r] * BLK, BLK), BLK)
+        out_ref[r] = held[at, :].astype(bf16)
 
 
 def pack_kernel(scalars, arrived, rows_out, cols_out, held):
@@ -55,28 +74,36 @@
         cols_out[c:e, :] = jnp.transpose(held[:, c:e]).astype(bf16)
 
 
-def shift_masks(seg_s, base, offset, step, rows):
-    return seg_s[pl.ds(base + offset, rows), :] == seg_s[pl.ds(base + EDGE, rows), :]
+def split_rows(unit, cross):
+    row = lax.broadcasted_iota(jnp.int32, (SIDE, unit.shape[1]), 0)
+    out = jnp.zeros((SIDE, unit.shape[1]), f32)
+    for k, value in enumerate((unit, cross)):
+        high = value.astype(bf16).astype(f32)
+        out = jnp.where(row == 2 * k, high, out)
+        out = jnp.where(row == 2 * k + 1, value - high, out)
+    return out.astype(bf16)
 
 
 def main_kernel(
     scalars,
-    x_ref,
+    own_hbm,
+    other_hbm,
     gb_ref,
-    win_ref,
+    win_hbm,
     taps_ref,
     scale_ref,
     shift_ref,
     seg_ref,
-    delta_ref,
-    wout_ref,
-    normed_ref,
-    swish_ref,
-    dlt_ref,
-    back_ref,
+    delta_hbm,
+    wout_hbm,
+    x_hbm,
+    normed_hbm,
+    swish_hbm,
+    dlt_hbm,
+    keep_hbm,
+    send_hbm,
     tap_ref,
     stats_ref,
-    totals_ref,
     glu_s,
     dc_s,
     seg_s,
@@ -87,52 +114,50 @@
     lin_s,
     sig_s,
     tap_s,
+    own_ref,
+    other_ref,
+    win_ref,
+    delta_ref,
+    wout_ref,
+    x_ref,
+    normed_ref,
+    swish_ref,
+    dlt_ref,
+    keep_ref,
+    send_ref,
+    sems,
+    out_sems,
 ):
+    def send(k, source, target):
+        copy = pltpu.make_async_copy(source, target, out_sems.at[k])
+        copy.start()
+        sends.append(copy)
+
+    sends = []
+    copies = [
+        pltpu.make_async_copy(source, target, sems.at[k])
+        for k, (source, target) in enumerate(
+            (
+                (own_hbm, own_ref),
+                (other_hbm, other_ref),
+                (win_hbm, win_ref),
+                (delta_hbm, delta_ref),
+                (wout_hbm, wout_ref),
+            )
+        )
+    ]
+    for copy in copies:
+        copy.start()
     width, slots = x_ref.shape
     part = win_ref.shape[1]
     taps = taps_ref.shape[0]
     rest = part - LANES
     live = scalars[1] * BLK
+    core = scalars[3]
     chunk = 64
     steps = width // chunk
-
-    def fold(v):
-        return jnp.sum(v.reshape(chunk // BLK, BLK, slots), axis=0)
-
-    def sum_body(i, acc):
-        return acc + fold(x_ref[pl.ds(i * chunk, chunk), :].astype(f32))
-
-    zero = jnp.zeros((BLK, slots), f32)
-    center = jnp.sum(lax.fori_loop(0, steps, sum_body, zero, unroll=2), axis=0, keepdims=True) / width
-
-    def square_body(i, acc):
-        return acc + fold(jnp.square(x_ref[pl.ds(i * chunk, chunk), :].astype(f32) - center))
-
-    spread = jnp.sum(lax.fori_loop(0, steps, square_body, zero, unroll=2), axis=0, keepdims=True) / width
-    row_scale = lax.rsqrt(spread + epsilon)
-    stats_ref[...] = jnp.zeros_like(stats_ref)
-    stats_ref[0:1, :] = center
-    stats_ref[1:2, :] = row_scale
-
-    def norm_body(i, carry):
-        at = pl.ds(i * chunk, chunk)
-        standard = (x_ref[at, :].astype(f32) - center) * row_scale
-        normed_ref[at, :] = (standard * gb_ref[at, 0:1] + gb_ref[at, 1:2]).astype(bf16)
-        return carry
-
-    lax.fori_loop(0, steps, norm_body, 0, unroll=2)
-
-    glu_s[...] = jnp.zeros_like(glu_s)
-    dc_s[...] = jnp.zeros_like(dc_s)
-    normed = normed_ref[...]
-    linear = dot_general(win_ref[0], normed, 1, 0)
-    gate_sigmoid = jax.nn.sigmoid(dot_general(win_ref[1], normed, 1, 0))
-    lin_s[...] = linear
-    sig_s[...] = gate_sigmoid
-    is_live = lax.broadcasted_iota(jnp.int32, (part, slots), 1) < live
-    glu = jnp.where(is_live, (linear * gate_sigmoid).astype(bf16).astype(f32), 0.0)
-    glu_s[0, EDGE : EDGE + slots, :] = jnp.transpose(glu[0:LANES])
-    glu_s[1, EDGE : EDGE + slots, 0:rest] = jnp.transpose(glu[LANES:part])
+    chips = own_ref.shape[0]
+    per_part = part // chunk
 
     w_s[...] = jnp.zeros_like(w_s)
     w_s[0] = taps_ref[:, 0:LANES]
@@ -144,6 +169,61 @@
     bn_s[1, 1:2, 0:rest] = shift_ref[:, LANES:part]
     seg_s[...] = jnp.full(seg_s.shape, -1, jnp.int32)
     seg_s[EDGE : EDGE + slots, :] = jnp.broadcast_to(seg_ref[...], (slots, LANES))
+
+    glu_s[...] = jnp.zeros_like(glu_s)
+    dc_s[...] = jnp.zeros_like(dc_s)
+    tap_s[...] = jnp.zeros_like(tap_s)
+
+    copies[0].wait()
+    copies[1].wait()
+
+    def fold(v):
+        return jnp.sum(v.reshape(chunk // BLK, BLK, slots), axis=0)
+
+    def sum_body(i, acc):
+        chip, row = i // per_part, pl.multiple_of(lax.rem(i, per_part) * chunk, chunk)
+        for ref, c in ((own_ref, core), (other_ref, 1 - core)):
+            value = ref[chip, pl.ds(row, chunk), :]
+            to = pl.multiple_of((2 * chip + c) * part + row, chunk)
+            x_ref[pl.ds(to, chunk), :] = value
+            acc = acc + fold(value.astype(f32))
+        return acc
+
+    zero = jnp.zeros((BLK, slots), f32)
+    center = lax.fori_loop(0, chips * per_part, sum_body, zero)
+    center = jnp.sum(center, axis=0, keepdims=True) / width
+
+    send(0, x_ref, x_hbm)
+
+    def square_body(i, acc):
+        return acc + fold(jnp.square(x_ref[pl.ds(i * chunk, chunk), :].astype(f32) - center))
+
+    spread = jnp.sum(lax.fori_loop(0, steps, square_body, zero, unroll=2), axis=0, keepdims=True) / width
+    row_scale = lax.rsqrt(spread + epsilon)
+    stats_ref[...] = jnp.zeros_like(stats_ref)
+    stats_ref[0:1, :] = center
+    stats_ref[1:2, :] = row_scale
+
+    def norm_body(i, carry):
+        at = pl.ds(i * chunk, chunk)
+        standard = (x_ref[at, :].astype(f32) - center) * row_scale
+        normed_ref[at, :] = (standard * gb_ref[at, 0:1] + gb_ref[at, 1:2]).astype(bf16)
+        return carry
+
+    lax.fori_loop(0, steps, norm_body, 0, unroll=2)
+
+    send(1, normed_ref, normed_hbm)
+
+    copies[2].wait()
+    normed = normed_ref[...]
+    linear = dot_general(win_ref[0], normed, 1, 0)
+    gate_sigmoid = jax.nn.sigmoid(dot_general(win_ref[1], normed, 1, 0))
+    lin_s[...] = linear
+    sig_s[...] = gate_sigmoid
+    is_live = lax.broadcasted_iota(jnp.int32, (part, slots), 1) < live
+    glu = jnp.where(is_live, (linear * gate_sigmoid).astype(bf16).astype(f32), 0.0)
+    glu_s[0, EDGE : EDGE + slots, :] = jnp.transpose(glu[0:LANES])
+    glu_s[1, EDGE : EDGE + slots, 0:rest] = jnp.transpose(glu[LANES:part])
 
     rows = 64
     blocks = slots // rows
@@ -163,6 +243,8 @@
 
     lax.fori_loop(0, blocks, conv_body, 0)
 
+    copies[3].wait()
+    copies[4].wait()
     delta_swish = dot_general(delta_ref[...], wout_ref[...], 1, 1)
     row_live = lax.broadcasted_iota(jnp.int32, (slots, LANES), 0) < live
     for h in range(2):
@@ -177,7 +259,8 @@
             swish_ref[:, LANES:part] = swish[:, 0:rest]
             dc_s[h, EDGE : EDGE + slots, 0:rest] = delta_swish[:, LANES:part] * slope[:, 0:rest]
 
-    tap_s[...] = jnp.zeros_like(tap_s)
+    send(2, swish_ref, swish_hbm)
+
 
     def back_body(i, carry):
         base = pl.multiple_of(i * rows, rows)
@@ -206,23 +289,150 @@
         dlt_ref[0, c:e, :] = (dglu * s).astype(bf16)
         dlt_ref[1, c:e, :] = (dglu * lin_s[c:e, :] * s * (1.0 - s)).astype(bf16)
 
+    send(3, dlt_ref, dlt_hbm)
+
     unit = jnp.zeros((BLK, slots), f32)
     cross = jnp.zeros((BLK, slots), f32)
-    wide = 256
-    for d in range(0, width, wide):
+    wide = 2 * part
+    for z in range(chips):
+        d = z * wide
         term = dot_general(win_ref[0, :, d : d + wide], dlt_ref[0], 0, 0)
         term = term + dot_general(win_ref[1, :, d : d + wide], dlt_ref[1], 0, 0)
         term = term.astype(bf16)
-        back_ref[d : d + wide, :] = term
+        first, second = term[0:part], term[part:wide]
+        keep_ref[z, 0:part, :] = jnp.where(core == 0, first, second)
+        send_ref[z, 0:part, :] = jnp.where(core == 0, second, first)
         weighted = term.astype(f32) * gb_ref[d : d + wide, 0:1]
         standard = (x_ref[d : d + wide, :].astype(f32) - center) * row_scale
         unit = unit + jnp.sum(weighted.reshape(wide // BLK, BLK, slots), axis=0)
         cross = cross + jnp.sum((weighted * standard).reshape(wide // BLK, BLK, slots), axis=0)
-    totals_ref[0:1, :] = jnp.sum(unit, axis=0, keepdims=True)
-    totals_ref[1:2, :] = jnp.sum(cross, axis=0, keepdims=True)
-
-
-def weight_kernel(normed_ref, swish_ref, dlt_ref, delta_ref, wout_ref, tap_ref, mixed_ref, grad_ref):
+    totals = split_rows(
+        jnp.sum(unit, axis=0, keepdims=True), jnp.sum(cross, axis=0, keepdims=True)
+    )
+    for z in range(chips):
+        send_ref[z, part : part + SIDE, :] = totals
+    send(4, send_ref, send_hbm)
+    for z in range(chips):
+        keep_ref[z, part : part + SIDE, :] = totals
+    send(5, keep_ref, keep_hbm)
+    for copy in sends:
+        copy.wait()
+
+
+def pair_kernel(scalars, keep_ref, got_ref, *outs):
+    chips, rows, _ = keep_ref.shape
+    part = rows - SIDE
+    side = keep_ref[0, part:rows, :].astype(f32) + got_ref[0, part:rows, :].astype(f32)
+    totals = split_rows(side[0:1] + side[1:2], side[2:3] + side[3:4])
+    for j in range(chips):
+        z = scalars[4] ^ j
+        total = keep_ref[z, 0:part, :].astype(f32) + got_ref[z, 0:part, :].astype(f32)
+        outs[j][0:part, :] = total.astype(bf16)
+        outs[j][part:rows, :] = totals
+
+
+def sum_kernel(in_ref, out_ref):
+    for k in range(out_ref.shape[0]):
+        total = sum(in_ref[i, k].astype(f32) for i in range(in_ref.shape[0]))
+        out_ref[k] = total.astype(bf16)
+
+
+def share_kernel(in_ref, home_ref, out_ref):
+    peers, _, wide = in_ref.shape
+    lines = home_ref.shape[1]
+    total = sum(in_ref[i].astype(f32) for i in range(peers)).astype(bf16)
+    for i in range(peers):
+        out_ref[i, :, 0:wide] = total
+        for k in range(lines):
+            at = wide + k * 2 * LANES
+            out_ref[i, :, at : at + 2 * LANES] = home_ref[i, k]
+
+
+def unpack_kernel(target, in_ref, weight_ref, out_ref, tap_ref, side_ref, frame_ref, held, turned_rows):
+    pieces, _, full = in_ref.shape
+    taps, part = tap_ref.shape
+    width = weight_ref.shape[1]
+    wide = full - 2 * LANES
+    extra = wide - width
+    per = part // BLK
+    left = pieces - 2 * per
+    cols = 2 * extra
+    for d in range(0, width, cols):
+        weight_ref[:, d : d + cols] = in_ref[0 : 2 * per, :, d : d + cols].reshape(2 * part, cols)
+        out_ref[0 : left * BLK, d : d + cols] = in_ref[2 * per : pieces, :, d : d + cols].reshape(
+            left * BLK, cols
+        )
+    for c in range(0, width, extra):
+        rows = [in_ref[r * (width // extra) + c // extra, :, width:wide] for r in range(per - left)]
+        out_ref[left * BLK : part, c : c + extra] = jnp.concatenate(rows, axis=0)
+    first = (per - left) * (width // extra)
+    for r in range(taps // BLK):
+        tap_ref[r * BLK : (r + 1) * BLK, :] = in_ref[first + r, :, width : width + part].astype(f32)
+    total = jnp.zeros((BLK, LANES), f32)
+    for s in range(pieces):
+        held[s] = in_ref[s, :, wide:full].astype(f32)
+        total = total + held[s, :, LANES:]
+    turned = pltpu.roll(total, LANES - part % LANES, 1)
+    low = lax.broadcasted_iota(jnp.int32, (1, LANES), 1) < part % LANES
+    for k in range(2):
+        side_ref[k : k + 1, 0:LANES] = jnp.where(
+            low, turned[3 * k : 3 * k + 1], total[3 * k + 1 : 3 * k + 2]
+        )
+        side_ref[k : k + 1, LANES:part] = turned[3 * k + 2 : 3 * k + 3, 0 : part - LANES]
+    for k in range(frame_ref.shape[1] // BLK):
+        turned_rows[k * BLK : (k + 1) * BLK, :] = held[target[k]]
+    for c in range(0, part, LANES):
+        e = min(part, c + LANES)
+        frame_ref[c:e, :] = jnp.transpose(turned_rows[:, c:e]).astype(bf16)
+
+
+def fan_kernel(in_ref, out_ref):
+    lines, peers, _, full = out_ref.shape
+    wide = full - 2 * LANES
+    for i in range(peers):
+        piece = in_ref[i, :, 0:wide]
+        for k in range(lines):
+            at = wide + k * 2 * LANES
+            out_ref[k, i, :, 0:wide] = piece
+            out_ref[k, i, :, wide:full] = in_ref[i, :, at : at + 2 * LANES]
+
+
+def weight_kernel(
+    scalars,
+    swish_hbm,
+    wout_hbm,
+    dlt_hbm,
+    normed_hbm,
+    delta_hbm,
+    tap_ref,
+    keep_hbm,
+    send_hbm,
+    grad_hbm,
+    swish_ref,
+    wout_ref,
+    dlt_ref,
+    normed_ref,
+    delta_ref,
+    keep_ref,
+    send_ref,
+    grad_ref,
+    sems,
+    out_sems,
+):
+    inward = (
+        (swish_hbm, swish_ref),
+        (wout_hbm, wout_ref),
+        (dlt_hbm, dlt_ref),
+        (normed_hbm, normed_ref),
+        (delta_hbm, delta_ref),
+    )
+    copies = [
+        pltpu.make_async_copy(source, target, sems.at[k]) for k, (source, target) in enumerate(inward)
+    ]
+    for copy in copies:
+        copy.start()
+    copies[0].wait()
+    copies[1].wait()
     width = normed_ref.shape[0]
     part = swish_ref.shape[1]
     taps = tap_ref.shape[1]
@@ -231,7 +441,22 @@
     per = part // BLK
     extra = grad_ref.shape[2] - width
     cols = 512
-    mixed_ref[...] = dot_general(swish_ref[...], wout_ref[...], 1, 0).astype(bf16)
+    core = scalars[3]
+    chips, half = keep_ref.shape[0:2]
+    for z in range(chips):
+        at = slice(2 * z * half, 2 * (z + 1) * half)
+        term = dot_general(swish_ref[at, :], wout_ref[...], 1, 0).astype(bf16)
+        first, second = term[0:half], term[half : 2 * half]
+        keep_ref[z] = jnp.where(core == 0, first, second)
+        send_ref[z] = jnp.where(core == 0, second, first)
+    sends = [
+        pltpu.make_async_copy(keep_ref, keep_hbm, out_sems.at[0]),
+        pltpu.make_async_copy(send_ref, send_hbm, out_sems.at[1]),
+    ]
+    for copy in sends:
+        copy.start()
+    for copy in copies[2:]:
+        copy.wait()
     swish_t = jnp.transpose(swish_ref[...].astype(f32)).astype(bf16)
     for d in range(0, width, cols):
         for k in range(2):
@@ -251,22 +476,31 @@
         at = slice(r * BLK, (r + 1) * BLK)
         grad_ref[first + r, :, width : width + LANES] = tap_ref[0, at, :].astype(bf16)
         grad_ref[first + r, :, width + LANES : width + part] = tap_ref[1, at, 0:rest].astype(bf16)
-
-
-def row_kernel(scalars, dn_ref, x_ref, stats_ref, totals_ref, gain_ref, delta_ref, out_ref, held):
+    last = pltpu.make_async_copy(grad_ref, grad_hbm, out_sems.at[2])
+    last.start()
+    for copy in sends:
+        copy.wait()
+    last.wait()
+
+
+def row_kernel(scalars, dn0, dn1, dn2, dn3, x_ref, stats_ref, gain_ref, delta_ref, out_ref, held):
     start, blocks = scalars[0], scalars[1]
-    part, slots = dn_ref.shape
+    terms = (dn0, dn1, dn2, dn3)
+    slots, part = x_ref.shape
     width = scalars[2].astype(f32)
     rest = part - LANES
     count = slots // BLK
     live = blocks * BLK
-    side = jnp.concatenate([stats_ref[0:2, :], totals_ref[...], jnp.zeros((4, slots), f32)], axis=0)
+    totals = sum(term[part : part + SIDE, :].astype(f32) for term in terms)
+    unit, cross = totals[0:1] + totals[1:2], totals[2:3] + totals[3:4]
+    row = lax.broadcasted_iota(jnp.int32, (BLK, slots), 0)
+    side = jnp.where(row == 2, unit, jnp.where(row == 3, cross, stats_ref[...]))
     side = jnp.transpose(side)
     center, row_scale = side[:, 0:1], side[:, 1:2]
     unit, cross = side[:, 2:3] / width, side[:, 3:4] / width
     sums = []
     for h, (c, e) in enumerate(((0, LANES), (LANES, part))):
-        dn = jnp.transpose(dn_ref[c:e, :].astype(f32))
+        dn = jnp.transpose(sum(term[c:e, :].astype(f32) for term in terms))
         standard = (x_ref[:, c:e].astype(f32) - center) * row_scale
         sums.append((jnp.sum(dn * standard, axis=0, keepdims=True), jnp.sum(dn, axis=0, keepdims=True)))
         on = lax.broadcasted_iota(jnp.int32, (slots, e - c), 0) < live
@@ -322,12 +556,22 @@
     is_mine = jnp.arange(replicas, dtype=jnp.int32) == my_index
     my_start = jnp.sum(jnp.where(is_mine, starts, 0))
     my_blocks = jnp.sum(jnp.where(is_mine, replica_blocks, 0))
-    scalars = jnp.stack([lax.rem(my_start, replicas), my_blocks, jnp.int32(width)])
-
-    outbox = frames.reshape(load_blocks, BLK, part)[send]
+    core = lax.axis_index("core")
+    scalars = jnp.stack([lax.rem(my_start, replicas), my_blocks, jnp.int32(width), core, lax.axis_index("zl")])
+
+    sds = jax.ShapeDtypeStruct
+    outbox = full_call(
+        outbox_kernel,
+        sds((replicas, BLK, part), bf16),
+        [pltpu.VMEM((load_rows, part), f32)],
+        1,
+        1000,
+        400000,
+    )(send, frames.T)
     arrived = lax.all_to_all(outbox, DP, split_axis=0, concat_axis=0, tiled=True)
 
-    sds = jax.ShapeDtypeStruct
+    both = jnp.stack([norm_gain, norm_bias], axis=1)
+    arrived, both, seg_column = lax.optimization_barrier((arrived, both, segment[:, None]))
     packed, packed_t = full_call(
         pack_kernel,
         (sds((slots, part), bf16), sds((part, slots), bf16)),
@@ -336,19 +580,21 @@
         1000,
         1000000,
     )(scalars, arrived)
-    gathered = lax.all_gather(packed_t, TENSOR, axis=0, tiled=True)
-
-    both = jnp.stack([norm_gain, norm_bias], axis=1)
-    normed, swish, dlt, back, tap, stats, totals = full_call(
+    own = lax.all_gather(packed_t, "zl", axis=0)
+    other = lax.ppermute(own, "core", SWAP)
+    chips = own.shape[0]
+
+    gathered, normed, swish, dlt, keep, send_half, tap, stats = full_call(
         main_kernel,
         (
             sds((width, slots), bf16),
+            sds((width, slots), bf16),
             sds((slots, part), bf16),
             sds((2, part, slots), bf16),
-            sds((width, slots), bf16),
+            sds((chips, part + SIDE, slots), bf16),
+            sds((chips, part + SIDE, slots), bf16),
             sds((2, taps, LANES), f32),
             sds((BLK, slots), f32),
-            sds((2, slots), f32),
         ),
         [
             pltpu.VMEM((2, slots + 2 * EDGE, LANES), f32),
@@ -361,39 +607,86 @@
             pltpu.VMEM((part, slots), f32),
             pltpu.VMEM((part, slots), f32),
             pltpu.VMEM((2, taps, BLK, LANES), f32),
+            pltpu.VMEM(own.shape, bf16),
+            pltpu.VMEM(other.shape, bf16),
+            pltpu.VMEM(input_weight.shape, bf16),
+            pltpu.VMEM(delta.shape, bf16),
+            pltpu.VMEM(output_weight.shape, bf16),
+            pltpu.VMEM((width, slots), bf16),
+            pltpu.VMEM((width, slots), bf16),
+            pltpu.VMEM((slots, part), bf16),
+            pltpu.VMEM((2, part, slots), bf16),
+            pltpu.VMEM((chips, part + SIDE, slots), bf16),
+            pltpu.VMEM((chips, part + SIDE, slots), bf16),
+            pltpu.SemaphoreType.DMA((5,)),
+            pltpu.SemaphoreType.DMA((6,)),
         ],
         1,
         2000000000,
         10000000,
+        (1, 2, 4, 9, 10),
+        (0, 1, 2, 3, 4, 5),
+        60,
     )(
         scalars,
-        gathered,
+        own,
+        other,
         both,
         input_weight,
         depth_weight,
         batch_scale[None],
         batch_shift[None],
-        segment[:, None],
+        seg_column,
         delta,
         output_weight,
     )
-    delta_normed = lax.psum_scatter(back, TENSOR, scatter_dimension=0, tiled=True)
-    totals = lax.psum(totals, TENSOR)
+    got = lax.ppermute(send_half, "core", SWAP)
+    paired = full_call(
+        pair_kernel, (sds(keep.shape[1:], bf16),) * chips, [], 1, 1000000, 2400000
+    )(scalars, keep, got)
+    terms = [paired[0]] + [
+        lax.ppermute(paired[j], "zl", [(z, z ^ j) for z in range(chips)]) for j in range(1, chips)
+    ]
 
     pieces = replicas
-    mixed, grads = full_call(
+    mixed_keep, mixed_send, grads = full_call(
         weight_kernel,
-        (sds((slots, width), bf16), sds((pieces, BLK, width + 2 * LANES), bf16)),
-        [],
-        0,
+        (
+            sds((chips, rows_part, width), bf16),
+            sds((chips, rows_part, width), bf16),
+            sds((pieces, BLK, width + 2 * LANES), bf16),
+        ),
+        [
+            pltpu.VMEM(swish.shape, bf16),
+            pltpu.VMEM(output_weight.shape, bf16),
+            pltpu.VMEM(dlt.shape, bf16),
+            pltpu.VMEM(normed.shape, bf16),
+            pltpu.VMEM(delta.shape, bf16),
+            pltpu.VMEM((chips, rows_part, width), bf16),
+            pltpu.VMEM((chips, rows_part, width), bf16),
+            pltpu.VMEM((pieces, BLK, width + 2 * LANES), bf16),
+            pltpu.SemaphoreType.DMA((5,)),
+            pltpu.SemaphoreType.DMA((3,)),
+        ],
+        1,
         1500000000,
         8000000,
-    )(normed, swish, dlt, delta, output_weight, tap)
-    mixed_sum = lax.psum_scatter(mixed, TENSOR, scatter_dimension=0, tiled=True)
-
-    grads = lax.all_to_all(grads, DP, split_axis=0, concat_axis=0, tiled=True)
-    mine = jnp.sum(grads.astype(f32), axis=0).astype(bf16)
-    spread = jnp.broadcast_to(mine[None], (pieces,) + mine.shape)
+        (1, 2, 3, 4, 5),
+        (0, 1, 2),
+        60,
+    )(scalars, swish, output_weight, dlt, normed, delta, tap)
+    lines, peers = lax.axis_size("x"), lax.axis_size(("zh", "y"))
+    grads, _ = lax.optimization_barrier((grads, paired[0]))
+    grads = grads.reshape((lines, peers) + grads.shape[1:])
+    grads = lax.all_to_all(grads, "x", split_axis=0, concat_axis=0, tiled=True)
+    grads, *terms = lax.optimization_barrier((grads, *terms))
+    grads = full_call(sum_kernel, sds(grads.shape[1:], bf16), [], 0, 1000000, 2300000)(grads)
+    grads = lax.all_to_all(grads, ("zh", "y"), split_axis=0, concat_axis=0, tiled=True)
+
+    mixed = mixed_keep.astype(f32) + lax.ppermute(mixed_send, "core", SWAP).astype(f32)
+    mixed = mixed.astype(bf16).reshape(chips * rows_part, width)
+    mixed, *terms = lax.optimization_barrier((mixed, *terms))
+    mixed_sum = lax.psum_scatter(mixed, "zl", scatter_dimension=0, tiled=True)
 
     column_start = tensor_index * part
     gain_part = lax.dynamic_slice_in_dim(norm_gain, column_start, part)[None]
@@ -405,19 +698,34 @@
         1,
         1000000,
         1000000,
-    )(scalars, delta_normed, packed, stats, totals, gain_part, delta_part)
-    returned = lax.all_to_all(homebound, DP, split_axis=0, concat_axis=0, tiled=True)
-    frame_gradient = returned[target][:, :, :part].reshape(load_rows, part)
-    side = jnp.sum(returned[:, 0:6, part:].astype(f32), axis=0).reshape(2, part)
-
-    whole = lax.all_to_all(spread, DP, split_axis=0, concat_axis=0, tiled=True)
-    per = part // BLK
-    weight_grad = whole[: 2 * per, :, :width].reshape(2, part, width)
-    over = whole[: 2 * per, :, width:].reshape(BLK, 6, BLK, 2 * LANES)
-    over = over.transpose(0, 2, 1, 3).reshape(BLK * BLK, width)
-    out_grad = jnp.concatenate([whole[2 * per :, :, :width].reshape(-1, width), over], axis=0)
-    tap_grad = whole[2 * per : 2 * per + taps // BLK, :, width : width + part]
-    tap_grad = tap_grad.reshape(taps, part).astype(f32)
+    )(scalars, *terms, packed, stats, gain_part, delta_part)
+    wide = grads.shape[-1]
+    shared = full_call(
+        share_kernel, sds((peers, BLK, wide + lines * 2 * LANES), bf16), [], 0, 1000000, 1500000
+    )(grads, homebound.reshape(peers, lines, BLK, 2 * LANES))
+    shared = lax.all_to_all(shared, ("zh", "y"), split_axis=0, concat_axis=0, tiled=True)
+    fanned = full_call(
+        fan_kernel, sds((lines, peers, BLK, wide + 2 * LANES), bf16), [], 0, 1000000, 3000000
+    )(shared)
+    whole = lax.all_to_all(fanned, "x", split_axis=0, concat_axis=0, tiled=True)
+    whole = whole.reshape((pieces,) + whole.shape[2:])
+    target = lax.rem(target, lines) * peers + target // lines
+    weight_grad, out_grad, tap_grad, side, frame_gradient = full_call(
+        unpack_kernel,
+        (
+            sds((2 * part, width), bf16),
+            sds((part, width), bf16),
+            sds((taps, part), f32),
+            sds((2, part), f32),
+            sds((part, load_rows), bf16),
+        ),
+        [pltpu.VMEM((pieces, BLK, 2 * LANES), f32), pltpu.VMEM((load_rows, 2 * LANES), f32)],
+        1,
+        1000000,
+        5000000,
+    )(target, whole)
+    weight_grad = weight_grad.reshape(2, part, width)
+    frame_gradient = frame_gradient.T
 
     row_start = tensor_index * rows_part
     live_mine = (row_start + jnp.arange(rows_part, dtype=jnp.int32) < my_blocks * BLK)[:, None]

time: 302 us -> 228 us (0.75)
  the two profiles are of different devices: /device:TPU:38 before, /device:TPU:72 now
where the time goes in v2:
time: 228 us; the launch traced here: 226 us
  waiting for transfers between devices  84.9 us (37%)
  starting transfers between devices  57.9 us (25%)
  Pallas kernels  30.8 us (14%)
  blocking collectives  18.3 us (8%)
  between operations  16.9 us (7%)
  local copies, waits for them, and re-layouts  12.6 us (6%)
  other arithmetic  5.13 us (2%)
    pallas_call x10, Pallas kernels, call(): pl.pallas_call(kernel, out_shape=out_shape, in_specs=specs, out_specs=out...  30.8 us
    all_to_all x1, waiting for transfers between devices, on_device(): lax.all_to_all(shared, ('zh', 'y'), split_axis=0, concat_axis=0, tiled=True)  21.5 us
    all_gather x1, blocking collectives, on_device(): own = lax.all_gather(packed_t, 'zl', axis=0)  18.3 us
    all_to_all x1, starting transfers between devices, on_device(): lax.all_to_all(outbox, DP, split_axis=0, concat_axis=0, tiled=True)  18.1 us
    ppermute x3, waiting for transfers between devices, on_device(): lax.ppermute(paired[j], 'zl', [(z, z ^ j) for z in range(chips)])  17.3 us
    all_to_all x1, waiting for transfers between devices, on_device(): whole = lax.all_to_all(fanned, 'x', split_axis=0, concat_axis=0, tiled=True)  14.6 us
    all_to_all x1, waiting for transfers between devices, on_device(): lax.all_to_all(outbox, DP, split_axis=0, concat_axis=0, tiled=True)  12.9 us
    all_to_all x1, waiting for transfers between devices, on_device(): lax.all_to_all(grads, ('zh', 'y'), split_axis=0, concat_axis=0, tiled=True)  11.7 us
  transfers between devices with their start and end apart: 13, of which 9 were waited for; matrix products, arithmetic and copies ran while one was open for 6% of the time, Pallas kernels for 5%

profile of v2, /device:TPU:72, one launch (start us, length us, event | category | flops | bytes accessed | tf_op | source)
XLA Modules:
  0.0 226.4 jit_solution(3340157246169091175)
XLA Ops:
  12.5 18.1 %all-to-all-start = ((bf16[64,8,192]{2,1,0:T(8,128)(2,1)}), bf16[64,8,192]{2,1,0:T(8,128)(2,1)S(1)}, u32[]{:S(2)}, u32[]{:S(2)}) async-start(bf16[64,8,192]{2,1,0:T(8,128)(2,1)} %shard_map.162), calls=%async_computation | async-start | bytes 524288 | tf_op jit(solution)/shard_map/all_to_all | solution.py:571
  34.7 12.9 %all-to-all-done.arrived = bf16[64,8,192]{2,1,0:T(8,128)(2,1)S(1)} async-done(((bf16[64,8,192]{2,1,0:T(8,128)(2,1)}), bf16[64,8,192]{2,1,0:T(8,128)(2,1)S(1)}, u32[]{:S(2)}, u32[]{:S(2)}) %all-to-all-start) | async-done | bytes 196640 | tf_op jit(solution)/shard_map/all_to_all | solution.py:571
  48.5 18.3 %all-gather = bf16[768,512]{1,0:T(8,128)(2,1)S(1)} all-gather(bf16[192,512]{1,0:T(8,128)(2,1)S(1)} %get-tuple-element.44), channel_id=2, replica_groups=mesh['zh'=2,'y'=8,'x'=4,'zl'=4,'core'=2] {'zl'}, dimensions={0}, use_global_device_ids=true | all-gather | bytes 983040 | tf_op jit(solution)/shard_map/all_gather | solution.py:583
  66.8 1.9 collective-permute-start
  71.8 15.9 %shard_map.164 = (bf16[1536,512]{1,0:T(8,128)(2,1)}, bf16[1536,512]{1,0:T(8,128)(2,1)}, bf16[512,192]{1,0:T(8,128)(2,1)}, bf16[2,192,512]{2,1,0:T(8,128)(2,1)}, ...) custom-call(s32[5]{0:T(128)} %copy-done.4, ...), custom_call_target="tpu_custom_call" | custom-call | flops 2000000000 | bytes 10000000 | tf_op jit(solution)/shard_map/pallas_call | solution.py:41
  87.7 2.2 collective-permute-start.2
  90.0 5.9 %shard_map.165 = (bf16[4,64,1536]{2,1,0:T(8,128)(2,1)}, bf16[4,64,1536]{2,1,0:T(8,128)(2,1)}, bf16[64,8,1792]{2,1,0:T(8,128)(2,1)}) custom-call(s32[5]{0:T(128)} %copy-done.4, bf16[512,192]{1,0:T(8,128)(2,1)} %get-tuple-element.48.swish_hbm, bf16[192,1536]{1,0:T(8,128)(2,1)} %wout_hbm.3, bf16[2,192,512]{2,1,0:T(8,128)(2,1)} %get-tuple-element.49.dlt_hbm, ...), custom_call_target="tpu_custom_call" | custom-call | flops 1500000000 | bytes 8000000 | tf_op jit(solution)/shard_map/pallas_call | solution.py:41
  97.3 3.9 %all-to-all-start.1 = ((bf16[4,16,8,1792]{3,2,1,0:T(8,128)(2,1)}), bf16[4,16,8,1792]{3,2,1,0:T(8,128)(2,1)S(1)}, u32[]{:S(2)}, u32[]{:S(2)}) async-start(bf16[4,16,8,1792]{3,2,1,0:T(8,128)(2,1)} %bitcast.31), calls=%async_computation.1 | async-start | bytes 3670016 | tf_op jit(solution)/shard_map/all_to_all | solution.py:681
  101.2 1.9 collective-permute-start.1
  103.1 4.1 %collective-permute-start.3 = (bf16[208,512]{1,0:T(8,128)(2,1)}, bf16[208,512]{1,0:T(8,128)(2,1)S(1)}, u32[]{:S(2)}, u32[]{:S(2)}) collective-permute-start(bf16[208,512]{1,0:T(8,128)(2,1)} %get-tuple-element.59), channel_id=1, source_target_pairs={{0,2},{2,0},{4,6},{6,4},{1,3},{3,1},{5,7},{7,5},{8,10},{10,8},{12,... | collective-permute-start | bytes 638984 | tf_op jit(solution)/shard_map/ppermute | solution.py:648
  107.3 2.7 %collective-permute-start.4 = (bf16[208,512]{1,0:T(8,128)(2,1)S(1)}, bf16[208,512]{1,0:T(8,128)(2,1)S(1)}, u32[]{:S(2)}, u32[]{:S(2)}) collective-permute-start(bf16[208,512]{1,0:T(8,128)(2,1)S(1)} %get-tuple-element.60), channel_id=1, source_target_pairs={{0,4},{2,6},{4,0},{6,2},{1,5},{3,7},{5,1},{7,3},{8,12},{10,14},{12... | collective-permute-start | bytes 638984 | tf_op jit(solution)/shard_map/ppermute | solution.py:648
  110.0 2.6 %collective-permute-start.5 = (bf16[208,512]{1,0:T(8,128)(2,1)S(1)}, bf16[208,512]{1,0:T(8,128)(2,1)S(1)}, u32[]{:S(2)}, u32[]{:S(2)}) collective-permute-start(bf16[208,512]{1,0:T(8,128)(2,1)S(1)} %get-tuple-element.61), channel_id=1, source_target_pairs={{0,6},{2,4},{4,2},{6,0},{1,7},{3,5},{5,3},{7,1},{8,14},{10,12},{12... | collective-permute-start | bytes 638984 | tf_op jit(solution)/shard_map/ppermute | solution.py:648
  112.6 2.3 %collective-permute-done.3.dn1 = bf16[208,512]{1,0:T(8,128)(2,1)S(1)} collective-permute-done((bf16[208,512]{1,0:T(8,128)(2,1)}, bf16[208,512]{1,0:T(8,128)(2,1)S(1)}, u32[]{:S(2)}, u32[]{:S(2)}) %collective-permute-start.3) | collective-permute-done | bytes 213024 | tf_op jit(solution)/shard_map/ppermute | solution.py:648
  114.9 9.9 %collective-permute-done.4.dn2 = bf16[208,512]{1,0:T(8,128)(2,1)S(1)} collective-permute-done((bf16[208,512]{1,0:T(8,128)(2,1)S(1)}, bf16[208,512]{1,0:T(8,128)(2,1)S(1)}, u32[]{:S(2)}, u32[]{:S(2)}) %collective-permute-start.4) | collective-permute-done | bytes 213024 | tf_op jit(solution)/shard_map/ppermute | solution.py:648
  124.8 5.1 %collective-permute-done.5.dn3 = bf16[208,512]{1,0:T(8,128)(2,1)S(1)} collective-permute-done((bf16[208,512]{1,0:T(8,128)(2,1)S(1)}, bf16[208,512]{1,0:T(8,128)(2,1)S(1)}, u32[]{:S(2)}, u32[]{:S(2)}) %collective-permute-start.5) | collective-permute-done | bytes 213024 | tf_op jit(solution)/shard_map/ppermute | solution.py:648
  130.9 9.6 %all-to-all-start.2 = ((bf16[16,8,1792]{2,1,0:T(8,128)(2,1)}), bf16[16,8,1792]{2,1,0:T(8,128)(2,1)S(1)}, u32[]{:S(2)}, u32[]{:S(2)}) async-start(bf16[16,8,1792]{2,1,0:T(8,128)(2,1)} %shard_map.167), calls=%async_computation.2 | async-start | bytes 917504 | tf_op jit(solution)/shard_map/all_to_all | solution.py:684
  142.5 2.2 add_convert_fusion
  146.0 11.7 %all-to-all-done.2.in_ref = bf16[16,8,1792]{2,1,0:T(8,128)(2,1)S(1)} async-done(((bf16[16,8,1792]{2,1,0:T(8,128)(2,1)}), bf16[16,8,1792]{2,1,0:T(8,128)(2,1)S(1)}, u32[]{:S(2)}, u32[]{:S(2)}) %all-to-all-start.2) | async-done | bytes 458784 | tf_op jit(solution)/shard_map/all_to_all | solution.py:684
  158.6 5.3 %all-to-all-start.3 = ((bf16[16,8,2816]{2,1,0:T(8,128)(2,1)}), bf16[16,8,2816]{2,1,0:T(8,128)(2,1)S(1)}, u32[]{:S(2)}, u32[]{:S(2)}) async-start(bf16[16,8,2816]{2,1,0:T(8,128)(2,1)} %shard_map.169), calls=%async_computation.3 | async-start | bytes 1441792 | tf_op jit(solution)/shard_map/all_to_all | solution.py:706
  164.7 21.5 %all-to-all-done.3.in_ref = bf16[16,8,2816]{2,1,0:T(8,128)(2,1)S(1)} async-done(((bf16[16,8,2816]{2,1,0:T(8,128)(2,1)}), bf16[16,8,2816]{2,1,0:T(8,128)(2,1)S(1)}, u32[]{:S(2)}, u32[]{:S(2)}) %all-to-all-start.3) | async-done | bytes 720928 | tf_op jit(solution)/shard_map/all_to_all | solution.py:706
  187.7 5.4 %all-to-all-start.4 = ((bf16[4,16,8,2048]{3,2,1,0:T(8,128)(2,1)}), bf16[4,16,8,2048]{3,2,1,0:T(8,128)(2,1)S(1)}, u32[]{:S(2)}, u32[]{:S(2)}) async-start(bf16[4,16,8,2048]{3,2,1,0:T(8,128)(2,1)} %copy-done), calls=%async_computation.4 | async-start | bytes 4194304 | tf_op jit(solution)/shard_map/all_to_all | solution.py:710
  193.9 5.3 %reduce-scatter.4.cloned.1.call-done = bf16[64,1536]{1,0:T(8,128)(2,1)} async-done(((bf16[256,1536]{1,0:T(8,128)(2,1)}), bf16[64,1536]{1,0:T(8,128)(2,1)}) %reduce-scatter.4.cloned.1.call-update) | async-done | bytes 196624
  202.5 14.6 %all-to-all-done.4 = bf16[4,16,8,2048]{3,2,1,0:T(8,128)(2,1)S(1)} async-done(((bf16[4,16,8,2048]{3,2,1,0:T(8,128)(2,1)}), bf16[4,16,8,2048]{3,2,1,0:T(8,128)(2,1)S(1)}, u32[]{:S(2)}, u32[]{:S(2)}) %all-to-all-start.4) | async-done | bytes 2097184 | tf_op jit(solution)/shard_map/all_to_all | solution.py:710
  217.0 2.0 shard_map.171
  (56 shorter events, 24.1 us)
Async XLA Ops:
  7.2 63.8 %all-gather.3.cloned.1.call-start = ((), (), s32[]{:S(2)}) async-start(), calls=%async_computation.6 | async-start | bytes 1769472 | tf_op jit(solution)/shard_map/all_gather | solution.py:549
  8.7 61.3 %copy-start.8 = (s32[512]{0:T(512)S(1)}, s32[512]{0:T(512)}, u32[]{:S(2)}) copy-start(s32[512]{0:T(512)} %param.21) | copy-start | bytes 6148
  10.2 0.9 copy-start.2
  12.5 35.2 %all-to-all-start = ((bf16[64,8,192]{2,1,0:T(8,128)(2,1)}), bf16[64,8,192]{2,1,0:T(8,128)(2,1)S(1)}, u32[]{:S(2)}, u32[]{:S(2)}) async-start(bf16[64,8,192]{2,1,0:T(8,128)(2,1)} %shard_map.162), calls=%async_computation | async-start | bytes 524288 | tf_op jit(solution)/shard_map/all_to_all | solution.py:571
  34.7 36.3 %copy-start.4 = (s32[5]{0:T(128)}, s32[5]{0:T(128)S(1)}, u32[]{:S(2)}) copy-start(s32[5]{0:T(128)S(1)} %stack.28.scalars) | copy-start | bytes 64
  66.8 4.2 %copy-start.7 = (bf16[768,512]{1,0:T(8,128)(2,1)}, bf16[768,512]{1,0:T(8,128)(2,1)S(1)}, u32[]{:S(2)}) copy-start(bf16[768,512]{1,0:T(8,128)(2,1)S(1)} %all-gather) | copy-start | bytes 2359300
  66.8 4.2 %collective-permute-start = (bf16[4,192,512]{2,1,0:T(8,128)(2,1)S(1)}, bf16[4,192,512]{2,1,0:T(8,128)(2,1)S(1)}, u32[]{:S(2)}, u32[]{:S(2)}) collective-permute-start(bf16[4,192,512]{2,1,0:T(8,128)(2,1)S(1)} %bitcast.32), channel_id=1, source_target_pairs={{0,1},{1,0},{2,3},{3,2},{4,5},{5,4},{6,7},{7,6},{8,9},{9,8},{10,11... | collective-permute-start | bytes 2359304 | tf_op jit(solution)/shard_map/ppermute | solution.py:584
  70.9 0.9 copy-start.9
  87.7 8.2 %collective-permute-start.2 = (bf16[4,208,512]{2,1,0:T(8,128)(2,1)}, bf16[4,208,512]{2,1,0:T(8,128)(2,1)S(1)}, u32[]{:S(2)}, u32[]{:S(2)}) collective-permute-start(bf16[4,208,512]{2,1,0:T(8,128)(2,1)} %get-tuple-element.56), channel_id=1, source_target_pairs={{0,1},{1,0},{2,3},{3,2},{4,5},{5,4},{6,7},{7,6},{8,9},{9,8},{10,11... | collective-permute-start | bytes 2555912 | tf_op jit(solution)/shard_map/ppermute | solution.py:643
  90.0 6.0 %copy-start.1 = (bf16[4,208,512]{2,1,0:T(8,128)(2,1)S(1)}, bf16[4,208,512]{2,1,0:T(8,128)(2,1)}, u32[]{:S(2)}) copy-start(bf16[4,208,512]{2,1,0:T(8,128)(2,1)} %get-tuple-element.55.keep_ref) | copy-start | bytes 2555908
  90.0 6.0 %copy-start.5 = (s32[5]{0:T(128)S(1)}, s32[5]{0:T(128)}, u32[]{:S(2)}) copy-start(s32[5]{0:T(128)} %copy-done.4) | copy-start | bytes 64
  97.3 32.5 %all-to-all-start.1 = ((bf16[4,16,8,1792]{3,2,1,0:T(8,128)(2,1)}), bf16[4,16,8,1792]{3,2,1,0:T(8,128)(2,1)S(1)}, u32[]{:S(2)}, u32[]{:S(2)}) async-start(bf16[4,16,8,1792]{3,2,1,0:T(8,128)(2,1)} %bitcast.31), calls=%async_computation.1 | async-start | bytes 3670016 | tf_op jit(solution)/shard_map/all_to_all | solution.py:681
  101.2 41.2 %collective-permute-start.1 = (bf16[4,64,1536]{2,1,0:T(8,128)(2,1)}, bf16[4,64,1536]{2,1,0:T(8,128)(2,1)}, u32[]{:S(2)}, u32[]{:S(2)}) collective-permute-start(bf16[4,64,1536]{2,1,0:T(8,128)(2,1)} %get-tuple-element.53), channel_id=1, source_target_pairs={{0,1},{1,0},{2,3},{3,2},{4,5},{5,4},{6,7},{7,6},{8,9},{9,8},{10,11... | collective-permute-start | bytes 2359304 | tf_op jit(solution)/shard_map/ppermute | solution.py:686
  103.1 11.7 %collective-permute-start.3 = (bf16[208,512]{1,0:T(8,128)(2,1)}, bf16[208,512]{1,0:T(8,128)(2,1)S(1)}, u32[]{:S(2)}, u32[]{:S(2)}) collective-permute-start(bf16[208,512]{1,0:T(8,128)(2,1)} %get-tuple-element.59), channel_id=1, source_target_pairs={{0,2},{2,0},{4,6},{6,4},{1,3},{3,1},{5,7},{7,5},{8,10},{10,8},{12,... | collective-permute-start | bytes 638984 | tf_op jit(solution)/shard_map/ppermute | solution.py:648
  107.3 17.5 %collective-permute-start.4 = (bf16[208,512]{1,0:T(8,128)(2,1)S(1)}, bf16[208,512]{1,0:T(8,128)(2,1)S(1)}, u32[]{:S(2)}, u32[]{:S(2)}) collective-permute-start(bf16[208,512]{1,0:T(8,128)(2,1)S(1)} %get-tuple-element.60), channel_id=1, source_target_pairs={{0,4},{2,6},{4,0},{6,2},{1,5},{3,7},{5,1},{7,3},{8,12},{10,14},{12... | collective-permute-start | bytes 638984 | tf_op jit(solution)/shard_map/ppermute | solution.py:648
  110.0 19.8 %collective-permute-start.5 = (bf16[208,512]{1,0:T(8,128)(2,1)S(1)}, bf16[208,512]{1,0:T(8,128)(2,1)S(1)}, u32[]{:S(2)}, u32[]{:S(2)}) collective-permute-start(bf16[208,512]{1,0:T(8,128)(2,1)S(1)} %get-tuple-element.61), channel_id=1, source_target_pairs={{0,6},{2,4},{4,2},{6,0},{1,7},{3,5},{5,3},{7,1},{8,14},{10,12},{12... | collective-permute-start | bytes 638984 | tf_op jit(solution)/shard_map/ppermute | solution.py:648
  130.9 11.6 %copy-start.6 = (bf16[4,64,1536]{2,1,0:T(8,128)(2,1)S(1)}, bf16[4,64,1536]{2,1,0:T(8,128)(2,1)}, u32[]{:S(2)}) copy-start(bf16[4,64,1536]{2,1,0:T(8,128)(2,1)} %get-tuple-element.52) | copy-start | bytes 2359300
  130.9 26.8 %all-to-all-start.2 = ((bf16[16,8,1792]{2,1,0:T(8,128)(2,1)}), bf16[16,8,1792]{2,1,0:T(8,128)(2,1)S(1)}, u32[]{:S(2)}, u32[]{:S(2)}) async-start(bf16[16,8,1792]{2,1,0:T(8,128)(2,1)} %shard_map.167), calls=%async_computation.2 | async-start | bytes 917504 | tf_op jit(solution)/shard_map/all_to_all | solution.py:684
  140.5 4.2 %copy-start.3 = (f32[8,512]{1,0:T(8,128)S(1)}, f32[8,512]{1,0:T(8,128)}, u32[]{:S(2)}) copy-start(f32[8,512]{1,0:T(8,128)} %get-tuple-element.73.stats_ref) | copy-start | bytes 49156
  158.6 27.6 %all-to-all-start.3 = ((bf16[16,8,2816]{2,1,0:T(8,128)(2,1)}), bf16[16,8,2816]{2,1,0:T(8,128)(2,1)S(1)}, u32[]{:S(2)}, u32[]{:S(2)}) async-start(bf16[16,8,2816]{2,1,0:T(8,128)(2,1)} %shard_map.169), calls=%async_computation.3 | async-start | bytes 1441792 | tf_op jit(solution)/shard_map/all_to_all | solution.py:706
  163.9 35.3 %reduce-scatter.4.cloned.1.call-start = ((), (), s32[]{:S(2)}) async-start(), calls=%async_computation.7 | async-start | bytes 983040
  186.3 1.3 copy-start
  187.7 29.4 %all-to-all-start.4 = ((bf16[4,16,8,2048]{3,2,1,0:T(8,128)(2,1)}), bf16[4,16,8,2048]{3,2,1,0:T(8,128)(2,1)S(1)}, u32[]{:S(2)}, u32[]{:S(2)}) async-start(bf16[4,16,8,2048]{3,2,1,0:T(8,128)(2,1)} %copy-done), calls=%async_computation.4 | async-start | bytes 4194304 | tf_op jit(solution)/shard_map/all_to_all | solution.py:710
Sparse Core Ops, SparseCore 0:
  10.1 45.8 all-gather.2
  168.2 31.0 reduce-scatter.3

commit v3 on v2

--- a/solution.py
+++ b/solution.py
@@ -51,14 +51,21 @@
     return call
 
 
-def outbox_kernel(send, frames_t, out_ref, held):
-    part = frames_t.shape[0]
+def outbox_kernel(replica_blocks, place, frames_hbm, out_ref, held, frames_t, sem):
+    copy = pltpu.make_async_copy(frames_hbm, frames_t, sem)
+    copy.start()
+    part, rows = frames_t.shape
+    count = out_ref.shape[0]
+    copy.wait()
     for c in range(0, part, LANES):
         e = min(part, c + LANES)
         held[:, c:e] = jnp.transpose(frames_t[c:e, :].astype(f32))
-    for r in range(out_ref.shape[0]):
-        at = pl.ds(pl.multiple_of(send[r] * BLK, BLK), BLK)
+    start = jnp.int32(0)
+    for r in range(count):
+        block = jnp.minimum(lax.div(start - place[0] + (count - 1), count), rows // BLK - 1)
+        at = pl.ds(pl.multiple_of(block * BLK, BLK), BLK)
         out_ref[r] = held[at, :].astype(bf16)
+        start = start + replica_blocks[r]
 
 
 def pack_kernel(scalars, arrived, rows_out, cols_out, held):
@@ -88,7 +95,8 @@
     scalars,
     own_hbm,
     other_hbm,
-    gb_ref,
+    gain_ref,
+    bias_ref,
     win_hbm,
     taps_ref,
     scale_ref,
@@ -97,13 +105,16 @@
     delta_hbm,
     wout_hbm,
     x_hbm,
-    normed_hbm,
-    swish_hbm,
-    dlt_hbm,
     keep_hbm,
     send_hbm,
-    tap_ref,
+    mixed_keep_hbm,
+    mixed_send_hbm,
+    grad_hbm,
     stats_ref,
+    gb_ref,
+    dsw_s,
+    mixed_s,
+    grad_ref,
     glu_s,
     dc_s,
     seg_s,
@@ -167,8 +178,11 @@
     bn_s[1, 0:1, 0:rest] = scale_ref[:, LANES:part]
     bn_s[0, 1:2, :] = shift_ref[:, 0:LANES]
     bn_s[1, 1:2, 0:rest] = shift_ref[:, LANES:part]
-    seg_s[...] = jnp.full(seg_s.shape, -1, jnp.int32)
-    seg_s[EDGE : EDGE + slots, :] = jnp.broadcast_to(seg_ref[...], (slots, LANES))
+    row = lax.broadcasted_iota(jnp.int32, (BLK, width), 0)
+    gb_ref[...] = jnp.transpose(jnp.where(row == 0, gain_ref[...], bias_ref[...]))
+    segments = jnp.broadcast_to(seg_ref[...].astype(f32), (BLK, slots))
+    seg_s[...] = jnp.full(seg_s.shape, -1.0, f32)
+    seg_s[EDGE : EDGE + slots, :] = jnp.broadcast_to(jnp.transpose(segments)[:, 0:1], (slots, LANES))
 
     glu_s[...] = jnp.zeros_like(glu_s)
     dc_s[...] = jnp.zeros_like(dc_s)
@@ -212,7 +226,6 @@
 
     lax.fori_loop(0, steps, norm_body, 0, unroll=2)
 
-    send(1, normed_ref, normed_hbm)
 
     copies[2].wait()
     normed = normed_ref[...]
@@ -227,9 +240,12 @@
 
     rows = 64
     blocks = slots // rows
+    copies[3].wait()
+    copies[4].wait()
 
     def conv_body(i, carry):
         base = pl.multiple_of(i * rows, rows)
+        dsw_s[pl.ds(base, rows), :] = dot_general(delta_ref[pl.ds(base, rows), :], wout_ref[...], 1, 1)
         here = seg_s[pl.ds(base + EDGE, rows), :]
         acc = [jnp.zeros((rows, LANES), f32) for _ in range(2)]
         for j in range(taps):
@@ -243,9 +259,7 @@
 
     lax.fori_loop(0, blocks, conv_body, 0)
 
-    copies[3].wait()
-    copies[4].wait()
-    delta_swish = dot_general(delta_ref[...], wout_ref[...], 1, 1)
+    delta_swish = dsw_s[...]
     row_live = lax.broadcasted_iota(jnp.int32, (slots, LANES), 0) < live
     for h in range(2):
         pre = pre_s[h]
@@ -259,11 +273,13 @@
             swish_ref[:, LANES:part] = swish[:, 0:rest]
             dc_s[h, EDGE : EDGE + slots, 0:rest] = delta_swish[:, LANES:part] * slope[:, 0:rest]
 
-    send(2, swish_ref, swish_hbm)
+    swish_t = jnp.transpose(swish_ref[...].astype(f32)).astype(bf16)
 
 
     def back_body(i, carry):
         base = pl.multiple_of(i * rows, rows)
+        mixed = dot_general(swish_ref[pl.ds(base, rows), :], wout_ref[...], 1, 0)
+        mixed_s[lax.rem(i, 2) ^ core, i // 2] = mixed.astype(bf16)
         here = seg_s[pl.ds(base + EDGE, rows), :]
         alive = (base + lax.broadcasted_iota(jnp.int32, (rows, LANES), 0)) < live
         glu_here = [glu_s[h, pl.ds(base + EDGE, rows), :] for h in range(2)]
@@ -280,8 +296,33 @@
         return carry
 
     lax.fori_loop(0, blocks, back_body, 0)
-    for h in range(2):
-        tap_ref[h] = jnp.sum(tap_s[h], axis=1)
+    send(1, mixed_s.at[0], mixed_keep_hbm)
+    send(2, mixed_s.at[1], mixed_send_hbm)
+
+    per = part // BLK
+    parts = grad_ref.shape[0]
+    extra = grad_ref.shape[2] - width
+    left = parts - 2 * per
+    cols = 512
+    for d in range(0, width, cols):
+        block = dot_general(swish_t, delta_ref[:, d : d + cols], 1, 0).astype(bf16)
+        grad_ref[2 * per : parts, :, d : d + cols] = block[0 : left * BLK].reshape(left, BLK, cols)
+        over = block[left * BLK :].reshape(per - left, BLK, cols)
+        for r in range(per - left):
+            for c in range(0, cols, extra):
+                at = r * (width // extra) + (d + c) // extra
+                grad_ref[at, :, width : width + extra] = over[r, :, c : c + extra]
+    first = (per - left) * (width // extra)
+    grad_ref[first:parts, :, width : width + extra] = jnp.zeros((parts - first, BLK, extra), bf16)
+    for h, (c, e) in enumerate(((0, LANES), (LANES, part))):
+        tap = jnp.sum(tap_s[h], axis=1)[:, 0 : e - c].astype(bf16)
+        for r in range(taps // BLK):
+            grad_ref[first + r, :, width + c : width + e] = tap[r * BLK : (r + 1) * BLK]
+
+    def depart(k, begin, end):
+        send(k, grad_ref.at[begin:end], grad_hbm.at[begin:end])
+
+    depart(3, 2 * per, parts)
 
     for h, (c, e) in enumerate(((0, LANES), (LANES, part))):
         dglu = jnp.transpose(dglu_s[h])[0 : e - c]
@@ -289,7 +330,6 @@
         dlt_ref[0, c:e, :] = (dglu * s).astype(bf16)
         dlt_ref[1, c:e, :] = (dglu * lin_s[c:e, :] * s * (1.0 - s)).astype(bf16)
 
-    send(3, dlt_ref, dlt_hbm)
 
     unit = jnp.zeros((BLK, slots), f32)
     cross = jnp.zeros((BLK, slots), f32)
@@ -300,8 +340,10 @@
         term = term + dot_general(win_ref[1, :, d : d + wide], dlt_ref[1], 0, 0)
         term = term.astype(bf16)
         first, second = term[0:part], term[part:wide]
+        send_ref[z, 0:part, :] = jnp.where(core == 0, second, first)
+        send(6 + z, send_ref.at[z, 0:part], send_hbm.at[z, 0:part])
         keep_ref[z, 0:part, :] = jnp.where(core == 0, first, second)
-        send_ref[z, 0:part, :] = jnp.where(core == 0, second, first)
+        send(6 + chips + z, keep_ref.at[z, 0:part], keep_hbm.at[z, 0:part])
         weighted = term.astype(f32) * gb_ref[d : d + wide, 0:1]
         standard = (x_ref[d : d + wide, :].astype(f32) - center) * row_scale
         unit = unit + jnp.sum(weighted.reshape(wide // BLK, BLK, slots), axis=0)
@@ -311,10 +353,16 @@
     )
     for z in range(chips):
         send_ref[z, part : part + SIDE, :] = totals
-    send(4, send_ref, send_hbm)
-    for z in range(chips):
         keep_ref[z, part : part + SIDE, :] = totals
-    send(5, keep_ref, keep_hbm)
+    below = pl.ds(part, SIDE)
+    send(6 + 2 * chips, send_ref.at[:, below], send_hbm.at[:, below])
+    send(7 + 2 * chips, keep_ref.at[:, below], keep_hbm.at[:, below])
+
+    for k in range(2):
+        for d in range(0, width, cols):
+            block = dot_general(dlt_ref[k], normed_ref[d : d + cols, :], 1, 1).astype(bf16)
+            grad_ref[k * per : (k + 1) * per, :, d : d + cols] = block.reshape(per, BLK, cols)
+        depart(4 + k, k * per, (k + 1) * per)
     for copy in sends:
         copy.wait()
 
@@ -395,92 +443,6 @@
             at = wide + k * 2 * LANES
             out_ref[k, i, :, 0:wide] = piece
             out_ref[k, i, :, wide:full] = in_ref[i, :, at : at + 2 * LANES]
-
-
-def weight_kernel(
-    scalars,
-    swish_hbm,
-    wout_hbm,
-    dlt_hbm,
-    normed_hbm,
-    delta_hbm,
-    tap_ref,
-    keep_hbm,
-    send_hbm,
-    grad_hbm,
-    swish_ref,
-    wout_ref,
-    dlt_ref,
-    normed_ref,
-    delta_ref,
-    keep_ref,
-    send_ref,
-    grad_ref,
-    sems,
-    out_sems,
-):
-    inward = (
-        (swish_hbm, swish_ref),
-        (wout_hbm, wout_ref),
-        (dlt_hbm, dlt_ref),
-        (normed_hbm, normed_ref),
-        (delta_hbm, delta_ref),
-    )
-    copies = [
-        pltpu.make_async_copy(source, target, sems.at[k]) for k, (source, target) in enumerate(inward)
-    ]
-    for copy in copies:
-        copy.start()
-    copies[0].wait()
-    copies[1].wait()
-    width = normed_ref.shape[0]
-    part = swish_ref.shape[1]
-    taps = tap_ref.shape[1]
-    rest = part - LANES
-    pieces = grad_ref.shape[0]
-    per = part // BLK
-    extra = grad_ref.shape[2] - width
-    cols = 512
-    core = scalars[3]
-    chips, half = keep_ref.shape[0:2]
-    for z in range(chips):
-        at = slice(2 * z * half, 2 * (z + 1) * half)
-        term = dot_general(swish_ref[at, :], wout_ref[...], 1, 0).astype(bf16)
-        first, second = term[0:half], term[half : 2 * half]
-        keep_ref[z] = jnp.where(core == 0, first, second)
-        send_ref[z] = jnp.where(core == 0, second, first)
-    sends = [
-        pltpu.make_async_copy(keep_ref, keep_hbm, out_sems.at[0]),
-        pltpu.make_async_copy(send_ref, send_hbm, out_sems.at[1]),
-    ]
-    for copy in sends:
-        copy.start()
-    for copy in copies[2:]:
-        copy.wait()
-    swish_t = jnp.transpose(swish_ref[...].astype(f32)).astype(bf16)
-    for d in range(0, width, cols):
-        for k in range(2):
-            block = dot_general(dlt_ref[k], normed_ref[d : d + cols, :], 1, 1).astype(bf16)
-            grad_ref[k * per : (k + 1) * per, :, d : d + cols] = block.reshape(per, BLK, cols)
-        block = dot_general(swish_t, delta_ref[:, d : d + cols], 1, 0).astype(bf16)
-        left = pieces - 2 * per
-        grad_ref[2 * per : pieces, :, d : d + cols] = block[0 : left * BLK].reshape(left, BLK, cols)
-        over = block[left * BLK :].reshape(per - left, BLK, cols)
-        for r in range(per - left):
-            for c in range(0, cols, extra):
-                at = r * (width // extra) + (d + c) // extra
-                grad_ref[at, :, width : width + extra] = over[r, :, c : c + extra]
-    first = (per - left) * (width // extra)
-    grad_ref[first:pieces, :, width : width + extra] = jnp.zeros((pieces - first, BLK, extra), bf16)
-    for r in range(taps // BLK):
-        at = slice(r * BLK, (r + 1) * BLK)
-        grad_ref[first + r, :, width : width + LANES] = tap_ref[0, at, :].astype(bf16)
-        grad_ref[first + r, :, width + LANES : width + part] = tap_ref[1, at, 0:rest].astype(bf16)
-    last = pltpu.make_async_copy(grad_ref, grad_hbm, out_sems.at[2])
-    last.start()
-    for copy in sends:
-        copy.wait()
-    last.wait()
 
 
 def row_kernel(scalars, dn0, dn1, dn2, dn3, x_ref, stats_ref, gain_ref, delta_ref, out_ref, held):
@@ -550,7 +512,6 @@
 
     ends = jnp.cumsum(replica_blocks)
     starts = ends - replica_blocks
-    send = jnp.clip((starts - my_index + replicas - 1) // replicas, 0, load_blocks - 1)
     numbers = my_index + replicas * jnp.arange(load_blocks, dtype=jnp.int32)
     target = jnp.sum((ends[None, :] <= numbers[:, None]).astype(jnp.int32), axis=1)
     is_mine = jnp.arange(replicas, dtype=jnp.int32) == my_index
@@ -563,15 +524,18 @@
     outbox = full_call(
         outbox_kernel,
         sds((replicas, BLK, part), bf16),
-        [pltpu.VMEM((load_rows, part), f32)],
-        1,
+        [
+            pltpu.VMEM((load_rows, part), f32),
+            pltpu.VMEM((part, load_rows), bf16),
+            pltpu.SemaphoreType.DMA(()),
+        ],
+        2,
         1000,
         400000,
-    )(send, frames.T)
+        (2,),
+    )(replica_blocks, my_index[None], frames.T)
     arrived = lax.all_to_all(outbox, DP, split_axis=0, concat_axis=0, tiled=True)
 
-    both = jnp.stack([norm_gain, norm_bias], axis=1)
-    arrived, both, seg_column = lax.optimization_barrier((arrived, both, segment[:, None]))
     packed, packed_t = full_call(
         pack_kernel,
         (sds((slots, part), bf16), sds((part, slots), bf16)),
@@ -584,22 +548,27 @@
     other = lax.ppermute(own, "core", SWAP)
     chips = own.shape[0]
 
-    gathered, normed, swish, dlt, keep, send_half, tap, stats = full_call(
+    pieces = replicas
+    half = sds((chips, rows_part, width), bf16)
+    gathered, keep, send_half, mixed_keep, mixed_send, grads, stats = full_call(
         main_kernel,
         (
             sds((width, slots), bf16),
-            sds((width, slots), bf16),
-            sds((slots, part), bf16),
-            sds((2, part, slots), bf16),
             sds((chips, part + SIDE, slots), bf16),
             sds((chips, part + SIDE, slots), bf16),
-            sds((2, taps, LANES), f32),
+            half,
+            half,
+            sds((pieces, BLK, width + 2 * LANES), bf16),
             sds((BLK, slots), f32),
         ),
         [
+            pltpu.VMEM((width, BLK), f32),
+            pltpu.VMEM((slots, part), f32),
+            pltpu.VMEM((2, chips, rows_part, width), bf16),
+            pltpu.VMEM((pieces, BLK, width + 2 * LANES), bf16),
             pltpu.VMEM((2, slots + 2 * EDGE, LANES), f32),
             pltpu.VMEM((2, slots + 2 * EDGE, LANES), f32),
-            pltpu.VMEM((slots + 2 * EDGE, LANES), jnp.int32),
+            pltpu.VMEM((slots + 2 * EDGE, LANES), f32),
             pltpu.VMEM((2, taps, LANES), f32),
             pltpu.VMEM((2, BLK, LANES), f32),
             pltpu.VMEM((2, slots, LANES), f32),
@@ -619,24 +588,25 @@
             pltpu.VMEM((chips, part + SIDE, slots), bf16),
             pltpu.VMEM((chips, part + SIDE, slots), bf16),
             pltpu.SemaphoreType.DMA((5,)),
-            pltpu.SemaphoreType.DMA((6,)),
+            pltpu.SemaphoreType.DMA((8 + 2 * chips,)),
         ],
         1,
-        2000000000,
-        10000000,
-        (1, 2, 4, 9, 10),
+        3000000000,
+        12000000,
+        (1, 2, 5, 10, 11),
         (0, 1, 2, 3, 4, 5),
         60,
     )(
         scalars,
         own,
         other,
-        both,
+        norm_gain[None],
+        norm_bias[None],
         input_weight,
         depth_weight,
         batch_scale[None],
         batch_shift[None],
-        seg_column,
+        segment[None],
         delta,
         output_weight,
     )
@@ -644,48 +614,21 @@
     paired = full_call(
         pair_kernel, (sds(keep.shape[1:], bf16),) * chips, [], 1, 1000000, 2400000
     )(scalars, keep, got)
-    terms = [paired[0]] + [
-        lax.ppermute(paired[j], "zl", [(z, z ^ j) for z in range(chips)]) for j in range(1, chips)
-    ]
-
-    pieces = replicas
-    mixed_keep, mixed_send, grads = full_call(
-        weight_kernel,
-        (
-            sds((chips, rows_part, width), bf16),
-            sds((chips, rows_part, width), bf16),
-            sds((pieces, BLK, width + 2 * LANES), bf16),
-        ),
-        [
-            pltpu.VMEM(swish.shape, bf16),
-            pltpu.VMEM(output_weight.shape, bf16),
-            pltpu.VMEM(dlt.shape, bf16),
-            pltpu.VMEM(normed.shape, bf16),
-            pltpu.VMEM(delta.shape, bf16),
-            pltpu.VMEM((chips, rows_part, width), bf16),
-            pltpu.VMEM((chips, rows_part, width), bf16),
-            pltpu.VMEM((pieces, BLK, width + 2 * LANES), bf16),
-            pltpu.SemaphoreType.DMA((5,)),
-            pltpu.SemaphoreType.DMA((3,)),
-        ],
-        1,
-        1500000000,
-        8000000,
-        (1, 2, 3, 4, 5),
-        (0, 1, 2),
-        60,
-    )(scalars, swish, output_weight, dlt, normed, delta, tap)
+    terms = {0: paired[0]}
+    for j in range(chips - 1, 0, -1):
+        terms[j] = lax.ppermute(paired[j], "zl", [(z, z ^ j) for z in range(chips)])
+    terms = [terms[j] for j in range(chips)]
+
     lines, peers = lax.axis_size("x"), lax.axis_size(("zh", "y"))
-    grads, _ = lax.optimization_barrier((grads, paired[0]))
     grads = grads.reshape((lines, peers) + grads.shape[1:])
     grads = lax.all_to_all(grads, "x", split_axis=0, concat_axis=0, tiled=True)
     grads, *terms = lax.optimization_barrier((grads, *terms))
     grads = full_call(sum_kernel, sds(grads.shape[1:], bf16), [], 0, 1000000, 2300000)(grads)
     grads = lax.all_to_all(grads, ("zh", "y"), split_axis=0, concat_axis=0, tiled=True)
 
+    mixed_send, *terms = lax.optimization_barrier((mixed_send, *terms))
     mixed = mixed_keep.astype(f32) + lax.ppermute(mixed_send, "core", SWAP).astype(f32)
     mixed = mixed.astype(bf16).reshape(chips * rows_part, width)
-    mixed, *terms = lax.optimization_barrier((mixed, *terms))
     mixed_sum = lax.psum_scatter(mixed, "zl", scatter_dimension=0, tiled=True)
 
     column_start = tensor_index * part

time: 228 us -> 220 us (0.965)
  Pallas kernels: 30.8 us -> 25.8 us
  local copies, waits for them, and re-layouts: 12.6 us -> 10.3 us
    pallas_call x10 -> x9, Pallas kernels: 30.8 us -> 25.8 us  [call(): pl.pallas_call(kernel, out_shape=out_shape, in_specs=specs, out_specs=out...]
    ppermute x1, waiting for transfers between devices: 0.01 us -> 2.46 us  [on_device(): got = lax.ppermute(send_half, 'core', SWAP)]
    unnamed x22 -> x26, local copies, waits for them, and re-layouts: 5.15 us -> 5.83 us
  transfers between devices with their start and end apart: 13 -> 13, of which waited for: 9 -> 10; matrix products, arithmetic and copies ran while one was open for 6% -> 5% of each run, Pallas kernels for 5% -> 3%
where the time goes in v3:
time: 220 us; the launch traced here: 219 us
  waiting for transfers between devices  84.9 us (39%)
  starting transfers between devices  56.8 us (26%)
  Pallas kernels  25.8 us (12%)
  blocking collectives  19.1 us (9%)
  between operations  16.9 us (8%)
  local copies, waits for them, and re-layouts  10.3 us (5%)
  other arithmetic  5.11 us (2%)
    pallas_call x9, Pallas kernels, call(): pl.pallas_call(kernel, out_shape=out_shape, in_specs=specs, out_specs=out...  25.8 us
    all_to_all x1, waiting for transfers between devices, on_device(): lax.all_to_all(shared, ('zh', 'y'), split_axis=0, concat_axis=0, tiled=True)  20 us
    all_gather x1, blocking collectives, on_device(): own = lax.all_gather(packed_t, 'zl', axis=0)  19.1 us
    all_to_all x1, starting transfers between devices, on_device(): lax.all_to_all(outbox, DP, split_axis=0, concat_axis=0, tiled=True)  18.1 us
    ppermute x3, waiting for transfers between devices, on_device(): terms[j] = lax.ppermute(paired[j], 'zl', [(z, z ^ j) for z in range(chips)])  17.1 us
    all_to_all x1, waiting for transfers between devices, on_device(): whole = lax.all_to_all(fanned, 'x', split_axis=0, concat_axis=0, tiled=True)  13.3 us
    all_to_all x1, waiting for transfers between devices, on_device(): lax.all_to_all(outbox, DP, split_axis=0, concat_axis=0, tiled=True)  12.1 us
    all_to_all x1, waiting for transfers between devices, on_device(): lax.all_to_all(grads, ('zh', 'y'), split_axis=0, concat_axis=0, tiled=True)  12.1 us
  transfers between devices with their start and end apart: 13, of which 10 were waited for; matrix products, arithmetic and copies ran while one was open for 5% of the time, Pallas kernels for 3%

profile of v3, /device:TPU:72, one launch (start us, length us, event | category | flops | bytes accessed | tf_op | source)
XLA Modules:
  0.0 218.9 jit_solution(3245273449218317946)
XLA Ops:
  9.5 1.7 shard_map.162
  11.2 18.1 %all-to-all-start = ((bf16[64,8,192]{2,1,0:T(8,128)(2,1)}), bf16[64,8,192]{2,1,0:T(8,128)(2,1)S(1)}, u32[]{:S(2)}, u32[]{:S(2)}) async-start(bf16[64,8,192]{2,1,0:T(8,128)(2,1)} %shard_map.162), calls=%async_computation | async-start | bytes 524288 | tf_op jit(solution)/shard_map/all_to_all | solution.py:537
  34.2 12.1 %all-to-all-done.arrived = bf16[64,8,192]{2,1,0:T(8,128)(2,1)S(1)} async-done(((bf16[64,8,192]{2,1,0:T(8,128)(2,1)}), bf16[64,8,192]{2,1,0:T(8,128)(2,1)S(1)}, u32[]{:S(2)}, u32[]{:S(2)}) %all-to-all-start) | async-done | bytes 196640 | tf_op jit(solution)/shard_map/all_to_all | solution.py:537
  47.2 19.1 %all-gather = bf16[768,512]{1,0:T(8,128)(2,1)S(1)} all-gather(bf16[192,512]{1,0:T(8,128)(2,1)S(1)} %get-tuple-element.35), channel_id=2, replica_groups=mesh['zh'=2,'y'=8,'x'=4,'zl'=4,'core'=2] {'zl'}, dimensions={0}, use_global_device_ids=true | all-gather | bytes 983040 | tf_op jit(solution)/shard_map/all_gather | solution.py:547
  66.4 1.9 collective-permute-start
  71.5 17.1 %shard_map.164 = (bf16[1536,512]{1,0:T(8,128)(2,1)}, bf16[4,208,512]{2,1,0:T(8,128)(2,1)}, bf16[4,208,512]{2,1,0:T(8,128)(2,1)}, bf16[4,64,1536]{2,1,0:T(8,128)(...) custom-call(s32[5]{0:T(128)} %copy-done.4, bf16[4,192,512]{2,1,0:T(8,128)(2,1)} %bitcast.35, ...), custom_call_target="tpu_custom_call" | custom-call | flops 3000000000 | bytes 12000000 | tf_op jit(solution)/shard_map/pallas_call | solution.py:41
  88.6 3.8 %all-to-all-start.1 = ((bf16[4,16,8,1792]{3,2,1,0:T(8,128)(2,1)}), bf16[4,16,8,1792]{3,2,1,0:T(8,128)(2,1)S(1)}, u32[]{:S(2)}, u32[]{:S(2)}) async-start(bf16[4,16,8,1792]{3,2,1,0:T(8,128)(2,1)} %bitcast.33), calls=%async_computation.1 | async-start | bytes 3670016 | tf_op jit(solution)/shard_map/all_to_all | solution.py:624
  92.4 2.0 collective-permute-start.1
  94.4 2.5 %collective-permute-done.1.got_ref = bf16[4,208,512]{2,1,0:T(8,128)(2,1)S(1)} collective-permute-done((bf16[4,208,512]{2,1,0:T(8,128)(2,1)}, bf16[4,208,512]{2,1,0:T(8,128)(2,1)S(1)}, u32[]{:S(2)}, u32[]{:S(2)}) %collective-permute-start.1) | collective-permute-done | bytes 852000 | tf_op jit(solution)/shard_map/ppermute | solution.py:613
  97.6 4.3 %collective-permute-start.2 = (bf16[208,512]{1,0:T(8,128)(2,1)S(1)}, bf16[208,512]{1,0:T(8,128)(2,1)S(1)}, u32[]{:S(2)}, u32[]{:S(2)}) collective-permute-start(bf16[208,512]{1,0:T(8,128)(2,1)S(1)} %get-tuple-element.43), channel_id=1, source_target_pairs={{0,2},{2,0},{4,6},{6,4},{1,3},{3,1},{5,7},{7,5},{8,10},{10,8},{12,... | collective-permute-start | bytes 638984 | tf_op jit(solution)/shard_map/ppermute | solution.py:619
  101.9 2.7 %collective-permute-start.3 = (bf16[208,512]{1,0:T(8,128)(2,1)S(1)}, bf16[208,512]{1,0:T(8,128)(2,1)S(1)}, u32[]{:S(2)}, u32[]{:S(2)}) collective-permute-start(bf16[208,512]{1,0:T(8,128)(2,1)S(1)} %get-tuple-element.44), channel_id=1, source_target_pairs={{0,4},{2,6},{4,0},{6,2},{1,5},{3,7},{5,1},{7,3},{8,12},{10,14},{12... | collective-permute-start | bytes 638984 | tf_op jit(solution)/shard_map/ppermute | solution.py:619
  104.6 2.6 %collective-permute-start.4 = (bf16[208,512]{1,0:T(8,128)(2,1)S(1)}, bf16[208,512]{1,0:T(8,128)(2,1)S(1)}, u32[]{:S(2)}, u32[]{:S(2)}) collective-permute-start(bf16[208,512]{1,0:T(8,128)(2,1)S(1)} %get-tuple-element.45), channel_id=1, source_target_pairs={{0,6},{2,4},{4,2},{6,0},{1,7},{3,5},{5,3},{7,1},{8,14},{10,12},{12... | collective-permute-start | bytes 638984 | tf_op jit(solution)/shard_map/ppermute | solution.py:619
  108.7 10.7 %collective-permute-done.3.dn2 = bf16[208,512]{1,0:T(8,128)(2,1)S(1)} collective-permute-done((bf16[208,512]{1,0:T(8,128)(2,1)S(1)}, bf16[208,512]{1,0:T(8,128)(2,1)S(1)}, u32[]{:S(2)}, u32[]{:S(2)}) %collective-permute-start.3) | collective-permute-done | bytes 213024 | tf_op jit(solution)/shard_map/ppermute | solution.py:619
  119.4 4.9 %collective-permute-done.4.dn3 = bf16[208,512]{1,0:T(8,128)(2,1)S(1)} collective-permute-done((bf16[208,512]{1,0:T(8,128)(2,1)S(1)}, bf16[208,512]{1,0:T(8,128)(2,1)S(1)}, u32[]{:S(2)}, u32[]{:S(2)}) %collective-permute-start.4) | collective-permute-done | bytes 213024 | tf_op jit(solution)/shard_map/ppermute | solution.py:619
  125.3 9.4 %all-to-all-start.2 = ((bf16[16,8,1792]{2,1,0:T(8,128)(2,1)}), bf16[16,8,1792]{2,1,0:T(8,128)(2,1)S(1)}, u32[]{:S(2)}, u32[]{:S(2)}) async-start(bf16[16,8,1792]{2,1,0:T(8,128)(2,1)} %shard_map.166), calls=%async_computation.2 | async-start | bytes 917504 | tf_op jit(solution)/shard_map/all_to_all | solution.py:627
  134.7 1.9 collective-permute-start.5
  139.2 12.1 %all-to-all-done.2.in_ref = bf16[16,8,1792]{2,1,0:T(8,128)(2,1)S(1)} async-done(((bf16[16,8,1792]{2,1,0:T(8,128)(2,1)}), bf16[16,8,1792]{2,1,0:T(8,128)(2,1)S(1)}, u32[]{:S(2)}, u32[]{:S(2)}) %all-to-all-start.2) | async-done | bytes 458784 | tf_op jit(solution)/shard_map/all_to_all | solution.py:627
  152.2 5.4 %all-to-all-start.3 = ((bf16[16,8,2816]{2,1,0:T(8,128)(2,1)}), bf16[16,8,2816]{2,1,0:T(8,128)(2,1)S(1)}, u32[]{:S(2)}, u32[]{:S(2)}) async-start(bf16[16,8,2816]{2,1,0:T(8,128)(2,1)} %shard_map.168), calls=%async_computation.3 | async-start | bytes 1441792 | tf_op jit(solution)/shard_map/all_to_all | solution.py:649
  157.6 2.2 %add_convert_fusion = bf16[4,64,1536]{2,1,0:T(8,128)(2,1)} fusion(bf16[4,64,1536]{2,1,0:T(8,128)(2,1)} %collective-permute-done.5, bf16[4,64,1536]{2,1,0:T(8,128)(2,1)S(1)} %copy-done.7), kind=kLoop, calls=%fused_computation | loop fusion | flops 1572864 | bytes 2359296 | tf_op jit(solution)/shard_map/convert_element_type | solution.py:631
  159.9 20.0 %all-to-all-done.3.in_ref = bf16[16,8,2816]{2,1,0:T(8,128)(2,1)S(1)} async-done(((bf16[16,8,2816]{2,1,0:T(8,128)(2,1)}), bf16[16,8,2816]{2,1,0:T(8,128)(2,1)S(1)}, u32[]{:S(2)}, u32[]{:S(2)}) %all-to-all-start.3) | async-done | bytes 720928 | tf_op jit(solution)/shard_map/all_to_all | solution.py:649
  181.4 4.6 %all-to-all-start.4 = ((bf16[4,16,8,2048]{3,2,1,0:T(8,128)(2,1)}), bf16[4,16,8,2048]{3,2,1,0:T(8,128)(2,1)S(1)}, u32[]{:S(2)}, u32[]{:S(2)}) async-start(bf16[4,16,8,2048]{3,2,1,0:T(8,128)(2,1)} %copy-done), calls=%async_computation.4 | async-start | bytes 4194304 | tf_op jit(solution)/shard_map/all_to_all | solution.py:653
  186.9 6.1 %reduce-scatter.4.cloned.1.call-done = bf16[64,1536]{1,0:T(8,128)(2,1)} async-done(((bf16[256,1536]{1,0:T(8,128)(2,1)}), bf16[64,1536]{1,0:T(8,128)(2,1)}) %reduce-scatter.4.cloned.1.call-update) | async-done | bytes 196624
  196.2 13.3 %all-to-all-done.4 = bf16[4,16,8,2048]{3,2,1,0:T(8,128)(2,1)S(1)} async-done(((bf16[4,16,8,2048]{3,2,1,0:T(8,128)(2,1)}), bf16[4,16,8,2048]{3,2,1,0:T(8,128)(2,1)S(1)}, u32[]{:S(2)}, u32[]{:S(2)}) %all-to-all-start.4) | async-done | bytes 2097184 | tf_op jit(solution)/shard_map/all_to_all | solution.py:653
  209.5 2.0 shard_map.170
  (56 shorter events, 21.5 us)
Async XLA Ops:
  7.2 61.1 %copy-start.9 = (f32[1536]{0:T(1024)S(1)}, f32[1536]{0:T(1024)}, u32[]{:S(2)}) copy-start(f32[1536]{0:T(1024)} %param.12) | copy-start | bytes 18436
  7.2 61.7 %copy-start.10 = (f32[1536]{0:T(1024)S(1)}, f32[1536]{0:T(1024)}, u32[]{:S(2)}) copy-start(f32[1536]{0:T(1024)} %param.13) | copy-start | bytes 18436
  7.2 63.3 %all-gather.3.cloned.1.call-start = ((), (), s32[]{:S(2)}) async-start(), calls=%async_computation.6 | async-start | bytes 1769472 | tf_op jit(solution)/shard_map/all_gather | solution.py:511
  7.9 0.9 copy-start.2
  11.2 35.2 %all-to-all-start = ((bf16[64,8,192]{2,1,0:T(8,128)(2,1)}), bf16[64,8,192]{2,1,0:T(8,128)(2,1)S(1)}, u32[]{:S(2)}, u32[]{:S(2)}) async-start(bf16[64,8,192]{2,1,0:T(8,128)(2,1)} %shard_map.162), calls=%async_computation | async-start | bytes 524288 | tf_op jit(solution)/shard_map/all_to_all | solution.py:537
  34.2 36.3 %copy-start.4 = (s32[5]{0:T(128)}, s32[5]{0:T(128)S(1)}, u32[]{:S(2)}) copy-start(s32[5]{0:T(128)S(1)} %stack.19.scalars) | copy-start | bytes 64
  66.4 4.2 %copy-start.8 = (bf16[768,512]{1,0:T(8,128)(2,1)}, bf16[768,512]{1,0:T(8,128)(2,1)S(1)}, u32[]{:S(2)}) copy-start(bf16[768,512]{1,0:T(8,128)(2,1)S(1)} %all-gather) | copy-start | bytes 2359300
  66.4 4.2 %collective-permute-start = (bf16[4,192,512]{2,1,0:T(8,128)(2,1)S(1)}, bf16[4,192,512]{2,1,0:T(8,128)(2,1)S(1)}, u32[]{:S(2)}, u32[]{:S(2)}) collective-permute-start(bf16[4,192,512]{2,1,0:T(8,128)(2,1)S(1)} %bitcast.34), channel_id=1, source_target_pairs={{0,1},{1,0},{2,3},{3,2},{4,5},{5,4},{6,7},{7,6},{8,9},{9,8},{10,11... | collective-permute-start | bytes 2359304 | tf_op jit(solution)/shard_map/ppermute | solution.py:548
  70.5 0.9 copy-start.11
  88.6 8.3 %copy-start.1 = (bf16[4,208,512]{2,1,0:T(8,128)(2,1)S(1)}, bf16[4,208,512]{2,1,0:T(8,128)(2,1)}, u32[]{:S(2)}) copy-start(bf16[4,208,512]{2,1,0:T(8,128)(2,1)} %get-tuple-element.40.keep_ref) | copy-start | bytes 2555908
  88.6 8.3 %copy-start.5 = (s32[5]{0:T(128)S(1)}, s32[5]{0:T(128)}, u32[]{:S(2)}) copy-start(s32[5]{0:T(128)} %copy-done.4) | copy-start | bytes 64
  88.6 35.7 %all-to-all-start.1 = ((bf16[4,16,8,1792]{3,2,1,0:T(8,128)(2,1)}), bf16[4,16,8,1792]{3,2,1,0:T(8,128)(2,1)S(1)}, u32[]{:S(2)}, u32[]{:S(2)}) async-start(bf16[4,16,8,1792]{3,2,1,0:T(8,128)(2,1)} %bitcast.33), calls=%async_computation.1 | async-start | bytes 3670016 | tf_op jit(solution)/shard_map/all_to_all | solution.py:624
  92.4 4.5 %collective-permute-start.1 = (bf16[4,208,512]{2,1,0:T(8,128)(2,1)}, bf16[4,208,512]{2,1,0:T(8,128)(2,1)S(1)}, u32[]{:S(2)}, u32[]{:S(2)}) collective-permute-start(bf16[4,208,512]{2,1,0:T(8,128)(2,1)} %get-tuple-element.41), channel_id=1, source_target_pairs={{0,1},{1,0},{2,3},{3,2},{4,5},{5,4},{6,7},{7,6},{8,9},{9,8},{10,11... | collective-permute-start | bytes 2555912 | tf_op jit(solution)/shard_map/ppermute | solution.py:613
  97.6 11.1 %collective-permute-start.2 = (bf16[208,512]{1,0:T(8,128)(2,1)S(1)}, bf16[208,512]{1,0:T(8,128)(2,1)S(1)}, u32[]{:S(2)}, u32[]{:S(2)}) collective-permute-start(bf16[208,512]{1,0:T(8,128)(2,1)S(1)} %get-tuple-element.43), channel_id=1, source_target_pairs={{0,2},{2,0},{4,6},{6,4},{1,3},{3,1},{5,7},{7,5},{8,10},{10,8},{12,... | collective-permute-start | bytes 638984 | tf_op jit(solution)/shard_map/ppermute | solution.py:619
  101.9 17.5 %collective-permute-start.3 = (bf16[208,512]{1,0:T(8,128)(2,1)S(1)}, bf16[208,512]{1,0:T(8,128)(2,1)S(1)}, u32[]{:S(2)}, u32[]{:S(2)}) collective-permute-start(bf16[208,512]{1,0:T(8,128)(2,1)S(1)} %get-tuple-element.44), channel_id=1, source_target_pairs={{0,4},{2,6},{4,0},{6,2},{1,5},{3,7},{5,1},{7,3},{8,12},{10,14},{12... | collective-permute-start | bytes 638984 | tf_op jit(solution)/shard_map/ppermute | solution.py:619
  104.6 19.6 %collective-permute-start.4 = (bf16[208,512]{1,0:T(8,128)(2,1)S(1)}, bf16[208,512]{1,0:T(8,128)(2,1)S(1)}, u32[]{:S(2)}, u32[]{:S(2)}) collective-permute-start(bf16[208,512]{1,0:T(8,128)(2,1)S(1)} %get-tuple-element.45), channel_id=1, source_target_pairs={{0,6},{2,4},{4,2},{6,0},{1,7},{3,5},{5,3},{7,1},{8,14},{10,12},{12... | collective-permute-start | bytes 638984 | tf_op jit(solution)/shard_map/ppermute | solution.py:619
  124.3 13.5 %copy-start.3 = (f32[8,512]{1,0:T(8,128)S(1)}, f32[8,512]{1,0:T(8,128)}, u32[]{:S(2)}) copy-start(f32[8,512]{1,0:T(8,128)} %get-tuple-element.57.stats_ref) | copy-start | bytes 49156
  125.3 25.9 %all-to-all-start.2 = ((bf16[16,8,1792]{2,1,0:T(8,128)(2,1)}), bf16[16,8,1792]{2,1,0:T(8,128)(2,1)S(1)}, u32[]{:S(2)}, u32[]{:S(2)}) async-start(bf16[16,8,1792]{2,1,0:T(8,128)(2,1)} %shard_map.166), calls=%async_computation.2 | async-start | bytes 917504 | tf_op jit(solution)/shard_map/all_to_all | solution.py:627
  134.7 23.0 %collective-permute-start.5 = (bf16[4,64,1536]{2,1,0:T(8,128)(2,1)}, bf16[4,64,1536]{2,1,0:T(8,128)(2,1)}, u32[]{:S(2)}, u32[]{:S(2)}) collective-permute-start(bf16[4,64,1536]{2,1,0:T(8,128)(2,1)} %get-tuple-element.50), channel_id=1, source_target_pairs={{0,1},{1,0},{2,3},{3,2},{4,5},{5,4},{6,7},{7,6},{8,9},{9,8},{10,11... | collective-permute-start | bytes 2359304 | tf_op jit(solution)/shard_map/ppermute | solution.py:630
  139.1 18.5 %copy-start.7 = (bf16[4,64,1536]{2,1,0:T(8,128)(2,1)S(1)}, bf16[4,64,1536]{2,1,0:T(8,128)(2,1)}, u32[]{:S(2)}) copy-start(bf16[4,64,1536]{2,1,0:T(8,128)(2,1)} %get-tuple-element.37) | copy-start | bytes 2359300
  152.2 27.7 %all-to-all-start.3 = ((bf16[16,8,2816]{2,1,0:T(8,128)(2,1)}), bf16[16,8,2816]{2,1,0:T(8,128)(2,1)S(1)}, u32[]{:S(2)}, u32[]{:S(2)}) async-start(bf16[16,8,2816]{2,1,0:T(8,128)(2,1)} %shard_map.168), calls=%async_computation.3 | async-start | bytes 1441792 | tf_op jit(solution)/shard_map/all_to_all | solution.py:649
  157.6 35.4 %reduce-scatter.4.cloned.1.call-start = ((), (), s32[]{:S(2)}) async-start(), calls=%async_computation.7 | async-start | bytes 983040
  180.0 1.3 copy-start
  181.4 28.1 %all-to-all-start.4 = ((bf16[4,16,8,2048]{3,2,1,0:T(8,128)(2,1)}), bf16[4,16,8,2048]{3,2,1,0:T(8,128)(2,1)S(1)}, u32[]{:S(2)}, u32[]{:S(2)}) async-start(bf16[4,16,8,2048]{3,2,1,0:T(8,128)(2,1)} %copy-done), calls=%async_computation.4 | async-start | bytes 4194304 | tf_op jit(solution)/shard_map/all_to_all | solution.py:653
  (1 other events, 0.7 us)
Sparse Core Ops, SparseCore 0:
  10.1 46.3 all-gather.2
  161.8 31.0 reduce-scatter.3

commit v4 on v3

--- a/solution.py
+++ b/solution.py
@@ -112,7 +112,6 @@
     grad_hbm,
     stats_ref,
     gb_ref,
-    dsw_s,
     mixed_s,
     grad_ref,
     glu_s,
@@ -245,7 +244,6 @@
 
     def conv_body(i, carry):
         base = pl.multiple_of(i * rows, rows)
-        dsw_s[pl.ds(base, rows), :] = dot_general(delta_ref[pl.ds(base, rows), :], wout_ref[...], 1, 1)
         here = seg_s[pl.ds(base + EDGE, rows), :]
         acc = [jnp.zeros((rows, LANES), f32) for _ in range(2)]
         for j in range(taps):
@@ -259,7 +257,7 @@
 
     lax.fori_loop(0, blocks, conv_body, 0)
 
-    delta_swish = dsw_s[...]
+    delta_swish = dot_general(delta_ref[...], wout_ref[...], 1, 1)
     row_live = lax.broadcasted_iota(jnp.int32, (slots, LANES), 0) < live
     for h in range(2):
         pre = pre_s[h]
@@ -330,6 +328,12 @@
         dlt_ref[0, c:e, :] = (dglu * s).astype(bf16)
         dlt_ref[1, c:e, :] = (dglu * lin_s[c:e, :] * s * (1.0 - s)).astype(bf16)
 
+
+    for k in range(2):
+        for d in range(0, width, cols):
+            block = dot_general(dlt_ref[k], normed_ref[d : d + cols, :], 1, 1).astype(bf16)
+            grad_ref[k * per : (k + 1) * per, :, d : d + cols] = block.reshape(per, BLK, cols)
+        depart(4 + k, k * per, (k + 1) * per)
 
     unit = jnp.zeros((BLK, slots), f32)
     cross = jnp.zeros((BLK, slots), f32)
@@ -357,12 +361,6 @@
     below = pl.ds(part, SIDE)
     send(6 + 2 * chips, send_ref.at[:, below], send_hbm.at[:, below])
     send(7 + 2 * chips, keep_ref.at[:, below], keep_hbm.at[:, below])
-
-    for k in range(2):
-        for d in range(0, width, cols):
-            block = dot_general(dlt_ref[k], normed_ref[d : d + cols, :], 1, 1).astype(bf16)
-            grad_ref[k * per : (k + 1) * per, :, d : d + cols] = block.reshape(per, BLK, cols)
-        depart(4 + k, k * per, (k + 1) * per)
     for copy in sends:
         copy.wait()
 
@@ -563,7 +561,6 @@
         ),
         [
             pltpu.VMEM((width, BLK), f32),
-            pltpu.VMEM((slots, part), f32),
             pltpu.VMEM((2, chips, rows_part, width), bf16),
             pltpu.VMEM((pieces, BLK, width + 2 * LANES), bf16),
             pltpu.VMEM((2, slots + 2 * EDGE, LANES), f32),
@@ -617,7 +614,7 @@
     terms = {0: paired[0]}
     for j in range(chips - 1, 0, -1):
         terms[j] = lax.ppermute(paired[j], "zl", [(z, z ^ j) for z in range(chips)])
-    terms = [terms[j] for j in range(chips)]
+    terms = [terms[j] for j in (0, 3, 2, 1)]
 
     lines, peers = lax.axis_size("x"), lax.axis_size(("zh", "y"))
     grads = grads.reshape((lines, peers) + grads.shape[1:])

time: 220 us -> 218 us (level)
  the two profiles are of different devices: /device:TPU:72 before, /device:TPU:8 now
where the time goes in v4:
time: 218 us; the launch traced here: 217 us
  waiting for transfers between devices  79.9 us (37%)
  starting transfers between devices  59 us (27%)
  Pallas kernels  24.8 us (11%)
  blocking collectives  20.9 us (10%)
  between operations  16.9 us (8%)
  local copies, waits for them, and re-layouts  10.3 us (5%)
  other arithmetic  5.11 us (2%)
    pallas_call x9, Pallas kernels, call(): pl.pallas_call(kernel, out_shape=out_shape, in_specs=specs, out_specs=out...  24.8 us
    all_gather x1, blocking collectives, on_device(): own = lax.all_gather(packed_t, 'zl', axis=0)  20.9 us
    all_to_all x1, waiting for transfers between devices, on_device(): lax.all_to_all(shared, ('zh', 'y'), split_axis=0, concat_axis=0, tiled=True)  19.9 us
    all_to_all x1, starting transfers between devices, on_device(): lax.all_to_all(outbox, DP, split_axis=0, concat_axis=0, tiled=True)  19 us
    all_to_all x1, waiting for transfers between devices, on_device(): lax.all_to_all(grads, ('zh', 'y'), split_axis=0, concat_axis=0, tiled=True)  12.3 us
    all_to_all x1, waiting for transfers between devices, on_device(): lax.all_to_all(outbox, DP, split_axis=0, concat_axis=0, tiled=True)  12.1 us
    ppermute x3, waiting for transfers between devices, on_device(): terms[j] = lax.ppermute(paired[j], 'zl', [(z, z ^ j) for z in range(chips)])  11.8 us
    all_to_all x1, waiting for transfers between devices, on_device(): whole = lax.all_to_all(fanned, 'x', split_axis=0, concat_axis=0, tiled=True)  11.7 us
  transfers between devices with their start and end apart: 13, of which 9 were waited for; matrix products, arithmetic and copies ran while one was open for 5% of the time, Pallas kernels for 3%

profile of v4, /device:TPU:8, one launch (start us, length us, event | category | flops | bytes accessed | tf_op | source)
XLA Modules:
  0.0 216.9 jit_solution(12123248369906431086)
XLA Ops:
  9.5 1.7 shard_map.162
  11.2 19.0 %all-to-all-start = ((bf16[64,8,192]{2,1,0:T(8,128)(2,1)}), bf16[64,8,192]{2,1,0:T(8,128)(2,1)S(1)}, u32[]{:S(2)}, u32[]{:S(2)}) async-start(bf16[64,8,192]{2,1,0:T(8,128)(2,1)} %shard_map.162), calls=%async_computation | async-start | bytes 524288 | tf_op jit(solution)/shard_map/all_to_all | solution.py:535
  35.1 12.1 %all-to-all-done.arrived = bf16[64,8,192]{2,1,0:T(8,128)(2,1)S(1)} async-done(((bf16[64,8,192]{2,1,0:T(8,128)(2,1)}), bf16[64,8,192]{2,1,0:T(8,128)(2,1)S(1)}, u32[]{:S(2)}, u32[]{:S(2)}) %all-to-all-start) | async-done | bytes 196640 | tf_op jit(solution)/shard_map/all_to_all | solution.py:535
  48.1 20.9 %all-gather = bf16[768,512]{1,0:T(8,128)(2,1)S(1)} all-gather(bf16[192,512]{1,0:T(8,128)(2,1)S(1)} %get-tuple-element.35), channel_id=2, replica_groups=mesh['zh'=2,'y'=8,'x'=4,'zl'=4,'core'=2] {'zl'}, dimensions={0}, use_global_device_ids=true | all-gather | bytes 983040 | tf_op jit(solution)/shard_map/all_gather | solution.py:545
  69.0 1.9 collective-permute-start
  74.1 16.2 %shard_map.164 = (bf16[1536,512]{1,0:T(8,128)(2,1)}, bf16[4,208,512]{2,1,0:T(8,128)(2,1)}, bf16[4,208,512]{2,1,0:T(8,128)(2,1)}, bf16[4,64,1536]{2,1,0:T(8,128)(...) custom-call(s32[5]{0:T(128)} %copy-done.4, bf16[4,192,512]{2,1,0:T(8,128)(2,1)} %bitcast.35, ...), custom_call_target="tpu_custom_call" | custom-call | flops 3000000000 | bytes 12000000 | tf_op jit(solution)/shard_map/pallas_call | solution.py:41
  90.3 3.8 %all-to-all-start.1 = ((bf16[4,16,8,1792]{3,2,1,0:T(8,128)(2,1)}), bf16[4,16,8,1792]{3,2,1,0:T(8,128)(2,1)S(1)}, u32[]{:S(2)}, u32[]{:S(2)}) async-start(bf16[4,16,8,1792]{3,2,1,0:T(8,128)(2,1)} %bitcast.33), calls=%async_computation.1 | async-start | bytes 3670016 | tf_op jit(solution)/shard_map/all_to_all | solution.py:621
  94.2 1.9 collective-permute-start.1
  96.1 2.5 %collective-permute-done.1.got_ref = bf16[4,208,512]{2,1,0:T(8,128)(2,1)S(1)} collective-permute-done((bf16[4,208,512]{2,1,0:T(8,128)(2,1)}, bf16[4,208,512]{2,1,0:T(8,128)(2,1)S(1)}, u32[]{:S(2)}, u32[]{:S(2)}) %collective-permute-start.1) | collective-permute-done | bytes 852000 | tf_op jit(solution)/shard_map/ppermute | solution.py:610
  99.4 3.6 %collective-permute-start.2 = (bf16[208,512]{1,0:T(8,128)(2,1)S(1)}, bf16[208,512]{1,0:T(8,128)(2,1)S(1)}, u32[]{:S(2)}, u32[]{:S(2)}) collective-permute-start(bf16[208,512]{1,0:T(8,128)(2,1)S(1)} %get-tuple-element.43), channel_id=1, source_target_pairs={{0,6},{2,4},{4,2},{6,0},{1,7},{3,5},{5,3},{7,1},{8,14},{10,12},{12... | collective-permute-start | bytes 638984 | tf_op jit(solution)/shard_map/ppermute | solution.py:616
  103.0 1.9 collective-permute-start.3
  104.9 4.6 %collective-permute-start.4 = (bf16[208,512]{1,0:T(8,128)(2,1)S(1)}, bf16[208,512]{1,0:T(8,128)(2,1)S(1)}, u32[]{:S(2)}, u32[]{:S(2)}) collective-permute-start(bf16[208,512]{1,0:T(8,128)(2,1)S(1)} %get-tuple-element.45), channel_id=1, source_target_pairs={{0,2},{2,0},{4,6},{6,4},{1,3},{3,1},{5,7},{7,5},{8,10},{10,8},{12,... | collective-permute-start | bytes 638984 | tf_op jit(solution)/shard_map/ppermute | solution.py:616
  109.5 1.8 collective-permute-done.2.dn1
  111.3 10.1 %collective-permute-done.3.dn2 = bf16[208,512]{1,0:T(8,128)(2,1)S(1)} collective-permute-done((bf16[208,512]{1,0:T(8,128)(2,1)S(1)}, bf16[208,512]{1,0:T(8,128)(2,1)S(1)}, u32[]{:S(2)}, u32[]{:S(2)}) %collective-permute-start.3) | collective-permute-done | bytes 213024 | tf_op jit(solution)/shard_map/ppermute | solution.py:616
  122.4 10.0 %all-to-all-start.2 = ((bf16[16,8,1792]{2,1,0:T(8,128)(2,1)}), bf16[16,8,1792]{2,1,0:T(8,128)(2,1)S(1)}, u32[]{:S(2)}, u32[]{:S(2)}) async-start(bf16[16,8,1792]{2,1,0:T(8,128)(2,1)} %shard_map.166), calls=%async_computation.2 | async-start | bytes 917504 | tf_op jit(solution)/shard_map/all_to_all | solution.py:624
  132.4 1.9 collective-permute-start.5
  136.9 12.3 %all-to-all-done.2.in_ref = bf16[16,8,1792]{2,1,0:T(8,128)(2,1)S(1)} async-done(((bf16[16,8,1792]{2,1,0:T(8,128)(2,1)}), bf16[16,8,1792]{2,1,0:T(8,128)(2,1)S(1)}, u32[]{:S(2)}, u32[]{:S(2)}) %all-to-all-start.2) | async-done | bytes 458784 | tf_op jit(solution)/shard_map/all_to_all | solution.py:624
  150.2 5.4 %all-to-all-start.3 = ((bf16[16,8,2816]{2,1,0:T(8,128)(2,1)}), bf16[16,8,2816]{2,1,0:T(8,128)(2,1)S(1)}, u32[]{:S(2)}, u32[]{:S(2)}) async-start(bf16[16,8,2816]{2,1,0:T(8,128)(2,1)} %shard_map.168), calls=%async_computation.3 | async-start | bytes 1441792 | tf_op jit(solution)/shard_map/all_to_all | solution.py:646
  155.6 2.2 %add_convert_fusion = bf16[4,64,1536]{2,1,0:T(8,128)(2,1)} fusion(bf16[4,64,1536]{2,1,0:T(8,128)(2,1)} %collective-permute-done.5, bf16[4,64,1536]{2,1,0:T(8,128)(2,1)S(1)} %copy-done.7), kind=kLoop, calls=%fused_computation | loop fusion | flops 1572864 | bytes 2359296 | tf_op jit(solution)/shard_map/convert_element_type | solution.py:628
  157.9 19.9 %all-to-all-done.3.in_ref = bf16[16,8,2816]{2,1,0:T(8,128)(2,1)S(1)} async-done(((bf16[16,8,2816]{2,1,0:T(8,128)(2,1)}), bf16[16,8,2816]{2,1,0:T(8,128)(2,1)S(1)}, u32[]{:S(2)}, u32[]{:S(2)}) %all-to-all-start.3) | async-done | bytes 720928 | tf_op jit(solution)/shard_map/all_to_all | solution.py:646
  179.2 4.7 %all-to-all-start.4 = ((bf16[4,16,8,2048]{3,2,1,0:T(8,128)(2,1)}), bf16[4,16,8,2048]{3,2,1,0:T(8,128)(2,1)S(1)}, u32[]{:S(2)}, u32[]{:S(2)}) async-start(bf16[4,16,8,2048]{3,2,1,0:T(8,128)(2,1)} %copy-done), calls=%async_computation.4 | async-start | bytes 4194304 | tf_op jit(solution)/shard_map/all_to_all | solution.py:650
  184.9 7.7 %reduce-scatter.4.cloned.1.call-done = bf16[64,1536]{1,0:T(8,128)(2,1)} async-done(((bf16[256,1536]{1,0:T(8,128)(2,1)}), bf16[64,1536]{1,0:T(8,128)(2,1)}) %reduce-scatter.4.cloned.1.call-update) | async-done | bytes 196624
  195.7 11.7 %all-to-all-done.4 = bf16[4,16,8,2048]{3,2,1,0:T(8,128)(2,1)S(1)} async-done(((bf16[4,16,8,2048]{3,2,1,0:T(8,128)(2,1)}), bf16[4,16,8,2048]{3,2,1,0:T(8,128)(2,1)S(1)}, u32[]{:S(2)}, u32[]{:S(2)}) %all-to-all-start.4) | async-done | bytes 2097184 | tf_op jit(solution)/shard_map/all_to_all | solution.py:650
  207.5 2.0 shard_map.170
  (56 shorter events, 20.0 us)
Async XLA Ops:
  7.2 63.8 %copy-start.9 = (f32[1536]{0:T(1024)S(1)}, f32[1536]{0:T(1024)}, u32[]{:S(2)}) copy-start(f32[1536]{0:T(1024)} %param.12) | copy-start | bytes 18436
  7.2 64.4 %copy-start.10 = (f32[1536]{0:T(1024)S(1)}, f32[1536]{0:T(1024)}, u32[]{:S(2)}) copy-start(f32[1536]{0:T(1024)} %param.13) | copy-start | bytes 18436
  7.2 66.0 %all-gather.3.cloned.1.call-start = ((), (), s32[]{:S(2)}) async-start(), calls=%async_computation.6 | async-start | bytes 1769472 | tf_op jit(solution)/shard_map/all_gather | solution.py:509
  7.9 0.9 copy-start.2
  11.2 36.1 %all-to-all-start = ((bf16[64,8,192]{2,1,0:T(8,128)(2,1)}), bf16[64,8,192]{2,1,0:T(8,128)(2,1)S(1)}, u32[]{:S(2)}, u32[]{:S(2)}) async-start(bf16[64,8,192]{2,1,0:T(8,128)(2,1)} %shard_map.162), calls=%async_computation | async-start | bytes 524288 | tf_op jit(solution)/shard_map/all_to_all | solution.py:535
  35.1 38.0 %copy-start.4 = (s32[5]{0:T(128)}, s32[5]{0:T(128)S(1)}, u32[]{:S(2)}) copy-start(s32[5]{0:T(128)S(1)} %stack.19.scalars) | copy-start | bytes 64
  69.0 4.2 %copy-start.8 = (bf16[768,512]{1,0:T(8,128)(2,1)}, bf16[768,512]{1,0:T(8,128)(2,1)S(1)}, u32[]{:S(2)}) copy-start(bf16[768,512]{1,0:T(8,128)(2,1)S(1)} %all-gather) | copy-start | bytes 2359300
  69.0 4.2 %collective-permute-start = (bf16[4,192,512]{2,1,0:T(8,128)(2,1)S(1)}, bf16[4,192,512]{2,1,0:T(8,128)(2,1)S(1)}, u32[]{:S(2)}, u32[]{:S(2)}) collective-permute-start(bf16[4,192,512]{2,1,0:T(8,128)(2,1)S(1)} %bitcast.34), channel_id=1, source_target_pairs={{0,1},{1,0},{2,3},{3,2},{4,5},{5,4},{6,7},{7,6},{8,9},{9,8},{10,11... | collective-permute-start | bytes 2359304 | tf_op jit(solution)/shard_map/ppermute | solution.py:546
  73.2 0.9 copy-start.11
  90.3 8.3 %copy-start.1 = (bf16[4,208,512]{2,1,0:T(8,128)(2,1)S(1)}, bf16[4,208,512]{2,1,0:T(8,128)(2,1)}, u32[]{:S(2)}) copy-start(bf16[4,208,512]{2,1,0:T(8,128)(2,1)} %get-tuple-element.40.keep_ref) | copy-start | bytes 2555908
  90.3 8.3 %copy-start.5 = (s32[5]{0:T(128)S(1)}, s32[5]{0:T(128)}, u32[]{:S(2)}) copy-start(s32[5]{0:T(128)} %copy-done.4) | copy-start | bytes 64
  90.3 31.0 %all-to-all-start.1 = ((bf16[4,16,8,1792]{3,2,1,0:T(8,128)(2,1)}), bf16[4,16,8,1792]{3,2,1,0:T(8,128)(2,1)S(1)}, u32[]{:S(2)}, u32[]{:S(2)}) async-start(bf16[4,16,8,1792]{3,2,1,0:T(8,128)(2,1)} %bitcast.33), calls=%async_computation.1 | async-start | bytes 3670016 | tf_op jit(solution)/shard_map/all_to_all | solution.py:621
  94.2 4.5 %collective-permute-start.1 = (bf16[4,208,512]{2,1,0:T(8,128)(2,1)}, bf16[4,208,512]{2,1,0:T(8,128)(2,1)S(1)}, u32[]{:S(2)}, u32[]{:S(2)}) collective-permute-start(bf16[4,208,512]{2,1,0:T(8,128)(2,1)} %get-tuple-element.41), channel_id=1, source_target_pairs={{0,1},{1,0},{2,3},{3,2},{4,5},{5,4},{6,7},{7,6},{8,9},{9,8},{10,11... | collective-permute-start | bytes 2555912 | tf_op jit(solution)/shard_map/ppermute | solution.py:610
  99.4 11.9 %collective-permute-start.2 = (bf16[208,512]{1,0:T(8,128)(2,1)S(1)}, bf16[208,512]{1,0:T(8,128)(2,1)S(1)}, u32[]{:S(2)}, u32[]{:S(2)}) collective-permute-start(bf16[208,512]{1,0:T(8,128)(2,1)S(1)} %get-tuple-element.43), channel_id=1, source_target_pairs={{0,6},{2,4},{4,2},{6,0},{1,7},{3,5},{5,3},{7,1},{8,14},{10,12},{12... | collective-permute-start | bytes 638984 | tf_op jit(solution)/shard_map/ppermute | solution.py:616
  103.0 18.3 %collective-permute-start.3 = (bf16[208,512]{1,0:T(8,128)(2,1)S(1)}, bf16[208,512]{1,0:T(8,128)(2,1)S(1)}, u32[]{:S(2)}, u32[]{:S(2)}) collective-permute-start(bf16[208,512]{1,0:T(8,128)(2,1)S(1)} %get-tuple-element.44), channel_id=1, source_target_pairs={{0,4},{2,6},{4,0},{6,2},{1,5},{3,7},{5,1},{7,3},{8,12},{10,14},{12... | collective-permute-start | bytes 638984 | tf_op jit(solution)/shard_map/ppermute | solution.py:616
  104.9 16.4 %collective-permute-start.4 = (bf16[208,512]{1,0:T(8,128)(2,1)S(1)}, bf16[208,512]{1,0:T(8,128)(2,1)S(1)}, u32[]{:S(2)}, u32[]{:S(2)}) collective-permute-start(bf16[208,512]{1,0:T(8,128)(2,1)S(1)} %get-tuple-element.45), channel_id=1, source_target_pairs={{0,2},{2,0},{4,6},{6,4},{1,3},{3,1},{5,7},{7,5},{8,10},{10,8},{12,... | collective-permute-start | bytes 638984 | tf_op jit(solution)/shard_map/ppermute | solution.py:616
  121.4 14.2 %copy-start.3 = (f32[8,512]{1,0:T(8,128)S(1)}, f32[8,512]{1,0:T(8,128)}, u32[]{:S(2)}) copy-start(f32[8,512]{1,0:T(8,128)} %get-tuple-element.57.stats_ref) | copy-start | bytes 49156
  122.4 26.8 %all-to-all-start.2 = ((bf16[16,8,1792]{2,1,0:T(8,128)(2,1)}), bf16[16,8,1792]{2,1,0:T(8,128)(2,1)S(1)}, u32[]{:S(2)}, u32[]{:S(2)}) async-start(bf16[16,8,1792]{2,1,0:T(8,128)(2,1)} %shard_map.166), calls=%async_computation.2 | async-start | bytes 917504 | tf_op jit(solution)/shard_map/all_to_all | solution.py:624
  132.4 23.2 %collective-permute-start.5 = (bf16[4,64,1536]{2,1,0:T(8,128)(2,1)}, bf16[4,64,1536]{2,1,0:T(8,128)(2,1)}, u32[]{:S(2)}, u32[]{:S(2)}) collective-permute-start(bf16[4,64,1536]{2,1,0:T(8,128)(2,1)} %get-tuple-element.50), channel_id=1, source_target_pairs={{0,1},{1,0},{2,3},{3,2},{4,5},{5,4},{6,7},{7,6},{8,9},{9,8},{10,11... | collective-permute-start | bytes 2359304 | tf_op jit(solution)/shard_map/ppermute | solution.py:627
  136.9 18.8 %copy-start.7 = (bf16[4,64,1536]{2,1,0:T(8,128)(2,1)S(1)}, bf16[4,64,1536]{2,1,0:T(8,128)(2,1)}, u32[]{:S(2)}) copy-start(bf16[4,64,1536]{2,1,0:T(8,128)(2,1)} %get-tuple-element.37) | copy-start | bytes 2359300
  150.2 27.6 %all-to-all-start.3 = ((bf16[16,8,2816]{2,1,0:T(8,128)(2,1)}), bf16[16,8,2816]{2,1,0:T(8,128)(2,1)S(1)}, u32[]{:S(2)}, u32[]{:S(2)}) async-start(bf16[16,8,2816]{2,1,0:T(8,128)(2,1)} %shard_map.168), calls=%async_computation.3 | async-start | bytes 1441792 | tf_op jit(solution)/shard_map/all_to_all | solution.py:646
  155.6 36.9 %reduce-scatter.4.cloned.1.call-start = ((), (), s32[]{:S(2)}) async-start(), calls=%async_computation.7 | async-start | bytes 983040
  177.9 1.3 copy-start
  179.2 28.2 %all-to-all-start.4 = ((bf16[4,16,8,2048]{3,2,1,0:T(8,128)(2,1)}), bf16[4,16,8,2048]{3,2,1,0:T(8,128)(2,1)S(1)}, u32[]{:S(2)}, u32[]{:S(2)}) async-start(bf16[4,16,8,2048]{3,2,1,0:T(8,128)(2,1)} %copy-done), calls=%async_computation.4 | async-start | bytes 4194304 | tf_op jit(solution)/shard_map/all_to_all | solution.py:650
  (1 other events, 0.7 us)
Sparse Core Ops, SparseCore 0:
  10.1 48.9 all-gather.2
  159.8 32.6 reduce-scatter.3

commit v5 on v4

--- a/solution.py
+++ b/solution.py
@@ -31,11 +31,11 @@
         specs = [pl.BlockSpec(memory_space=pltpu.SMEM)] * smem
         specs += [pl.BlockSpec(memory_space=pltpu.VMEM)] * (len(args) - smem)
         for place in copied:
-            specs[place] = pl.BlockSpec(memory_space=pl.ANY)
+            specs[place] = pl.BlockSpec(memory_space=pltpu.HBM)
         outs = jax.tree.map(lambda _: pl.BlockSpec(memory_space=pltpu.VMEM), out_shape)
         if sent:
             outs = tuple(
-                pl.BlockSpec(memory_space=pl.ANY if k in sent else pltpu.VMEM)
+                pl.BlockSpec(memory_space=pltpu.HBM if k in sent else pltpu.VMEM)
                 for k in range(len(out_shape))
             )
         return pl.pallas_call(
@@ -211,7 +211,7 @@
     def square_body(i, acc):
         return acc + fold(jnp.square(x_ref[pl.ds(i * chunk, chunk), :].astype(f32) - center))
 
-    spread = jnp.sum(lax.fori_loop(0, steps, square_body, zero, unroll=2), axis=0, keepdims=True) / width
+    spread = jnp.sum(lax.fori_loop(0, steps, square_body, zero, unroll=8), axis=0, keepdims=True) / width
     row_scale = lax.rsqrt(spread + epsilon)
     stats_ref[...] = jnp.zeros_like(stats_ref)
     stats_ref[0:1, :] = center
@@ -223,7 +223,7 @@
         normed_ref[at, :] = (standard * gb_ref[at, 0:1] + gb_ref[at, 1:2]).astype(bf16)
         return carry
 
-    lax.fori_loop(0, steps, norm_body, 0, unroll=2)
+    lax.fori_loop(0, steps, norm_body, 0, unroll=8)
 
 
     copies[2].wait()
@@ -432,15 +432,24 @@
         frame_ref[c:e, :] = jnp.transpose(turned_rows[:, c:e]).astype(bf16)
 
 
-def fan_kernel(in_ref, out_ref):
-    lines, peers, _, full = out_ref.shape
+def fan_kernel(in_ref, out_hbm, sems):
+    lines, _, _, full = out_hbm.shape
     wide = full - 2 * LANES
-    for i in range(peers):
-        piece = in_ref[i, :, 0:wide]
-        for k in range(lines):
-            at = wide + k * 2 * LANES
-            out_ref[k, i, :, 0:wide] = piece
-            out_ref[k, i, :, wide:full] = in_ref[i, :, at : at + 2 * LANES]
+    copies = []
+    for k in range(lines):
+        at = wide + k * 2 * LANES
+        to = out_hbm.at[k]
+        for n, (source, target) in enumerate(
+            (
+                (in_ref.at[:, :, 0:wide], to.at[:, :, 0:wide]),
+                (in_ref.at[:, :, at : at + 2 * LANES], to.at[:, :, wide:full]),
+            )
+        ):
+            copies.append(pltpu.make_async_copy(source, target, sems.at[2 * k + n]))
+    for copy in copies:
+        copy.start()
+    for copy in copies:
+        copy.wait()
 
 
 def row_kernel(scalars, dn0, dn1, dn2, dn3, x_ref, stats_ref, gain_ref, delta_ref, out_ref, held):
@@ -531,6 +540,7 @@
         1000,
         400000,
         (2,),
+        room=60,
     )(replica_blocks, my_index[None], frames.T)
     arrived = lax.all_to_all(outbox, DP, split_axis=0, concat_axis=0, tiled=True)
 
@@ -644,8 +654,16 @@
         share_kernel, sds((peers, BLK, wide + lines * 2 * LANES), bf16), [], 0, 1000000, 1500000
     )(grads, homebound.reshape(peers, lines, BLK, 2 * LANES))
     shared = lax.all_to_all(shared, ("zh", "y"), split_axis=0, concat_axis=0, tiled=True)
-    fanned = full_call(
-        fan_kernel, sds((lines, peers, BLK, wide + 2 * LANES), bf16), [], 0, 1000000, 3000000
+    fanned, = full_call(
+        fan_kernel,
+        (sds((lines, peers, BLK, wide + 2 * LANES), bf16),),
+        [pltpu.SemaphoreType.DMA((2 * lines,))],
+        0,
+        1000000,
+        3000000,
+        (),
+        (0,),
+        room=16,
     )(shared)
     whole = lax.all_to_all(fanned, "x", split_axis=0, concat_axis=0, tiled=True)
     whole = whole.reshape((pieces,) + whole.shape[2:])

time: 218 us -> 217 us (level)
    unnamed x26 -> x22, local copies, waits for them, and re-layouts: 5.83 us -> 4.31 us
where the time goes in v5:
time: 217 us; the launch traced here: 216 us
  waiting for transfers between devices  80 us (37%)
  starting transfers between devices  58.6 us (27%)
  Pallas kernels  25.3 us (12%)
  blocking collectives  21.5 us (10%)
  between operations  16.9 us (8%)
  local copies, waits for them, and re-layouts  8.76 us (4%)
  other arithmetic  5.11 us (2%)
    pallas_call x9, Pallas kernels, call(): pl.pallas_call(kernel, out_shape=out_shape, in_specs=specs, out_specs=out...  25.3 us
    all_gather x1, blocking collectives, on_device(): own = lax.all_gather(packed_t, 'zl', axis=0)  21.5 us
    all_to_all x1, waiting for transfers between devices, on_device(): lax.all_to_all(shared, ('zh', 'y'), split_axis=0, concat_axis=0, tiled=True)  19.9 us
    all_to_all x1, starting transfers between devices, on_device(): lax.all_to_all(outbox, DP, split_axis=0, concat_axis=0, tiled=True)  19 us
    all_to_all x1, waiting for transfers between devices, on_device(): lax.all_to_all(grads, ('zh', 'y'), split_axis=0, concat_axis=0, tiled=True)  12.3 us
    all_to_all x1, waiting for transfers between devices, on_device(): lax.all_to_all(outbox, DP, split_axis=0, concat_axis=0, tiled=True)  12.1 us
    ppermute x3, waiting for transfers between devices, on_device(): terms[j] = lax.ppermute(paired[j], 'zl', [(z, z ^ j) for z in range(chips)])  12 us
    all_to_all x1, waiting for transfers between devices, on_device(): whole = lax.all_to_all(fanned, 'x', split_axis=0, concat_axis=0, tiled=True)  11.9 us
  transfers between devices with their start and end apart: 13, of which 9 were waited for; matrix products, arithmetic and copies ran while one was open for 5% of the time, Pallas kernels for 3%

profile of v5, /device:TPU:8, one launch (start us, length us, event | category | flops | bytes accessed | tf_op | source)
XLA Modules:
  0.0 216.2 jit_solution(15463611159110294993)
XLA Ops:
  7.9 2.6 %shard_map.162 = bf16[64,8,192]{2,1,0:T(8,128)(2,1)} custom-call(s32[64]{0:T(128)} %replica_blocks.1, s32[1]{0:T(128)} %bitcast.6.place, bf16[192,256]{1,0:T(8,128)(2,1)} %bitcast.34), custom_call_target="tpu_custom_call" | custom-call | flops 1000 | bytes 400000 | tf_op jit(solution)/shard_map/pallas_call | solution.py:41
  10.5 19.0 %all-to-all-start = ((bf16[64,8,192]{2,1,0:T(8,128)(2,1)}), bf16[64,8,192]{2,1,0:T(8,128)(2,1)S(1)}, u32[]{:S(2)}, u32[]{:S(2)}) async-start(bf16[64,8,192]{2,1,0:T(8,128)(2,1)} %shard_map.162), calls=%async_computation | async-start | bytes 524288 | tf_op jit(solution)/shard_map/all_to_all | solution.py:545
  34.5 12.1 %all-to-all-done.arrived = bf16[64,8,192]{2,1,0:T(8,128)(2,1)S(1)} async-done(((bf16[64,8,192]{2,1,0:T(8,128)(2,1)}), bf16[64,8,192]{2,1,0:T(8,128)(2,1)S(1)}, u32[]{:S(2)}, u32[]{:S(2)}) %all-to-all-start) | async-done | bytes 196640 | tf_op jit(solution)/shard_map/all_to_all | solution.py:545
  47.5 21.5 %all-gather = bf16[768,512]{1,0:T(8,128)(2,1)S(1)} all-gather(bf16[192,512]{1,0:T(8,128)(2,1)S(1)} %get-tuple-element.35), channel_id=2, replica_groups=mesh['zh'=2,'y'=8,'x'=4,'zl'=4,'core'=2] {'zl'}, dimensions={0}, use_global_device_ids=true | all-gather | bytes 983040 | tf_op jit(solution)/shard_map/all_gather | solution.py:555
  69.0 1.9 collective-permute-start
  74.1 15.6 %shard_map.164 = (bf16[1536,512]{1,0:T(8,128)(2,1)}, bf16[4,208,512]{2,1,0:T(8,128)(2,1)}, bf16[4,208,512]{2,1,0:T(8,128)(2,1)}, bf16[4,64,1536]{2,1,0:T(8,128)(...) custom-call(s32[5]{0:T(128)} %copy-done.3, bf16[4,192,512]{2,1,0:T(8,128)(2,1)} %bitcast.33, ...), custom_call_target="tpu_custom_call" | custom-call | flops 3000000000 | bytes 12000000 | tf_op jit(solution)/shard_map/pallas_call | solution.py:41
  89.8 3.7 %all-to-all-start.1 = ((bf16[4,16,8,1792]{3,2,1,0:T(8,128)(2,1)}), bf16[4,16,8,1792]{3,2,1,0:T(8,128)(2,1)S(1)}, u32[]{:S(2)}, u32[]{:S(2)}) async-start(bf16[4,16,8,1792]{3,2,1,0:T(8,128)(2,1)} %bitcast.31), calls=%async_computation.1 | async-start | bytes 3670016 | tf_op jit(solution)/shard_map/all_to_all | solution.py:631
  93.5 2.0 collective-permute-start.1
  95.5 2.4 %collective-permute-done.1.got_ref = bf16[4,208,512]{2,1,0:T(8,128)(2,1)S(1)} collective-permute-done((bf16[4,208,512]{2,1,0:T(8,128)(2,1)}, bf16[4,208,512]{2,1,0:T(8,128)(2,1)S(1)}, u32[]{:S(2)}, u32[]{:S(2)}) %collective-permute-start.1) | collective-permute-done | bytes 852000 | tf_op jit(solution)/shard_map/ppermute | solution.py:620
  98.7 3.8 %collective-permute-start.2 = (bf16[208,512]{1,0:T(8,128)(2,1)S(1)}, bf16[208,512]{1,0:T(8,128)(2,1)S(1)}, u32[]{:S(2)}, u32[]{:S(2)}) collective-permute-start(bf16[208,512]{1,0:T(8,128)(2,1)S(1)} %get-tuple-element.43), channel_id=1, source_target_pairs={{0,6},{2,4},{4,2},{6,0},{1,7},{3,5},{5,3},{7,1},{8,14},{10,12},{12... | collective-permute-start | bytes 638984 | tf_op jit(solution)/shard_map/ppermute | solution.py:626
  102.5 1.9 collective-permute-start.3
  104.5 4.4 %collective-permute-start.4 = (bf16[208,512]{1,0:T(8,128)(2,1)S(1)}, bf16[208,512]{1,0:T(8,128)(2,1)S(1)}, u32[]{:S(2)}, u32[]{:S(2)}) collective-permute-start(bf16[208,512]{1,0:T(8,128)(2,1)S(1)} %get-tuple-element.45), channel_id=1, source_target_pairs={{0,2},{2,0},{4,6},{6,4},{1,3},{3,1},{5,7},{7,5},{8,10},{10,8},{12,... | collective-permute-start | bytes 638984 | tf_op jit(solution)/shard_map/ppermute | solution.py:626
  108.9 1.8 collective-permute-done.2.dn1
  110.6 10.3 %collective-permute-done.3.dn2 = bf16[208,512]{1,0:T(8,128)(2,1)S(1)} collective-permute-done((bf16[208,512]{1,0:T(8,128)(2,1)S(1)}, bf16[208,512]{1,0:T(8,128)(2,1)S(1)}, u32[]{:S(2)}, u32[]{:S(2)}) %collective-permute-start.3) | collective-permute-done | bytes 213024 | tf_op jit(solution)/shard_map/ppermute | solution.py:626
  121.9 9.7 %all-to-all-start.2 = ((bf16[16,8,1792]{2,1,0:T(8,128)(2,1)}), bf16[16,8,1792]{2,1,0:T(8,128)(2,1)S(1)}, u32[]{:S(2)}, u32[]{:S(2)}) async-start(bf16[16,8,1792]{2,1,0:T(8,128)(2,1)} %shard_map.166), calls=%async_computation.2 | async-start | bytes 917504 | tf_op jit(solution)/shard_map/all_to_all | solution.py:634
  131.6 1.9 collective-permute-start.5
  136.0 12.3 %all-to-all-done.2.in_ref = bf16[16,8,1792]{2,1,0:T(8,128)(2,1)S(1)} async-done(((bf16[16,8,1792]{2,1,0:T(8,128)(2,1)}), bf16[16,8,1792]{2,1,0:T(8,128)(2,1)S(1)}, u32[]{:S(2)}, u32[]{:S(2)}) %all-to-all-start.2) | async-done | bytes 458784 | tf_op jit(solution)/shard_map/all_to_all | solution.py:634
  149.3 5.4 %all-to-all-start.3 = ((bf16[16,8,2816]{2,1,0:T(8,128)(2,1)}), bf16[16,8,2816]{2,1,0:T(8,128)(2,1)S(1)}, u32[]{:S(2)}, u32[]{:S(2)}) async-start(bf16[16,8,2816]{2,1,0:T(8,128)(2,1)} %shard_map.168), calls=%async_computation.3 | async-start | bytes 1441792 | tf_op jit(solution)/shard_map/all_to_all | solution.py:656
  154.8 2.2 %add_convert_fusion = bf16[4,64,1536]{2,1,0:T(8,128)(2,1)} fusion(bf16[4,64,1536]{2,1,0:T(8,128)(2,1)} %collective-permute-done.5, bf16[4,64,1536]{2,1,0:T(8,128)(2,1)S(1)} %copy-done.5), kind=kLoop, calls=%fused_computation | loop fusion | flops 1572864 | bytes 2359296 | tf_op jit(solution)/shard_map/convert_element_type | solution.py:638
  157.0 19.9 %all-to-all-done.3.in_ref = bf16[16,8,2816]{2,1,0:T(8,128)(2,1)S(1)} async-done(((bf16[16,8,2816]{2,1,0:T(8,128)(2,1)}), bf16[16,8,2816]{2,1,0:T(8,128)(2,1)S(1)}, u32[]{:S(2)}, u32[]{:S(2)}) %all-to-all-start.3) | async-done | bytes 720928 | tf_op jit(solution)/shard_map/all_to_all | solution.py:656
  178.6 4.7 %all-to-all-start.4 = ((bf16[4,16,8,2048]{3,2,1,0:T(8,128)(2,1)}), bf16[4,16,8,2048]{3,2,1,0:T(8,128)(2,1)S(1)}, u32[]{:S(2)}, u32[]{:S(2)}) async-start(bf16[4,16,8,2048]{3,2,1,0:T(8,128)(2,1)} %copy-done), calls=%async_computation.4 | async-start | bytes 4194304 | tf_op jit(solution)/shard_map/all_to_all | solution.py:668
  184.2 7.5 %reduce-scatter.4.cloned.1.call-done = bf16[64,1536]{1,0:T(8,128)(2,1)} async-done(((bf16[256,1536]{1,0:T(8,128)(2,1)}), bf16[64,1536]{1,0:T(8,128)(2,1)}) %reduce-scatter.4.cloned.1.call-update) | async-done | bytes 196624
  195.0 11.9 %all-to-all-done.4 = bf16[4,16,8,2048]{3,2,1,0:T(8,128)(2,1)S(1)} async-done(((bf16[4,16,8,2048]{3,2,1,0:T(8,128)(2,1)}), bf16[4,16,8,2048]{3,2,1,0:T(8,128)(2,1)S(1)}, u32[]{:S(2)}, u32[]{:S(2)}) %all-to-all-start.4) | async-done | bytes 2097184 | tf_op jit(solution)/shard_map/all_to_all | solution.py:668
  206.8 2.0 shard_map.170
  (52 shorter events, 18.6 us)
Async XLA Ops:
  7.2 63.7 %copy-start.7 = (f32[1536]{0:T(1024)S(1)}, f32[1536]{0:T(1024)}, u32[]{:S(2)}) copy-start(f32[1536]{0:T(1024)} %param.12) | copy-start | bytes 18436
  7.2 64.3 %copy-start.8 = (f32[1536]{0:T(1024)S(1)}, f32[1536]{0:T(1024)}, u32[]{:S(2)}) copy-start(f32[1536]{0:T(1024)} %param.13) | copy-start | bytes 18436
  7.2 65.9 %all-gather.3.cloned.1.call-start = ((), (), s32[]{:S(2)}) async-start(), calls=%async_computation.6 | async-start | bytes 1769472 | tf_op jit(solution)/shard_map/all_gather | solution.py:518
  10.5 36.1 %all-to-all-start = ((bf16[64,8,192]{2,1,0:T(8,128)(2,1)}), bf16[64,8,192]{2,1,0:T(8,128)(2,1)S(1)}, u32[]{:S(2)}, u32[]{:S(2)}) async-start(bf16[64,8,192]{2,1,0:T(8,128)(2,1)} %shard_map.162), calls=%async_computation | async-start | bytes 524288 | tf_op jit(solution)/shard_map/all_to_all | solution.py:545
  34.5 38.7 %copy-start.3 = (s32[5]{0:T(128)}, s32[5]{0:T(128)S(1)}, u32[]{:S(2)}) copy-start(s32[5]{0:T(128)S(1)} %stack.19.scalars) | copy-start | bytes 64
  69.0 4.2 %copy-start.6 = (bf16[768,512]{1,0:T(8,128)(2,1)}, bf16[768,512]{1,0:T(8,128)(2,1)S(1)}, u32[]{:S(2)}) copy-start(bf16[768,512]{1,0:T(8,128)(2,1)S(1)} %all-gather) | copy-start | bytes 2359300
  69.0 4.2 %collective-permute-start = (bf16[4,192,512]{2,1,0:T(8,128)(2,1)S(1)}, bf16[4,192,512]{2,1,0:T(8,128)(2,1)S(1)}, u32[]{:S(2)}, u32[]{:S(2)}) collective-permute-start(bf16[4,192,512]{2,1,0:T(8,128)(2,1)S(1)} %bitcast.32), channel_id=1, source_target_pairs={{0,1},{1,0},{2,3},{3,2},{4,5},{5,4},{6,7},{7,6},{8,9},{9,8},{10,11... | collective-permute-start | bytes 2359304 | tf_op jit(solution)/shard_map/ppermute | solution.py:556
  73.1 0.9 copy-start.9
  89.7 8.2 %copy-start.1 = (bf16[4,208,512]{2,1,0:T(8,128)(2,1)S(1)}, bf16[4,208,512]{2,1,0:T(8,128)(2,1)}, u32[]{:S(2)}) copy-start(bf16[4,208,512]{2,1,0:T(8,128)(2,1)} %get-tuple-element.40.keep_ref) | copy-start | bytes 2555908
  89.7 8.2 %copy-start.4 = (s32[5]{0:T(128)S(1)}, s32[5]{0:T(128)}, u32[]{:S(2)}) copy-start(s32[5]{0:T(128)} %copy-done.3) | copy-start | bytes 64
  89.8 31.1 %all-to-all-start.1 = ((bf16[4,16,8,1792]{3,2,1,0:T(8,128)(2,1)}), bf16[4,16,8,1792]{3,2,1,0:T(8,128)(2,1)S(1)}, u32[]{:S(2)}, u32[]{:S(2)}) async-start(bf16[4,16,8,1792]{3,2,1,0:T(8,128)(2,1)} %bitcast.31), calls=%async_computation.1 | async-start | bytes 3670016 | tf_op jit(solution)/shard_map/all_to_all | solution.py:631
  93.5 4.5 %collective-permute-start.1 = (bf16[4,208,512]{2,1,0:T(8,128)(2,1)}, bf16[4,208,512]{2,1,0:T(8,128)(2,1)S(1)}, u32[]{:S(2)}, u32[]{:S(2)}) collective-permute-start(bf16[4,208,512]{2,1,0:T(8,128)(2,1)} %get-tuple-element.41), channel_id=1, source_target_pairs={{0,1},{1,0},{2,3},{3,2},{4,5},{5,4},{6,7},{7,6},{8,9},{9,8},{10,11... | collective-permute-start | bytes 2555912 | tf_op jit(solution)/shard_map/ppermute | solution.py:620
  98.7 11.9 %collective-permute-start.2 = (bf16[208,512]{1,0:T(8,128)(2,1)S(1)}, bf16[208,512]{1,0:T(8,128)(2,1)S(1)}, u32[]{:S(2)}, u32[]{:S(2)}) collective-permute-start(bf16[208,512]{1,0:T(8,128)(2,1)S(1)} %get-tuple-element.43), channel_id=1, source_target_pairs={{0,6},{2,4},{4,2},{6,0},{1,7},{3,5},{5,3},{7,1},{8,14},{10,12},{12... | collective-permute-start | bytes 638984 | tf_op jit(solution)/shard_map/ppermute | solution.py:626
  102.5 18.3 %collective-permute-start.3 = (bf16[208,512]{1,0:T(8,128)(2,1)S(1)}, bf16[208,512]{1,0:T(8,128)(2,1)S(1)}, u32[]{:S(2)}, u32[]{:S(2)}) collective-permute-start(bf16[208,512]{1,0:T(8,128)(2,1)S(1)} %get-tuple-element.44), channel_id=1, source_target_pairs={{0,4},{2,6},{4,0},{6,2},{1,5},{3,7},{5,1},{7,3},{8,12},{10,14},{12... | collective-permute-start | bytes 638984 | tf_op jit(solution)/shard_map/ppermute | solution.py:626
  104.5 16.4 %collective-permute-start.4 = (bf16[208,512]{1,0:T(8,128)(2,1)S(1)}, bf16[208,512]{1,0:T(8,128)(2,1)S(1)}, u32[]{:S(2)}, u32[]{:S(2)}) collective-permute-start(bf16[208,512]{1,0:T(8,128)(2,1)S(1)} %get-tuple-element.45), channel_id=1, source_target_pairs={{0,2},{2,0},{4,6},{6,4},{1,3},{3,1},{5,7},{7,5},{8,10},{10,8},{12,... | collective-permute-start | bytes 638984 | tf_op jit(solution)/shard_map/ppermute | solution.py:626
  120.9 13.8 %copy-start.2 = (f32[8,512]{1,0:T(8,128)S(1)}, f32[8,512]{1,0:T(8,128)}, u32[]{:S(2)}) copy-start(f32[8,512]{1,0:T(8,128)} %get-tuple-element.57.stats_ref) | copy-start | bytes 49156
  121.9 26.5 %all-to-all-start.2 = ((bf16[16,8,1792]{2,1,0:T(8,128)(2,1)}), bf16[16,8,1792]{2,1,0:T(8,128)(2,1)S(1)}, u32[]{:S(2)}, u32[]{:S(2)}) async-start(bf16[16,8,1792]{2,1,0:T(8,128)(2,1)} %shard_map.166), calls=%async_computation.2 | async-start | bytes 917504 | tf_op jit(solution)/shard_map/all_to_all | solution.py:634
  131.6 23.2 %collective-permute-start.5 = (bf16[4,64,1536]{2,1,0:T(8,128)(2,1)}, bf16[4,64,1536]{2,1,0:T(8,128)(2,1)}, u32[]{:S(2)}, u32[]{:S(2)}) collective-permute-start(bf16[4,64,1536]{2,1,0:T(8,128)(2,1)} %get-tuple-element.50), channel_id=1, source_target_pairs={{0,1},{1,0},{2,3},{3,2},{4,5},{5,4},{6,7},{7,6},{8,9},{9,8},{10,11... | collective-permute-start | bytes 2359304 | tf_op jit(solution)/shard_map/ppermute | solution.py:637
  136.0 18.8 %copy-start.5 = (bf16[4,64,1536]{2,1,0:T(8,128)(2,1)S(1)}, bf16[4,64,1536]{2,1,0:T(8,128)(2,1)}, u32[]{:S(2)}) copy-start(bf16[4,64,1536]{2,1,0:T(8,128)(2,1)} %get-tuple-element.37) | copy-start | bytes 2359300
  149.3 27.6 %all-to-all-start.3 = ((bf16[16,8,2816]{2,1,0:T(8,128)(2,1)}), bf16[16,8,2816]{2,1,0:T(8,128)(2,1)S(1)}, u32[]{:S(2)}, u32[]{:S(2)}) async-start(bf16[16,8,2816]{2,1,0:T(8,128)(2,1)} %shard_map.168), calls=%async_computation.3 | async-start | bytes 1441792 | tf_op jit(solution)/shard_map/all_to_all | solution.py:656
  154.7 37.0 %reduce-scatter.4.cloned.1.call-start = ((), (), s32[]{:S(2)}) async-start(), calls=%async_computation.7 | async-start | bytes 983040
  177.2 1.3 copy-start
  178.6 28.2 %all-to-all-start.4 = ((bf16[4,16,8,2048]{3,2,1,0:T(8,128)(2,1)}), bf16[4,16,8,2048]{3,2,1,0:T(8,128)(2,1)S(1)}, u32[]{:S(2)}, u32[]{:S(2)}) async-start(bf16[4,16,8,2048]{3,2,1,0:T(8,128)(2,1)} %copy-done), calls=%async_computation.4 | async-start | bytes 4194304 | tf_op jit(solution)/shard_map/all_to_all | solution.py:668
Sparse Core Ops, SparseCore 0:
  10.1 49.5 all-gather.2
  159.0 32.6 reduce-scatter.3

commit v6 on v5

--- a/solution.py
+++ b/solution.py
@@ -203,7 +203,7 @@
         return acc
 
     zero = jnp.zeros((BLK, slots), f32)
-    center = lax.fori_loop(0, chips * per_part, sum_body, zero)
+    center = lax.fori_loop(0, chips * per_part, sum_body, zero, unroll=3)
     center = jnp.sum(center, axis=0, keepdims=True) / width
 
     send(0, x_ref, x_hbm)
@@ -211,7 +211,7 @@
     def square_body(i, acc):
         return acc + fold(jnp.square(x_ref[pl.ds(i * chunk, chunk), :].astype(f32) - center))
 
-    spread = jnp.sum(lax.fori_loop(0, steps, square_body, zero, unroll=8), axis=0, keepdims=True) / width
+    spread = jnp.sum(lax.fori_loop(0, steps, square_body, zero, unroll=12), axis=0, keepdims=True) / width
     row_scale = lax.rsqrt(spread + epsilon)
     stats_ref[...] = jnp.zeros_like(stats_ref)
     stats_ref[0:1, :] = center
@@ -223,7 +223,7 @@
         normed_ref[at, :] = (standard * gb_ref[at, 0:1] + gb_ref[at, 1:2]).astype(bf16)
         return carry
 
-    lax.fori_loop(0, steps, norm_body, 0, unroll=8)
+    lax.fori_loop(0, steps, norm_body, 0, unroll=12)
 
 
     copies[2].wait()
@@ -242,20 +242,22 @@
     copies[3].wait()
     copies[4].wait()
 
+    tall = 2 * rows
+
     def conv_body(i, carry):
-        base = pl.multiple_of(i * rows, rows)
-        here = seg_s[pl.ds(base + EDGE, rows), :]
-        acc = [jnp.zeros((rows, LANES), f32) for _ in range(2)]
+        base = pl.multiple_of(i * tall, tall)
+        here = seg_s[pl.ds(base + EDGE, tall), :]
+        acc = [jnp.zeros((tall, LANES), f32) for _ in range(2)]
         for j in range(taps):
-            same = seg_s[pl.ds(base + j, rows), :] == here
+            same = seg_s[pl.ds(base + j, tall), :] == here
             for h in range(2):
-                value = jnp.where(same, glu_s[h, pl.ds(base + j, rows), :], 0.0)
+                value = jnp.where(same, glu_s[h, pl.ds(base + j, tall), :], 0.0)
                 acc[h] = acc[h] + value * w_s[h, j : j + 1, :]
         for h in range(2):
-            pre_s[h, pl.ds(base, rows), :] = acc[h] * bn_s[h, 0:1, :] + bn_s[h, 1:2, :]
+            pre_s[h, pl.ds(base, tall), :] = acc[h] * bn_s[h, 0:1, :] + bn_s[h, 1:2, :]
         return carry
 
-    lax.fori_loop(0, blocks, conv_body, 0)
+    lax.fori_loop(0, slots // tall, conv_body, 0)
 
     delta_swish = dot_general(delta_ref[...], wout_ref[...], 1, 1)
     row_live = lax.broadcasted_iota(jnp.int32, (slots, LANES), 0) < live

time: 217 us -> 217 us (level)
  no operation moved by 1% of the time
where the time goes in v6:
time: 217 us; the launch traced here: 216 us
  waiting for transfers between devices  80 us (37%)
  starting transfers between devices  58.6 us (27%)
  Pallas kernels  25 us (12%)
  blocking collectives  21.5 us (10%)
  between operations  16.9 us (8%)
  local copies, waits for them, and re-layouts  8.76 us (4%)
  other arithmetic  5.11 us (2%)
    pallas_call x9, Pallas kernels, call(): pl.pallas_call(kernel, out_shape=out_shape, in_specs=specs, out_specs=out...  25 us
    all_gather x1, blocking collectives, on_device(): own = lax.all_gather(packed_t, 'zl', axis=0)  21.5 us
    all_to_all x1, waiting for transfers between devices, on_device(): lax.all_to_all(shared, ('zh', 'y'), split_axis=0, concat_axis=0, tiled=True)  19.9 us
    all_to_all x1, starting transfers between devices, on_device(): lax.all_to_all(outbox, DP, split_axis=0, concat_axis=0, tiled=True)  19 us
    all_to_all x1, waiting for transfers between devices, on_device(): lax.all_to_all(grads, ('zh', 'y'), split_axis=0, concat_axis=0, tiled=True)  12.3 us
    all_to_all x1, waiting for transfers between devices, on_device(): lax.all_to_all(outbox, DP, split_axis=0, concat_axis=0, tiled=True)  12.1 us
    ppermute x3, waiting for transfers between devices, on_device(): terms[j] = lax.ppermute(paired[j], 'zl', [(z, z ^ j) for z in range(chips)])  12 us
    all_to_all x1, waiting for transfers between devices, on_device(): whole = lax.all_to_all(fanned, 'x', split_axis=0, concat_axis=0, tiled=True)  11.9 us
  transfers between devices with their start and end apart: 13, of which 9 were waited for; matrix products, arithmetic and copies ran while one was open for 5% of the time, Pallas kernels for 3%

profile of v6, /device:TPU:8, one launch (start us, length us, event | category | flops | bytes accessed | tf_op | source)
XLA Modules:
  0.0 215.9 jit_solution(10113040067356066007)
XLA Ops:
  7.9 2.6 %shard_map.162 = bf16[64,8,192]{2,1,0:T(8,128)(2,1)} custom-call(s32[64]{0:T(128)} %replica_blocks.1, s32[1]{0:T(128)} %bitcast.6.place, bf16[192,256]{1,0:T(8,128)(2,1)} %bitcast.34), custom_call_target="tpu_custom_call" | custom-call | flops 1000 | bytes 400000 | tf_op jit(solution)/shard_map/pallas_call | solution.py:41
  10.5 19.0 %all-to-all-start = ((bf16[64,8,192]{2,1,0:T(8,128)(2,1)}), bf16[64,8,192]{2,1,0:T(8,128)(2,1)S(1)}, u32[]{:S(2)}, u32[]{:S(2)}) async-start(bf16[64,8,192]{2,1,0:T(8,128)(2,1)} %shard_map.162), calls=%async_computation | async-start | bytes 524288 | tf_op jit(solution)/shard_map/all_to_all | solution.py:547
  34.5 12.1 %all-to-all-done.arrived = bf16[64,8,192]{2,1,0:T(8,128)(2,1)S(1)} async-done(((bf16[64,8,192]{2,1,0:T(8,128)(2,1)}), bf16[64,8,192]{2,1,0:T(8,128)(2,1)S(1)}, u32[]{:S(2)}, u32[]{:S(2)}) %all-to-all-start) | async-done | bytes 196640 | tf_op jit(solution)/shard_map/all_to_all | solution.py:547
  47.5 21.5 %all-gather = bf16[768,512]{1,0:T(8,128)(2,1)S(1)} all-gather(bf16[192,512]{1,0:T(8,128)(2,1)S(1)} %get-tuple-element.35), channel_id=2, replica_groups=mesh['zh'=2,'y'=8,'x'=4,'zl'=4,'core'=2] {'zl'}, dimensions={0}, use_global_device_ids=true | all-gather | bytes 983040 | tf_op jit(solution)/shard_map/all_gather | solution.py:557
  69.0 1.9 collective-permute-start
  74.1 15.4 %shard_map.164 = (bf16[1536,512]{1,0:T(8,128)(2,1)}, bf16[4,208,512]{2,1,0:T(8,128)(2,1)}, bf16[4,208,512]{2,1,0:T(8,128)(2,1)}, bf16[4,64,1536]{2,1,0:T(8,128)(...) custom-call(s32[5]{0:T(128)} %copy-done.3, bf16[4,192,512]{2,1,0:T(8,128)(2,1)} %bitcast.33, ...), custom_call_target="tpu_custom_call" | custom-call | flops 3000000000 | bytes 12000000 | tf_op jit(solution)/shard_map/pallas_call | solution.py:41
  89.5 3.7 %all-to-all-start.1 = ((bf16[4,16,8,1792]{3,2,1,0:T(8,128)(2,1)}), bf16[4,16,8,1792]{3,2,1,0:T(8,128)(2,1)S(1)}, u32[]{:S(2)}, u32[]{:S(2)}) async-start(bf16[4,16,8,1792]{3,2,1,0:T(8,128)(2,1)} %bitcast.31), calls=%async_computation.1 | async-start | bytes 3670016 | tf_op jit(solution)/shard_map/all_to_all | solution.py:633
  93.2 2.0 collective-permute-start.1
  95.3 2.4 %collective-permute-done.1.got_ref = bf16[4,208,512]{2,1,0:T(8,128)(2,1)S(1)} collective-permute-done((bf16[4,208,512]{2,1,0:T(8,128)(2,1)}, bf16[4,208,512]{2,1,0:T(8,128)(2,1)S(1)}, u32[]{:S(2)}, u32[]{:S(2)}) %collective-permute-start.1) | collective-permute-done | bytes 852000 | tf_op jit(solution)/shard_map/ppermute | solution.py:622
  98.5 3.8 %collective-permute-start.2 = (bf16[208,512]{1,0:T(8,128)(2,1)S(1)}, bf16[208,512]{1,0:T(8,128)(2,1)S(1)}, u32[]{:S(2)}, u32[]{:S(2)}) collective-permute-start(bf16[208,512]{1,0:T(8,128)(2,1)S(1)} %get-tuple-element.43), channel_id=1, source_target_pairs={{0,6},{2,4},{4,2},{6,0},{1,7},{3,5},{5,3},{7,1},{8,14},{10,12},{12... | collective-permute-start | bytes 638984 | tf_op jit(solution)/shard_map/ppermute | solution.py:628
  102.3 1.9 collective-permute-start.3
  104.2 4.4 %collective-permute-start.4 = (bf16[208,512]{1,0:T(8,128)(2,1)S(1)}, bf16[208,512]{1,0:T(8,128)(2,1)S(1)}, u32[]{:S(2)}, u32[]{:S(2)}) collective-permute-start(bf16[208,512]{1,0:T(8,128)(2,1)S(1)} %get-tuple-element.45), channel_id=1, source_target_pairs={{0,2},{2,0},{4,6},{6,4},{1,3},{3,1},{5,7},{7,5},{8,10},{10,8},{12,... | collective-permute-start | bytes 638984 | tf_op jit(solution)/shard_map/ppermute | solution.py:628
  108.6 1.8 collective-permute-done.2.dn1
  110.3 10.3 %collective-permute-done.3.dn2 = bf16[208,512]{1,0:T(8,128)(2,1)S(1)} collective-permute-done((bf16[208,512]{1,0:T(8,128)(2,1)S(1)}, bf16[208,512]{1,0:T(8,128)(2,1)S(1)}, u32[]{:S(2)}, u32[]{:S(2)}) %collective-permute-start.3) | collective-permute-done | bytes 213024 | tf_op jit(solution)/shard_map/ppermute | solution.py:628
  121.6 9.7 %all-to-all-start.2 = ((bf16[16,8,1792]{2,1,0:T(8,128)(2,1)}), bf16[16,8,1792]{2,1,0:T(8,128)(2,1)S(1)}, u32[]{:S(2)}, u32[]{:S(2)}) async-start(bf16[16,8,1792]{2,1,0:T(8,128)(2,1)} %shard_map.166), calls=%async_computation.2 | async-start | bytes 917504 | tf_op jit(solution)/shard_map/all_to_all | solution.py:636
  131.3 1.9 collective-permute-start.5
  135.8 12.3 %all-to-all-done.2.in_ref = bf16[16,8,1792]{2,1,0:T(8,128)(2,1)S(1)} async-done(((bf16[16,8,1792]{2,1,0:T(8,128)(2,1)}), bf16[16,8,1792]{2,1,0:T(8,128)(2,1)S(1)}, u32[]{:S(2)}, u32[]{:S(2)}) %all-to-all-start.2) | async-done | bytes 458784 | tf_op jit(solution)/shard_map/all_to_all | solution.py:636
  149.1 5.4 %all-to-all-start.3 = ((bf16[16,8,2816]{2,1,0:T(8,128)(2,1)}), bf16[16,8,2816]{2,1,0:T(8,128)(2,1)S(1)}, u32[]{:S(2)}, u32[]{:S(2)}) async-start(bf16[16,8,2816]{2,1,0:T(8,128)(2,1)} %shard_map.168), calls=%async_computation.3 | async-start | bytes 1441792 | tf_op jit(solution)/shard_map/all_to_all | solution.py:658
  154.5 2.2 %add_convert_fusion = bf16[4,64,1536]{2,1,0:T(8,128)(2,1)} fusion(bf16[4,64,1536]{2,1,0:T(8,128)(2,1)} %collective-permute-done.5, bf16[4,64,1536]{2,1,0:T(8,128)(2,1)S(1)} %copy-done.5), kind=kLoop, calls=%fused_computation | loop fusion | flops 1572864 | bytes 2359296 | tf_op jit(solution)/shard_map/convert_element_type | solution.py:640
  156.8 19.9 %all-to-all-done.3.in_ref = bf16[16,8,2816]{2,1,0:T(8,128)(2,1)S(1)} async-done(((bf16[16,8,2816]{2,1,0:T(8,128)(2,1)}), bf16[16,8,2816]{2,1,0:T(8,128)(2,1)S(1)}, u32[]{:S(2)}, u32[]{:S(2)}) %all-to-all-start.3) | async-done | bytes 720928 | tf_op jit(solution)/shard_map/all_to_all | solution.py:658
  178.3 4.7 %all-to-all-start.4 = ((bf16[4,16,8,2048]{3,2,1,0:T(8,128)(2,1)}), bf16[4,16,8,2048]{3,2,1,0:T(8,128)(2,1)S(1)}, u32[]{:S(2)}, u32[]{:S(2)}) async-start(bf16[4,16,8,2048]{3,2,1,0:T(8,128)(2,1)} %copy-done), calls=%async_computation.4 | async-start | bytes 4194304 | tf_op jit(solution)/shard_map/all_to_all | solution.py:670
  183.9 7.5 %reduce-scatter.4.cloned.1.call-done = bf16[64,1536]{1,0:T(8,128)(2,1)} async-done(((bf16[256,1536]{1,0:T(8,128)(2,1)}), bf16[64,1536]{1,0:T(8,128)(2,1)}) %reduce-scatter.4.cloned.1.call-update) | async-done | bytes 196624
  194.7 11.9 %all-to-all-done.4 = bf16[4,16,8,2048]{3,2,1,0:T(8,128)(2,1)S(1)} async-done(((bf16[4,16,8,2048]{3,2,1,0:T(8,128)(2,1)}), bf16[4,16,8,2048]{3,2,1,0:T(8,128)(2,1)S(1)}, u32[]{:S(2)}, u32[]{:S(2)}) %all-to-all-start.4) | async-done | bytes 2097184 | tf_op jit(solution)/shard_map/all_to_all | solution.py:670
  206.5 2.0 shard_map.170
  (52 shorter events, 18.6 us)
Async XLA Ops:
  7.2 63.7 %copy-start.7 = (f32[1536]{0:T(1024)S(1)}, f32[1536]{0:T(1024)}, u32[]{:S(2)}) copy-start(f32[1536]{0:T(1024)} %param.12) | copy-start | bytes 18436
  7.2 64.3 %copy-start.8 = (f32[1536]{0:T(1024)S(1)}, f32[1536]{0:T(1024)}, u32[]{:S(2)}) copy-start(f32[1536]{0:T(1024)} %param.13) | copy-start | bytes 18436
  7.2 65.9 %all-gather.3.cloned.1.call-start = ((), (), s32[]{:S(2)}) async-start(), calls=%async_computation.6 | async-start | bytes 1769472 | tf_op jit(solution)/shard_map/all_gather | solution.py:520
  10.5 36.1 %all-to-all-start = ((bf16[64,8,192]{2,1,0:T(8,128)(2,1)}), bf16[64,8,192]{2,1,0:T(8,128)(2,1)S(1)}, u32[]{:S(2)}, u32[]{:S(2)}) async-start(bf16[64,8,192]{2,1,0:T(8,128)(2,1)} %shard_map.162), calls=%async_computation | async-start | bytes 524288 | tf_op jit(solution)/shard_map/all_to_all | solution.py:547
  34.5 38.7 %copy-start.3 = (s32[5]{0:T(128)}, s32[5]{0:T(128)S(1)}, u32[]{:S(2)}) copy-start(s32[5]{0:T(128)S(1)} %stack.19.scalars) | copy-start | bytes 64
  69.0 4.2 %copy-start.6 = (bf16[768,512]{1,0:T(8,128)(2,1)}, bf16[768,512]{1,0:T(8,128)(2,1)S(1)}, u32[]{:S(2)}) copy-start(bf16[768,512]{1,0:T(8,128)(2,1)S(1)} %all-gather) | copy-start | bytes 2359300
  69.0 4.2 %collective-permute-start = (bf16[4,192,512]{2,1,0:T(8,128)(2,1)S(1)}, bf16[4,192,512]{2,1,0:T(8,128)(2,1)S(1)}, u32[]{:S(2)}, u32[]{:S(2)}) collective-permute-start(bf16[4,192,512]{2,1,0:T(8,128)(2,1)S(1)} %bitcast.32), channel_id=1, source_target_pairs={{0,1},{1,0},{2,3},{3,2},{4,5},{5,4},{6,7},{7,6},{8,9},{9,8},{10,11... | collective-permute-start | bytes 2359304 | tf_op jit(solution)/shard_map/ppermute | solution.py:558
  73.1 0.9 copy-start.9
  89.5 8.2 %copy-start.1 = (bf16[4,208,512]{2,1,0:T(8,128)(2,1)S(1)}, bf16[4,208,512]{2,1,0:T(8,128)(2,1)}, u32[]{:S(2)}) copy-start(bf16[4,208,512]{2,1,0:T(8,128)(2,1)} %get-tuple-element.40.keep_ref) | copy-start | bytes 2555908
  89.5 8.2 %copy-start.4 = (s32[5]{0:T(128)S(1)}, s32[5]{0:T(128)}, u32[]{:S(2)}) copy-start(s32[5]{0:T(128)} %copy-done.3) | copy-start | bytes 64
  89.5 31.1 %all-to-all-start.1 = ((bf16[4,16,8,1792]{3,2,1,0:T(8,128)(2,1)}), bf16[4,16,8,1792]{3,2,1,0:T(8,128)(2,1)S(1)}, u32[]{:S(2)}, u32[]{:S(2)}) async-start(bf16[4,16,8,1792]{3,2,1,0:T(8,128)(2,1)} %bitcast.31), calls=%async_computation.1 | async-start | bytes 3670016 | tf_op jit(solution)/shard_map/all_to_all | solution.py:633
  93.2 4.5 %collective-permute-start.1 = (bf16[4,208,512]{2,1,0:T(8,128)(2,1)}, bf16[4,208,512]{2,1,0:T(8,128)(2,1)S(1)}, u32[]{:S(2)}, u32[]{:S(2)}) collective-permute-start(bf16[4,208,512]{2,1,0:T(8,128)(2,1)} %get-tuple-element.41), channel_id=1, source_target_pairs={{0,1},{1,0},{2,3},{3,2},{4,5},{5,4},{6,7},{7,6},{8,9},{9,8},{10,11... | collective-permute-start | bytes 2555912 | tf_op jit(solution)/shard_map/ppermute | solution.py:622
  98.5 11.9 %collective-permute-start.2 = (bf16[208,512]{1,0:T(8,128)(2,1)S(1)}, bf16[208,512]{1,0:T(8,128)(2,1)S(1)}, u32[]{:S(2)}, u32[]{:S(2)}) collective-permute-start(bf16[208,512]{1,0:T(8,128)(2,1)S(1)} %get-tuple-element.43), channel_id=1, source_target_pairs={{0,6},{2,4},{4,2},{6,0},{1,7},{3,5},{5,3},{7,1},{8,14},{10,12},{12... | collective-permute-start | bytes 638984 | tf_op jit(solution)/shard_map/ppermute | solution.py:628
  102.3 18.3 %collective-permute-start.3 = (bf16[208,512]{1,0:T(8,128)(2,1)S(1)}, bf16[208,512]{1,0:T(8,128)(2,1)S(1)}, u32[]{:S(2)}, u32[]{:S(2)}) collective-permute-start(bf16[208,512]{1,0:T(8,128)(2,1)S(1)} %get-tuple-element.44), channel_id=1, source_target_pairs={{0,4},{2,6},{4,0},{6,2},{1,5},{3,7},{5,1},{7,3},{8,12},{10,14},{12... | collective-permute-start | bytes 638984 | tf_op jit(solution)/shard_map/ppermute | solution.py:628
  104.2 16.4 %collective-permute-start.4 = (bf16[208,512]{1,0:T(8,128)(2,1)S(1)}, bf16[208,512]{1,0:T(8,128)(2,1)S(1)}, u32[]{:S(2)}, u32[]{:S(2)}) collective-permute-start(bf16[208,512]{1,0:T(8,128)(2,1)S(1)} %get-tuple-element.45), channel_id=1, source_target_pairs={{0,2},{2,0},{4,6},{6,4},{1,3},{3,1},{5,7},{7,5},{8,10},{10,8},{12,... | collective-permute-start | bytes 638984 | tf_op jit(solution)/shard_map/ppermute | solution.py:628
  120.6 13.8 %copy-start.2 = (f32[8,512]{1,0:T(8,128)S(1)}, f32[8,512]{1,0:T(8,128)}, u32[]{:S(2)}) copy-start(f32[8,512]{1,0:T(8,128)} %get-tuple-element.57.stats_ref) | copy-start | bytes 49156
  121.6 26.5 %all-to-all-start.2 = ((bf16[16,8,1792]{2,1,0:T(8,128)(2,1)}), bf16[16,8,1792]{2,1,0:T(8,128)(2,1)S(1)}, u32[]{:S(2)}, u32[]{:S(2)}) async-start(bf16[16,8,1792]{2,1,0:T(8,128)(2,1)} %shard_map.166), calls=%async_computation.2 | async-start | bytes 917504 | tf_op jit(solution)/shard_map/all_to_all | solution.py:636
  131.3 23.2 %collective-permute-start.5 = (bf16[4,64,1536]{2,1,0:T(8,128)(2,1)}, bf16[4,64,1536]{2,1,0:T(8,128)(2,1)}, u32[]{:S(2)}, u32[]{:S(2)}) collective-permute-start(bf16[4,64,1536]{2,1,0:T(8,128)(2,1)} %get-tuple-element.50), channel_id=1, source_target_pairs={{0,1},{1,0},{2,3},{3,2},{4,5},{5,4},{6,7},{7,6},{8,9},{9,8},{10,11... | collective-permute-start | bytes 2359304 | tf_op jit(solution)/shard_map/ppermute | solution.py:639
  135.8 18.8 %copy-start.5 = (bf16[4,64,1536]{2,1,0:T(8,128)(2,1)S(1)}, bf16[4,64,1536]{2,1,0:T(8,128)(2,1)}, u32[]{:S(2)}) copy-start(bf16[4,64,1536]{2,1,0:T(8,128)(2,1)} %get-tuple-element.37) | copy-start | bytes 2359300
  149.1 27.6 %all-to-all-start.3 = ((bf16[16,8,2816]{2,1,0:T(8,128)(2,1)}), bf16[16,8,2816]{2,1,0:T(8,128)(2,1)S(1)}, u32[]{:S(2)}, u32[]{:S(2)}) async-start(bf16[16,8,2816]{2,1,0:T(8,128)(2,1)} %shard_map.168), calls=%async_computation.3 | async-start | bytes 1441792 | tf_op jit(solution)/shard_map/all_to_all | solution.py:658
  154.5 37.0 %reduce-scatter.4.cloned.1.call-start = ((), (), s32[]{:S(2)}) async-start(), calls=%async_computation.7 | async-start | bytes 983040
  177.0 1.3 copy-start
  178.3 28.2 %all-to-all-start.4 = ((bf16[4,16,8,2048]{3,2,1,0:T(8,128)(2,1)}), bf16[4,16,8,2048]{3,2,1,0:T(8,128)(2,1)S(1)}, u32[]{:S(2)}, u32[]{:S(2)}) async-start(bf16[4,16,8,2048]{3,2,1,0:T(8,128)(2,1)} %copy-done), calls=%async_computation.4 | async-start | bytes 4194304 | tf_op jit(solution)/shard_map/all_to_all | solution.py:670
Sparse Core Ops, SparseCore 0:
  10.1 49.5 all-gather.2
  158.7 32.6 reduce-scatter.3
